TPU v7x, 32 devices: a whole 2x2x4 slice. The times are simulated.
32 devices in a mesh: loc: 8 (over z, core), inc: 4 (over y, x).
Axes of the slice: x: 2, y: 2, z: 4, core: 2. Of those that a mesh axis runs over, the one named last changes fastest.
Arguments:
- cont_value: float32 [3200, 8192], P('loc', 'inc'), may hold values from -4 to 252, as said below
- flow_util: float32 [3200, 8192], P('loc', 'inc'), may hold values from -6 to 6
- move_cost: float32 [3200, 3200], P('loc'), may hold values from 0 to 6, as said below
- live_mask: int32 [3200], P('loc'), may hold values 0 or 1
- trans_weight: float32 [128, 128], replicated, may hold values from 0.02 to 1
- asset_policy: int32 [128, 64], replicated, may hold values from 0 to 63
- mass: float32 [3200, 8192], P('loc', 'inc'), may hold values from 0.1 to 1
Outputs:
- new_value: float32 [3200, 8192], P('loc', 'inc')
- new_mass: float32 [3200, 8192], P('loc', 'inc')
Inputs may be any that keep to these rules, and one draw needn't show every extreme that they name: cont_value lies within the stated bounds. move_cost is symmetric with a zero diagonal; off the diagonal it lies between 0.5 and 6.
All inputs are finite; a program needn't handle non-finite values. No bound on the sum of `live_mask` on one device may be relied on, other than what follows from the above.
Results may differ from a plain program's by a relative error of at most 0.004.
Values may be sent and summed in bfloat16 or wider, within the bound.
No kernel may reach another device: no remote copies, remote signals or barrier semaphores. Data moves between devices by JAX's collectives and lax.ppermute only.
A program may use at most 64 MiB of HBM per device.

v0:
```python
import jax
import jax.numpy as jnp
from jax import lax
from jax.sharding import PartitionSpec as P

E = 128
A = 64


DISCOUNT = 0.96


def shards(cont_value, flow_util, move_cost, live_mask, trans_weight, asset_policy, mass):
    high = lax.Precision.HIGHEST
    raised = trans_weight + 16.0 * jnp.eye(E, dtype=jnp.float32)
    trans_prob = raised / jnp.sum(raised, axis=1, keepdims=True)
    onehot = (asset_policy[:, :, None] == jnp.arange(A, dtype=jnp.int32)[None, None, :]).astype(
        jnp.float32
    )
    moved_rows = lax.all_to_all(cont_value, "inc", split_axis=0, concat_axis=1, tiled=True)
    expect = jnp.einsum("ef,jfb->jeb", trans_prob, moved_rows.reshape(-1, E, A), precision=high)
    chosen_all = jnp.einsum("jeb,eab->jea", expect, onehot, precision=high).reshape(-1, E * A)
    chosen = lax.all_to_all(chosen_all, "inc", split_axis=1, concat_axis=0, tiled=True)
    scores = DISCOUNT * chosen
    live_rows = live_mask[:, None] > 0
    local_max = jnp.max(jnp.where(live_rows, scores, jnp.float32(-1e30)), axis=0)
    column_max = lax.pmax(local_max, "loc")
    dest_weight = jnp.where(
        live_rows, jnp.exp(scores - column_max[None, :]), jnp.float32(0.0)
    ).astype(jnp.bfloat16)
    kernel = jnp.exp(-move_cost).astype(jnp.bfloat16)
    columns = kernel
    totals = jnp.dot(
        columns,
        lax.all_gather(dest_weight, "loc", axis=0, tiled=True),
        preferred_element_type=jnp.float32,
    )
    new_value = flow_util + column_max[None, :] + jnp.log(totals)
    shares = (mass / totals).astype(jnp.bfloat16)
    columns = kernel
    arrived = lax.psum_scatter(
        lax.dot_general(
            columns, shares, (((0,), (0,)), ((), ())), preferred_element_type=jnp.float32
        ).astype(jnp.bfloat16),
        "loc",
        scatter_dimension=0,
        tiled=True,
    ).astype(jnp.float32)
    movers = dest_weight.astype(jnp.float32) * arrived
    moved_mass = lax.all_to_all(movers, "inc", split_axis=0, concat_axis=1, tiled=True)
    shuffled = jnp.einsum("jea,eab->jeb", moved_mass.reshape(-1, E, A), onehot, precision=high)
    mixed_mass = jnp.einsum("ef,jeb->jfb", trans_prob, shuffled, precision=high).reshape(-1, E * A)
    new_mass = lax.all_to_all(mixed_mass, "inc", split_axis=1, concat_axis=0, tiled=True)
    return (new_value, new_mass)


def solution(mesh):
    return jax.shard_map(
        shards,
        mesh=mesh,
        in_specs=(
            P("loc", "inc"),
            P("loc", "inc"),
            P("loc", None),
            P("loc"),
            P(),
            P(),
            P("loc", "inc"),
        ),
        out_specs=(P("loc", "inc"), P("loc", "inc")),
        check_vma=False,
    )
```

profile of v0, /device:TPU:8, one launch (start us, length us, event | category | flops | bytes accessed | tf_op | source)
XLA Modules:
  0.0 556.4 jit_solution(14089480042023645202)
XLA Ops:
  7.2 3.3 all_to_all.48
  10.5 0.0 copy-start
  10.5 3.9 all-to-all-start
  14.3 0.8 copy.19
  15.2 0.0 copy-done
  15.2 0.1 fusion.18
  15.3 0.0 copy-start.3
  15.3 38.2 %all-to-all-done = f32[4,100,2048]{2,1,0:T(8,128)S(1)} async-done(((f32[4,100,2048]{2,1,0:T(8,128)}), f32[4,100,2048]{2,1,0:T(8,128)S(1)}, u32[]{:S(2)}, u32[]{:S(2)}) %all-to-all-start) | async-done | bytes 3276832 | tf_op jit(solution)/shard_map/all_to_all | solution.py:20
  53.5 3.4 copy.20
  56.9 0.0 copy-done.3
  56.9 10.7 %fusion.10 = f32[100,128,64]{1,0,2:T(8,128)S(1)} fusion(f32[100,128,64]{0,2,1:T(8,128)} %bitcast.40, f32[128,128]{1,0:T(8,128)S(1)} %copy-done, f32[128]{0:T(128)S(1)} %fusion.18), kind=kOutput, calls=%fused_computation.19 | convolution fusion | flops 1258356736 | bytes 6619648 | tf_op jit(solution)/shard_map/ef,jfb->jeb/dot_general | solution.py:21
  67.6 4.0 copy.23
  71.7 7.9 %fusion.4 = f32[128,64,100]{2,1,0:T(8,128)} fusion(f32[100,128,64]{0,2,1:T(8,128)} %copy.23, s32[128,64]{1,0:T(8,128)S(1)} %copy.19), kind=kOutput, calls=%fused_computation.7 | convolution fusion | flops 629669888 | bytes 6586368 | tf_op jit(solution)/shard_map/jeb,eab->jea/dot_general | solution.py:22
  79.6 5.4 copy.24
  85.0 0.0 copy-start.5
  85.0 3.9 all-to-all-start.1
  88.8 0.0 all-gather.2.cloned.1.call-start
  88.9 0.0 copy-done.5
  88.9 0.0 copy-start.1
  88.9 0.1 broadcast_in_dim.28
  89.0 38.2 %all-to-all-done.1 = f32[100,4,2048]{2,0,1:T(8,128)S(1)} async-done(((f32[100,4,2048]{2,0,1:T(8,128)}), f32[100,4,2048]{2,0,1:T(8,128)S(1)}, u32[]{:S(2)}, u32[]{:S(2)}) %all-to-all-start.1) | async-done | bytes 3276832 | tf_op jit(solution)/shard_map/all_to_all | solution.py:23
  127.2 0.0 copy-done.1
  127.2 0.5 select_reduce_fusion
  127.7 12.6 %pmax.7 = f32[2048]{0:T(1024)S(1)} all-reduce(f32[2048]{0:T(1024)S(1)} %select_reduce_fusion), channel_id=1, replica_groups=mesh['loc'=8,'inc'=4] {'loc'}, use_global_device_ids=true, to_apply=%region_2.3 | all-reduce | flops 2048 | bytes 16384 | tf_op jit(solution)/shard_map/pmax | solution.py:27
  140.2 2.0 multiply_bitcast_fusion
  142.3 0.0 copy-start.2
  142.3 2.2 mul.28
  144.4 0.0 copy-done.2
  144.5 1.7 select_convert_fusion
  146.1 0.0 all-gather.2.cloned.1.call-update
  146.2 0.0 reduce-scatter.2.cloned.1.call-start
  146.2 118.1 %all-gather.2.cloned.1.call-done = bf16[3200,2048]{1,0:T(8,128)(2,1)} async-done(((bf16[400,2048]{1,0:T(8,128)(2,1)}), bf16[3200,2048]{1,0:T(8,128)(2,1)}) %all-gather.2.cloned.1.call-update) | async-done | bytes 13107216 | tf_op jit(solution)/shard_map/all_gather | solution.py:35
  264.3 0.0 copy-start.6
  264.3 13.3 %fusion.5 = (f32[400,2048]{1,0:T(8,128)}, f32[2048,400]{0,1:T(8,128)S(1)}) fusion(f32[400,2048]{1,0:T(8,128)} %param.8, f32[2048]{0:T(1024)S(1)} %pmax.7, bf16[3200,2048]{1,0:T(8,128)(2,1)} %all-gather.2.cloned.1.call-done, f32[400,3200]{1,0:T(8,128)} %param.9), kind=kOutput, calls=%fused_computation.12 | convolution fusion | flops 5247078400 | bytes 28065792 | tf_op jit(solution)/shard_map/dot_general | solution.py:33
  277.7 0.0 copy-done.6
  277.7 12.5 %fusion = bf16[3200,2048]{1,0:T(8,128)(2,1)} fusion(f32[400,2048]{1,0:T(8,128)S(1)} %copy-done.6, f32[2048,400]{0,1:T(8,128)S(1)} %get-tuple-element.3, f32[400,3200]{1,0:T(8,128)} %param.9), kind=kOutput, calls=%fused_computation.1 | convolution fusion | flops 5253632000 | bytes 24780800 | tf_op jit(solution)/shard_map/dot_general | solution.py:42
  290.1 0.0 reduce-scatter.2.cloned.1.call-update
  290.2 132.7 %reduce-scatter.2.cloned.1.call-done = bf16[400,2048]{1,0:T(8,128)(2,1)} async-done(((bf16[3200,2048]{1,0:T(8,128)(2,1)}), bf16[400,2048]{1,0:T(8,128)(2,1)}) %reduce-scatter.2.cloned.1.call-update) | async-done | bytes 1638416 | tf_op jit(solution)/shard_map/reduce_scatter | solution.py:41
  422.8 3.9 convert_multiply_fusion
  426.8 2.1 all_to_all.53
  428.9 44.1 %all_to_all.64 = f32[4,100,2048]{2,1,0:T(8,128)} all-to-all(f32[4,100,2048]{2,1,0:T(8,128)S(1)} %all_to_all.53), channel_id=1, replica_groups=mesh['loc'=8,'inc'=4] {'inc'}, dimensions={0} | all-to-all | bytes 6553600 | tf_op jit(solution)/shard_map/all_to_all | solution.py:50
  473.0 5.1 copy.26
  478.1 7.0 %fusion.7 = f32[100,128,64]{0,2,1:T(8,128)} fusion(f32[100,128,64]{0,2,1:T(8,128)} %bitcast.39, s32[128,64]{1,0:T(8,128)S(1)} %copy.19), kind=kOutput, calls=%fused_computation.16 | convolution fusion | flops 629669888 | bytes 6586368 | tf_op jit(solution)/shard_map/jea,eab->jeb/dot_general | solution.py:51
  485.1 0.0 copy-start.4
  485.1 4.0 copy.27
  489.1 0.0 copy-done.4
  489.1 4.5 convolution_bitcast_fusion
  493.6 5.1 copy.28
  498.8 5.4 copy.29
  504.1 43.5 %all_to_all.65 = f32[100,4,2048]{2,0,1:T(8,128)S(1)} all-to-all(f32[100,4,2048]{2,0,1:T(8,128)} %copy.29), channel_id=1, replica_groups=mesh['loc'=8,'inc'=4] {'inc'}, dimensions={1} | all-to-all | bytes 6553600 | tf_op jit(solution)/shard_map/all_to_all | solution.py:53
  547.7 1.9 all_to_all.59
  (1 shorter events, 0.0 us)
Async XLA Ops:
  10.5 4.7 copy-start
  10.5 43.0 %all-to-all-start = ((f32[4,100,2048]{2,1,0:T(8,128)}), f32[4,100,2048]{2,1,0:T(8,128)S(1)}, u32[]{:S(2)}, u32[]{:S(2)}) async-start(f32[4,100,2048]{2,1,0:T(8,128)} %all_to_all.48), calls=%async_computation | async-start | bytes 6815744 | tf_op jit(solution)/shard_map/all_to_all | solution.py:20
  15.3 41.6 %copy-start.3 = (f32[128]{0:T(128)}, f32[128]{0:T(128)S(1)}, u32[]{:S(2)}) copy-start(f32[128]{0:T(128)S(1)} %fusion.18) | copy-start | bytes 1540
  85.0 3.9 copy-start.5
  85.0 42.2 %all-to-all-start.1 = ((f32[100,4,2048]{2,0,1:T(8,128)}), f32[100,4,2048]{2,0,1:T(8,128)S(1)}, u32[]{:S(2)}, u32[]{:S(2)}) async-start(f32[100,4,2048]{2,0,1:T(8,128)} %copy.24), calls=%async_computation.1 | async-start | bytes 6815744 | tf_op jit(solution)/shard_map/all_to_all | solution.py:23
  88.8 175.5 %all-gather.2.cloned.1.call-start = ((), (), s32[]{:S(2)}) async-start(), calls=%async_computation.5 | async-start | bytes 14745600 | tf_op jit(solution)/shard_map/all_gather | solution.py:35
  88.9 38.3 %copy-start.1 = (pred[400]{0:T(512)(128)(4,1)}, pred[400]{0:T(512)(128)(4,1)S(1)}, u32[]{:S(2)}) copy-start(pred[400]{0:T(512)(128)(4,1)S(1)} %broadcast_compare_fusion) | copy-start | bytes 1204
  142.3 2.2 copy-start.2
  146.2 276.7 %reduce-scatter.2.cloned.1.call-start = ((), (), s32[]{:S(2)}) async-start(), calls=%async_computation.6 | async-start | bytes 14745600 | tf_op jit(solution)/shard_map/reduce_scatter | solution.py:41
  264.3 13.3 %copy-start.6 = (f32[400,2048]{1,0:T(8,128)S(1)}, f32[400,2048]{1,0:T(8,128)}, u32[]{:S(2)}) copy-start(f32[400,2048]{1,0:T(8,128)} %param.13) | copy-start | bytes 9830404
  485.1 4.0 copy-start.4
Sparse Core Ops, SparseCore 0:
  146.3 117.9 all-gather.1
  290.3 132.4 reduce-scatter.1
where the time goes:
time: 557 us; the launch traced here: 556 us
  waiting for transfers between devices  327 us (59%)
  blocking collectives  100 us (18%)
  matrix products  55.9 us (10%)
  local copies, waits for them, and re-layouts  42.9 us (8%)
  between operations  14.2 us (3%)
  other arithmetic  8.22 us (1%)
  starting transfers between devices  7.79 us (1%)
    reduce_scatter x1, waiting for transfers between devices, shards(): lax.psum_scatter(lax.dot_general(columns, shares, (((0,), (0,)), ((), ())...  133 us
    all_gather x1, waiting for transfers between devices, shards(): lax.all_gather(dest_weight, 'loc', axis=0, tiled=True)  118 us
    all_to_all x1, blocking collectives, shards(): lax.all_to_all(movers, 'inc', split_axis=0, concat_axis=1, tiled=True)  44.1 us
    all_to_all x1, blocking collectives, shards(): lax.all_to_all(mixed_mass, 'inc', split_axis=1, concat_axis=0, tiled=True)  43.5 us
    all_to_all x1, waiting for transfers between devices, shards(): lax.all_to_all(chosen_all, 'inc', split_axis=1, concat_axis=0, tiled=True)  38.2 us
    all_to_all x1, waiting for transfers between devices, shards(): lax.all_to_all(cont_value, 'inc', split_axis=0, concat_axis=1, tiled=True)  38.2 us
    dot_general x1, matrix products, shards(): jnp.dot(columns, lax.all_gather(dest_weight, 'loc', axis=0, tiled=True),...  13.3 us
    pmax x1, blocking collectives, shards(): column_max = lax.pmax(local_max, 'loc')  12.6 us
  transfers between devices with their start and end apart: 4, of which 4 were waited for; matrix products, arithmetic and copies ran while one was open for 0% of the time, Pallas kernels for 0%

commit v1 on v0

v1 whole, which is shorter than its diff:
```python
import functools
import math

import jax
import jax.numpy as jnp
from jax import lax
from jax.experimental import pallas as pl
from jax.experimental.pallas import tpu as pltpu
from jax.sharding import PartitionSpec as P

DISCOUNT = 0.96
LANES = 128
TILE = 16
VALUE_LOW = -4.0
VALUE_HIGH = 252.0
STEP = (VALUE_HIGH - VALUE_LOW) / 65535.0
HALF = 32768.0
LN2 = math.log(2.0)
SCORE_STEP = DISCOUNT * STEP / LN2
SCORE_SHIFT = DISCOUNT * (HALF * STEP + VALUE_LOW)

BF = jnp.bfloat16
F32 = jnp.float32
VMEM = pl.BlockSpec(memory_space=pltpu.VMEM)
SMEM = pl.BlockSpec(memory_space=pltpu.SMEM)
ANY = pl.BlockSpec(memory_space=pl.ANY)


def dot(a, b):
    return lax.dot_general(a, b, (((1,), (0,)), ((), ())), preferred_element_type=F32)


def dot_nt(a, b):
    return lax.dot_general(a, b, (((1,), (1,)), ((), ())), preferred_element_type=F32)


def lanes_at(start, size):
    return pl.ds(pl.multiple_of(start, LANES), size)


def call(kernel, outs, ins, scratch=(), flops=0, specs=None, vmem=48):
    moved = sum(math.prod(x.shape) * x.dtype.itemsize for x in list(ins) + list(outs))
    return pl.pallas_call(
        kernel,
        out_shape=tuple(outs),
        in_specs=specs or [SMEM] + [VMEM] * (len(ins) - 1),
        out_specs=tuple([VMEM] * len(outs)),
        scratch_shapes=list(scratch),
        compiler_params=pltpu.CompilerParams(vmem_limit_bytes=vmem * 1024 * 1024),
        cost_estimate=pl.CostEstimate(flops=flops, bytes_accessed=moved, transcendentals=0),
    )(*ins)


class Plan:
    def __init__(self, n_loc, n_inc, counties, rows, columns, incomes, assets):
        self.n_loc, self.n_inc = n_loc, n_inc
        self.counties, self.rows, self.columns = counties, rows, columns
        self.incomes, self.assets = incomes, assets
        self.own_incomes = incomes // n_inc
        self.own_assets = assets // n_inc
        self.group_assets = LANES // self.own_incomes
        self.groups = self.own_assets // max(self.group_assets, 1)
        self.wide = n_inc * LANES
        self.part = columns // n_inc
        self.states = columns // n_loc
        self.packed = rows + TILE
        self.block_rows = counties // LANES
        self.window = (self.block_rows // 2 + 1) * LANES
        self.stride = rows // n_inc // TILE * TILE
        self.quarter = rows - self.stride * (n_inc - 1)

    def fits(self):
        power = lambda n: n & (n - 1) == 0
        return (
            power(self.n_loc)
            and power(self.n_inc)
            and self.incomes == LANES
            and self.own_incomes * self.group_assets == LANES
            and self.groups * self.group_assets == self.own_assets
            and self.groups == self.n_inc
            and self.states % LANES == 0
            and self.rows % TILE == 0
            and self.counties % LANES == 0
            and self.block_rows % 2 == 1
        )


def order_maps(plan):
    w, oa, oi = plan.wide, plan.own_assets, plan.own_incomes
    r = lax.broadcasted_iota(jnp.int32, (w, w), 0)
    c = lax.broadcasted_iota(jnp.int32, (w, w), 1)
    a = plan.assets
    spot = (r % a) // oa * LANES + r // a * oa + r % oa
    first = (c == spot).astype(BF)
    second = (c == r % oa * oi + r // oa).astype(BF)
    return first, second


def encode_kernel(plan, at, value, first, second, *refs):
    outs, (high, low) = refs[: plan.n_inc], refs[plan.n_inc :]
    inc, w = at[1], plan.wide
    for t in range(plan.n_inc):
        x = value[:, t * w : (t + 1) * w]
        code = jnp.clip(jnp.round((x - VALUE_LOW) * (1.0 / STEP)) - HALF, -HALF, HALF - 1.0)
        top = jnp.floor(code * (1.0 / 256.0))
        rest = code - 256.0 * top
        moved_top = dot(top.astype(BF), first[...]).astype(BF)
        moved_rest = dot(rest.astype(BF), first[...]).astype(BF)
        for q in range(plan.n_inc):
            high[q, :, t * LANES : (t + 1) * LANES] = moved_top[:, q * LANES : (q + 1) * LANES]
            low[q, :, t * LANES : (t + 1) * LANES] = moved_rest[:, q * LANES : (q + 1) * LANES]
    for k in range(plan.n_inc):
        q = inc ^ k
        code = dot(high[q], second[...]) * 256.0 + dot(low[q], second[...])
        outs[k][...] = code.astype(jnp.int32).astype(jnp.int16)


def weight_kernel(plan, at, *refs):
    ni, nl, rows = plan.n_inc, plan.n_loc, plan.rows
    codes, (mix_a, mix_b, live), refs = refs[:ni], refs[ni : ni + 3], refs[ni + 3 :]
    outs, (held, weights) = refs[:nl], refs[nl:]
    loc, inc, w = at[0], at[1], plan.wide
    alive = live[...] > 0.0
    for g in range(plan.groups):
        for k in range(ni):
            held[:, lanes_at((inc ^ k) * LANES, LANES)] = codes[k][
                :, g * LANES : (g + 1) * LANES
            ].astype(jnp.int32)
        code = held[...]
        top = (code >> 8).astype(F32).astype(BF)
        rest = (code & 255).astype(F32).astype(BF)
        mixed = (dot(top, mix_a[...]) + dot(top, mix_b[...])) * 256.0 + dot(rest, mix_a[...])
        score = mixed * SCORE_STEP
        peak = jnp.max(jnp.where(alive, score, -512.0), axis=0, keepdims=True)
        peak = jnp.ceil(peak)
        weights[0:rows, g * w : (g + 1) * w] = jnp.where(alive, jnp.exp2(score - peak), 0.0).astype(BF)
        weights[rows:, g * w : (g + 1) * w] = jnp.broadcast_to(peak, (TILE, w)).astype(BF)
    for k in range(nl):
        outs[k][...] = weights[:, lanes_at((loc ^ k) * plan.states, plan.states)]


def mass_kernel(plan, at, mass, hit, second, *refs):
    outs, (held,) = refs[: plan.n_inc], refs[plan.n_inc :]
    inc, w = at[1], plan.wide
    for t in range(plan.n_inc):
        x = mass[:, t * w : (t + 1) * w]
        top = x.astype(BF)
        rest = (x - top.astype(F32)).astype(BF)
        moved = (dot(top, hit[t]) + dot(rest, hit[t])).astype(BF)
        for q in range(plan.n_inc):
            held[q, :, t * LANES : (t + 1) * LANES] = moved[:, q * LANES : (q + 1) * LANES]
    for k in range(plan.n_inc):
        outs[k][...] = dot(held[inc ^ k], second[...]).astype(BF)


def spread_kernel(plan, at, *refs):
    ni, nl = plan.n_inc, plan.n_loc
    ins, outs, (held,) = refs[:ni], refs[ni : ni + nl], refs[ni + nl :]
    loc, inc = at[0], at[1]
    for k in range(ni):
        for g in range(plan.groups):
            held[:, lanes_at(g * plan.wide + (inc ^ k) * LANES, LANES)] = ins[k][
                :, g * LANES : (g + 1) * LANES
            ]
    for k in range(nl):
        outs[k][...] = held[:, lanes_at((loc ^ k) * plan.states, plan.states)]


def collect_kernel(plan, at, *refs):
    ni, nl = plan.n_inc, plan.n_loc
    ins, outs, (held,) = refs[:nl], refs[nl : nl + ni], refs[nl + ni :]
    loc, inc = at[0], at[1]
    for k in range(nl):
        held[:, lanes_at((loc ^ k) * plan.states, plan.states)] = ins[k][...]
    for k in range(ni):
        for g in range(plan.groups):
            outs[k][:, g * LANES : (g + 1) * LANES] = held[
                :, lanes_at(g * plan.wide + (inc ^ k) * LANES, LANES)
            ]


def window_kernel(plan, at, cost, outs, quarter, held):
    loc, inc, n = at[0], at[1], plan.counties
    near = jnp.exp(-cost[...]).astype(BF)
    held[:, :n] = near
    held[:, n:] = near[:, : plan.window - LANES]
    step = TILE
    for g in range(plan.rows // step):
        block = (loc * plan.rows + g * step) // LANES
        outs[g * step : (g + 1) * step, :] = held[
            g * step : (g + 1) * step, lanes_at(block * LANES, plan.window)
        ]
    quarter[...] = outs[pl.ds(pl.multiple_of(inc * plan.stride, TILE), plan.quarter), :]


def solve_kernel(plan, at, *refs):
    nl, ni, rows, n = plan.n_loc, plan.n_inc, plan.rows, plan.counties
    weights, masses, pieces, refs = refs[:nl], refs[nl : 2 * nl], refs[2 * nl], refs[2 * nl + 1 :]
    totals, movers, refs = refs[:nl], refs[nl : 2 * nl], refs[2 * nl :]
    strip, full, weight, share, sums, sem = refs
    loc = at[0]
    copies = []
    for p in range(nl):
        for q in range(ni):
            size = plan.stride if q < ni - 1 else plan.quarter
            start = p * rows + q * plan.stride
            copies.append(
                pltpu.make_async_copy(
                    pieces.at[p * ni + q, pl.ds(0, size)], strip.at[pl.ds(start, size)], sem
                )
            )
    for c in copies:
        c.start()

    peak = weights[0][rows : rows + 1, :].astype(F32)
    for k in range(1, nl):
        peak = jnp.maximum(peak, weights[k][rows : rows + 1, :].astype(F32))
    for k in range(nl):
        scale = jnp.exp2(weights[k][rows : rows + 1, :].astype(F32) - peak)
        at_rows = pl.ds(pl.multiple_of((loc ^ k) * rows, TILE), rows)
        weight[at_rows, :] = (weights[k][:rows, :].astype(F32) * scale).astype(BF)

    for c in copies:
        c.wait()
    blocks = plan.block_rows
    for i in range(blocks):
        for k in range(plan.window // LANES):
            j = (i + k) % blocks
            tile = strip[i * LANES : (i + 1) * LANES, k * LANES : (k + 1) * LANES]
            full[i * LANES : (i + 1) * LANES, j * LANES : (j + 1) * LANES] = tile
            if k:
                full[j * LANES : (j + 1) * LANES, i * LANES : (i + 1) * LANES] = tile.T

    chunk = LANES * (5 if blocks % 5 == 0 else 1)

    def first(i, carry):
        r = pl.ds(pl.multiple_of(i * chunk, LANES), chunk)
        sums[r, :] = dot(full[r, :], weight[...])
        return carry

    lax.fori_loop(0, n // chunk, first, 0)
    for k in range(nl):
        r = pl.ds(pl.multiple_of((loc ^ k) * rows, TILE), rows)
        total = sums[r, :]
        totals[k][:rows, :] = total.astype(BF)
        totals[k][rows:, :] = jnp.broadcast_to(peak, (TILE, plan.states)).astype(BF)
        share[r, :] = (masses[k][...].astype(F32) / total).astype(BF)

    def second(i, carry):
        r = pl.ds(pl.multiple_of(i * chunk, LANES), chunk)
        sums[r, :] = dot(full[r, :], share[...])
        return carry

    lax.fori_loop(0, n // chunk, second, 0)
    for k in range(nl):
        r = pl.ds(pl.multiple_of((loc ^ k) * rows, TILE), rows)
        movers[k][...] = (weight[r, :].astype(F32) * sums[r, :]).astype(BF)


def tail_kernel(plan, at, *refs):
    ni, nl = plan.n_inc, plan.n_loc
    ins, (mix_a, mix_b), refs = refs[:nl], refs[nl : nl + 2], refs[nl + 2 :]
    outs, (held, mixed) = refs[:ni], refs[ni:]
    loc, inc, w = at[0], at[1], plan.wide
    for k in range(nl):
        held[:, lanes_at((loc ^ k) * plan.states, plan.states)] = ins[k][...]
    for g in range(plan.groups):
        x = held[:, g * w : (g + 1) * w]
        mixed[...] = (dot_nt(x, mix_a[...]) + dot_nt(x, mix_b[...])).astype(BF)
        for k in range(ni):
            outs[k][:, g * LANES : (g + 1) * LANES] = mixed[:, lanes_at((inc ^ k) * LANES, LANES)]


def restore(plan, inc, ins, second, held):
    for k in range(plan.n_inc):
        back = dot_nt(ins[k][...], second[...]).astype(BF)
        for t in range(plan.n_inc):
            held[t, :, lanes_at((inc ^ k) * LANES, LANES)] = back[:, t * LANES : (t + 1) * LANES]


def next_mass_kernel(plan, at, *refs):
    ni, w = plan.n_inc, plan.wide
    ins, (first, second), (out, held) = refs[:ni], refs[ni : ni + 2], refs[ni + 2 :]
    restore(plan, at[1], ins, second, held)
    for t in range(ni):
        out[:, t * w : (t + 1) * w] = dot_nt(held[t], first[...])


def value_kernel(plan, at, *refs):
    ni, w, rows = plan.n_inc, plan.wide, plan.rows
    ins, (hit, second, flow), (out, held) = refs[:ni], refs[ni : ni + 3], refs[ni + 3 :]
    restore(plan, at[1], ins, second, held)
    for t in range(ni):
        got = dot_nt(held[t], hit[t])
        peak = got[rows : rows + 1, :] * LN2 + SCORE_SHIFT
        out[:, t * w : (t + 1) * w] = flow[:, t * w : (t + 1) * w] + (peak + jnp.log(got[:rows, :]))


def mix_maps(plan, trans_weight):
    e = plan.incomes
    raised = trans_weight + 16.0 * jnp.eye(e, dtype=F32)
    prob = raised / jnp.sum(raised, axis=1, keepdims=True)
    ni, oi, ga = plan.n_inc, plan.own_incomes, plan.group_assets
    turned = prob.T.reshape(ni, 1, oi, ni, 1, oi)
    grid = jnp.broadcast_to(turned, (ni, ga, oi, ni, ga, oi)).reshape(plan.wide, plan.wide)
    r = lax.broadcasted_iota(jnp.int32, grid.shape, 0) // oi % ga
    c = lax.broadcasted_iota(jnp.int32, grid.shape, 1) // oi % ga
    grid = jnp.where(r == c, grid, 0.0)
    top = lax.reduce_precision(grid, 8, 7)
    return top.astype(BF), (grid - top).astype(BF)


def policy_maps(plan, asset_policy, inc):
    ni, oa, a, w = plan.n_inc, plan.own_assets, plan.assets, plan.wide
    own = lax.dynamic_slice_in_dim(asset_policy, inc * plan.own_incomes, plan.own_incomes, 0)
    group = w // a
    row_income = jnp.arange(group, dtype=jnp.int32)[None, :, None]
    own = own.reshape(ni, group, a)
    lane = own // oa * LANES + row_income * oa + own % oa
    lane = lane.reshape(ni, w, 1)
    return (lane == lax.broadcasted_iota(jnp.int32, (ni, w, w), 2)).astype(BF)


def swap(x, axis, n, k):
    if k == 0:
        return x
    return lax.ppermute(x, axis, [(s, s ^ k) for s in range(n)])


def far_first(n):
    return sorted(range(1, n), key=lambda k: -k)


def exchange(blocks, axis, n):
    got = {0: blocks[0]}
    for k in far_first(n):
        got[k] = swap(blocks[k], axis, n, k)
    return [got[k] for k in range(n)]


def state_split(plan, cont_value, flow_util, move_cost, live_mask, trans_weight, asset_policy, mass):
    ni, nl, rows, n = plan.n_inc, plan.n_loc, plan.rows, plan.counties
    w, part, states, packed = plan.wide, plan.part, plan.states, plan.packed
    S = jax.ShapeDtypeStruct
    loc, inc = lax.axis_index("loc"), lax.axis_index("inc")
    at = jnp.stack([loc, inc]).astype(jnp.int32)
    bind = lambda f: functools.partial(f, plan)
    pass_flops = 2 * rows * plan.columns * w

    first, second = order_maps(plan)
    codes = call(
        bind(encode_kernel),
        [S((rows, part), jnp.int16)] * ni,
        [at, cont_value, first, second],
        [pltpu.VMEM((ni, rows, w), BF)] * 2,
        4 * pass_flops,
    )
    codes = exchange(codes, "inc", ni)

    _, quarter = call(
        bind(window_kernel),
        [S((rows, plan.window), BF), S((plan.quarter, plan.window), BF)],
        [at, move_cost],
        [pltpu.VMEM((rows, n + plan.window - LANES), BF)],
    )
    pieces = lax.all_gather(quarter, ("loc", "inc"), axis=0)

    hit = policy_maps(plan, asset_policy, inc)
    masses = call(
        bind(mass_kernel),
        [S((rows, part), BF)] * ni,
        [at, mass, hit, second],
        [pltpu.VMEM((ni, rows, w), BF)],
        3 * pass_flops,
    )
    masses = exchange(masses, "inc", ni)
    masses = call(
        bind(spread_kernel),
        [S((rows, states), BF)] * nl,
        [at, *masses],
        [pltpu.VMEM((rows, plan.columns), BF)],
    )

    mix_a, mix_b = mix_maps(plan, trans_weight)
    live = (live_mask > 0).astype(F32)[:, None]
    weights = call(
        bind(weight_kernel),
        [S((packed, states), BF)] * nl,
        [at, *codes, mix_a, mix_b, live],
        [pltpu.VMEM((rows, w), jnp.int32), pltpu.VMEM((packed, plan.columns), BF)],
        3 * pass_flops,
    )
    weights = exchange(weights, "loc", nl)
    masses = exchange(masses, "loc", nl)

    out = call(
        bind(solve_kernel),
        [S((packed, states), BF)] * nl + [S((rows, states), BF)] * nl,
        [at, *weights, *masses, pieces],
        [
            pltpu.VMEM((n, plan.window), BF),
            pltpu.VMEM((n, n), BF),
            pltpu.VMEM((n, states), BF),
            pltpu.VMEM((n, states), BF),
            pltpu.VMEM((n, states), F32),
            pltpu.SemaphoreType.DMA,
        ],
        4 * n * n * states,
        [SMEM] + [VMEM] * (2 * nl) + [ANY],
        60,
    )
    totals, movers = out[:nl], out[nl:]
    movers = exchange(movers, "loc", nl)
    totals = exchange(totals, "loc", nl)

    moved = call(
        bind(tail_kernel),
        [S((rows, part), BF)] * ni,
        [at, *movers, mix_a, mix_b],
        [pltpu.VMEM((rows, plan.columns), BF), pltpu.VMEM((rows, w), BF)],
        2 * pass_flops,
    )
    moved = exchange(moved, "inc", ni)
    totals = call(
        bind(collect_kernel),
        [S((packed, part), BF)] * ni,
        [at, *totals],
        [pltpu.VMEM((packed, plan.columns), BF)],
    )
    totals = exchange(totals, "inc", ni)

    (new_mass,) = call(
        bind(next_mass_kernel),
        [S((rows, plan.columns), F32)],
        [at, *moved, first, second],
        [pltpu.VMEM((ni, rows, w), BF)],
        2 * pass_flops,
    )
    (new_value,) = call(
        bind(value_kernel),
        [S((rows, plan.columns), F32)],
        [at, *totals, hit, second, flow_util],
        [pltpu.VMEM((ni, packed, w), BF)],
        2 * pass_flops,
    )
    return new_value, new_mass


def gathered(cont_value, flow_util, move_cost, live_mask, trans_weight, asset_policy, mass):
    high = lax.Precision.HIGHEST
    e, a = asset_policy.shape
    raised = trans_weight + 16.0 * jnp.eye(e, dtype=F32)
    trans_prob = raised / jnp.sum(raised, axis=1, keepdims=True)
    onehot = (asset_policy[:, :, None] == jnp.arange(a, dtype=jnp.int32)[None, None, :]).astype(F32)
    moved_rows = lax.all_to_all(cont_value, "inc", split_axis=0, concat_axis=1, tiled=True)
    expect = jnp.einsum("ef,jfb->jeb", trans_prob, moved_rows.reshape(-1, e, a), precision=high)
    chosen_all = jnp.einsum("jeb,eab->jea", expect, onehot, precision=high).reshape(-1, e * a)
    chosen = lax.all_to_all(chosen_all, "inc", split_axis=1, concat_axis=0, tiled=True)
    scores = DISCOUNT * chosen
    live_rows = live_mask[:, None] > 0
    local_max = jnp.max(jnp.where(live_rows, scores, F32(-1e30)), axis=0)
    column_max = lax.pmax(local_max, "loc")
    dest_weight = jnp.where(live_rows, jnp.exp(scores - column_max[None, :]), F32(0.0)).astype(BF)
    kernel = jnp.exp(-move_cost).astype(BF)
    totals = dot(kernel, lax.all_gather(dest_weight, "loc", axis=0, tiled=True))
    new_value = flow_util + column_max[None, :] + jnp.log(totals)
    shares = (mass / totals).astype(BF)
    arrived = lax.psum_scatter(
        lax.dot_general(
            kernel, shares, (((0,), (0,)), ((), ())), preferred_element_type=F32
        ).astype(BF),
        "loc",
        scatter_dimension=0,
        tiled=True,
    ).astype(F32)
    movers = dest_weight.astype(F32) * arrived
    moved_mass = lax.all_to_all(movers, "inc", split_axis=0, concat_axis=1, tiled=True)
    shuffled = jnp.einsum("jea,eab->jeb", moved_mass.reshape(-1, e, a), onehot, precision=high)
    mixed_mass = jnp.einsum("ef,jeb->jfb", trans_prob, shuffled, precision=high).reshape(-1, e * a)
    new_mass = lax.all_to_all(mixed_mass, "inc", split_axis=1, concat_axis=0, tiled=True)
    return new_value, new_mass


def solution(mesh):
    n_loc, n_inc = mesh.shape["loc"], mesh.shape["inc"]

    def shards(*args):
        rows, columns = args[0].shape
        plan = Plan(n_loc, n_inc, args[2].shape[1], rows, columns, *args[5].shape)
        if plan.fits():
            return state_split(plan, *args)
        return gathered(*args)

    split = P("loc", "inc")
    return jax.shard_map(
        shards,
        mesh=mesh,
        in_specs=(split, split, P("loc", None), P("loc"), P(), P(), split),
        out_specs=(split, split),
        check_vma=False,
    )
```

time: 557 us -> 333 us (0.60)
  waiting for transfers between devices: 327 us -> 168 us
  blocking collectives: 100 us -> 0 us
  Pallas kernels: 0 us -> 62.2 us
  matrix products: 55.9 us -> 0 us
  starting transfers between devices: 7.79 us -> 57.4 us
  local copies, waits for them, and re-layouts: 42.9 us -> 20.8 us
    ppermute x0 -> x40, waiting for transfers between devices: none -> 168 us  [swap(): return lax.ppermute(x, axis, [(s, s ^ k) for s in range(n)])]
    reduce_scatter x1 -> x0, waiting for transfers between devices: 133 us -> none  [shards(): lax.psum_scatter(lax.dot_general(columns, shares, (((0,), (0,)), ((), ())...]
    all_gather x1, waiting for transfers between devices: 118 us -> 0.01 us  [state_split(): pieces = lax.all_gather(quarter, ('loc', 'inc'), axis=0)]
    all_to_all x2 -> x0, blocking collectives: 87.6 us -> none  [the longest x1 44.1 us: shards(): lax.all_to_all(movers, 'inc', split_axis=0, concat_axis=1, tiled=True)]
    all_to_all x2 -> x0, waiting for transfers between devices: 76.4 us -> none  [the longest x1 38.2 us: shards(): lax.all_to_all(chosen_all, 'inc', split_axis=1, concat_axis=0, tiled=True)]
    pallas_call x0 -> x10, Pallas kernels: none -> 62.2 us  [call(): pl.pallas_call(kernel, out_shape=tuple(outs), in_specs=specs or [SMEM] +...]
    ppermute x0 -> x40, starting transfers between devices: none -> 57.4 us  [swap(): return lax.ppermute(x, axis, [(s, s ^ k) for s in range(n)])]
    dot_general x6 -> x0, matrix products: 55.9 us -> none  [the longest x1 13.3 us: shards(): jnp.dot(columns, lax.all_gather(dest_weight, 'loc', axis=0, tiled=True),...]
  transfers between devices with their start and end apart: 4 -> 41, of which waited for: 4 -> 24; matrix products, arithmetic and copies ran while one was open for 0% -> 5% of each run, Pallas kernels for 0% -> 8%
where the time goes in v1:
time: 333 us; the launch traced here: 329 us
  waiting for transfers between devices  168 us (50%)
  Pallas kernels  62.2 us (19%)
  starting transfers between devices  57.4 us (17%)
  local copies, waits for them, and re-layouts  20.8 us (6%)
  between operations  14.5 us (4%)
  other arithmetic  5.86 us (2%)
    ppermute x40, waiting for transfers between devices, swap(): return lax.ppermute(x, axis, [(s, s ^ k) for s in range(n)])  168 us
    pallas_call x10, Pallas kernels, call(): pl.pallas_call(kernel, out_shape=tuple(outs), in_specs=specs or [SMEM] +...  62.2 us
    ppermute x40, starting transfers between devices, swap(): return lax.ppermute(x, axis, [(s, s ^ k) for s in range(n)])  57.4 us
    unnamed x74, local copies, waits for them, and re-layouts  9.44 us
  transfers between devices with their start and end apart: 41, of which 24 were waited for; matrix products, arithmetic and copies ran while one was open for 5% of the time, Pallas kernels for 8%

profile of v1, /device:TPU:8, one launch (start us, length us, event | category | flops | bytes accessed | tf_op | source)
XLA Modules:
  0.0 329.0 jit_solution(5043134158232277502)
XLA Ops:
  7.3 4.7 %shard_map.90 = (bf16[400,1664]{1,0:T(8,128)(2,1)}, bf16[112,1664]{1,0:T(8,128)(2,1)}) custom-call(s32[2]{0:T(128)S(1)} %pad_add_fusion.at, f32[400,3200]{1,0:T(8,128)} %cost.1), custom_call_target="tpu_custom_call" | custom-call | bytes 6823944 | tf_op jit(solution)/shard_map/pallas_call | solution.py:43
  12.1 1.2 fusion.15
  13.4 2.1 copy-done.11
  15.5 5.2 %shard_map.86 = (s16[400,512]{1,0:T(8,128)(2,1)S(1)}, s16[400,512]{1,0:T(8,128)(2,1)}, s16[400,512]{1,0:T(8,128)(2,1)}, s16[400,512]{1,0:T(8,128)(2,1)}) custom-call(s32[2]{0:T(128)S(1)} %pad_add_fusion.at, f32[400,2048]{1,0:T(8,128)S(1)} %copy-done.11, bf16[512,512]{1,0:T(8,128)(2,1)S(1)} %get-tuple-element.103.first.refs_4_, ...), custom_call_target="tpu_custom_call" | custom-call | flops 3355443200 | bytes 5963784 | tf_op jit(solution)/shard_map/pallas_call | solution.py:43
  21.4 1.5 collective-permute-start
  22.9 1.5 collective-permute-start.1
  25.9 5.4 %shard_map.88 = (bf16[400,512]{1,0:T(8,128)(2,1)S(1)}, bf16[400,512]{1,0:T(8,128)(2,1)}, bf16[400,512]{1,0:T(8,128)(2,1)}, bf16[400,512]{1,0:T(8,128)(2,1)S(1)}) custom-call(s32[2]{0:T(128)S(1)} %pad_add_fusion.at, f32[400,2048]{1,0:T(8,128)} %mass.1, bf16[4,512,512]{2,1,0:T(8,128)(2,1)S(1)} %fusion.hit.refs_4_, ...), custom_call_target="tpu_custom_call" | custom-call | flops 2516582400 | bytes 7536648 | tf_op jit(solution)/shard_map/pallas_call | solution.py:43
  32.0 1.5 collective-permute-start.10
  33.5 1.5 collective-permute-start.11
  36.2 1.1 copy.10
  37.3 2.8 broadcast_in_dim.19
  40.0 6.1 %reshape.77 = f32[512,512]{1,0:T(8,128)} reshape(f32[4,4,32,4,4,32]{5,4,3,2,1,0:T(4,128)} %broadcast_in_dim.19) | data formatting | bytes 2097152 | tf_op jit(solution)/shard_map/reshape | solution.py:305
  46.2 2.4 fusion.4
  48.6 13.2 %collective-permute-done.10.refs_1_ = bf16[400,512]{1,0:T(8,128)(2,1)} collective-permute-done((bf16[400,512]{1,0:T(8,128)(2,1)}, bf16[400,512]{1,0:T(8,128)(2,1)}, u32[]{:S(2)}, u32[]{:S(2)}) %collective-permute-start.10) | collective-permute-done | bytes 409632 | tf_op jit(solution)/shard_map/ppermute | solution.py:327
  61.8 2.5 collective-permute-start.12
  64.4 1.3 reduce-precision_convert_fusion.refs_4_.refs_8_
  65.8 7.8 %collective-permute-done.12.refs_3_ = bf16[400,512]{1,0:T(8,128)(2,1)} collective-permute-done((bf16[400,512]{1,0:T(8,128)(2,1)}, bf16[400,512]{1,0:T(8,128)(2,1)}, u32[]{:S(2)}, u32[]{:S(2)}) %collective-permute-start.12) | collective-permute-done | bytes 409632 | tf_op jit(solution)/shard_map/ppermute | solution.py:327
  73.6 1.0 copy-done.7
  74.6 1.9 shard_map.89
  77.1 1.3 collective-permute-start.15
  78.5 2.6 collective-permute-start.16
  81.1 1.0 copy-done.16
  82.1 5.6 %shard_map.87 = (bf16[416,256]{1,0:T(8,128)(2,1)S(1)}, bf16[416,256]{1,0:T(8,128)(2,1)S(1)}, bf16[416,256]{1,0:T(8,128)(2,1)S(1)}, bf16[416,256]{1,0:T(8,128)(2,...) custom-call(s32[2]{0:T(128)S(1)} %pad_add_fusion.at, ...), custom_call_target="tpu_custom_call" | custom-call | flops 2516582400 | bytes 4392520 | tf_op jit(solution)/shard_map/pallas_call | solution.py:43
  88.9 10.1 %collective-permute-done.14.refs_10_ = bf16[400,256]{1,0:T(8,128)(2,1)S(1)} collective-permute-done((bf16[400,256]{1,0:T(8,128)(2,1)S(1)}, bf16[400,256]{1,0:T(8,128)(2,1)S(1)}, u32[]{:S(2)}, u32[]{:S(2)}) %collective-permute-start.14) | collective-permute-done | bytes 204832 | tf_op jit(solution)/shard_map/ppermute | solution.py:327
  99.0 6.0 %collective-permute-start.17 = (bf16[400,256]{1,0:T(8,128)(2,1)S(1)}, bf16[400,256]{1,0:T(8,128)(2,1)S(1)}, u32[]{:S(2)}, u32[]{:S(2)}) collective-permute-start(bf16[400,256]{1,0:T(8,128)(2,1)S(1)} %get-tuple-element.72), channel_id=1, source_target_pairs={{0,20},{4,16},{8,28},{12,24},{16,4},{20,0},{24,12},{28,8},{1,21},{... | collective-permute-start | bytes 614408 | tf_op jit(solution)/shard_map/ppermute | solution.py:327
  105.0 12.3 %collective-permute-done.15.refs_11_ = bf16[400,256]{1,0:T(8,128)(2,1)S(1)} collective-permute-done((bf16[400,256]{1,0:T(8,128)(2,1)S(1)}, bf16[400,256]{1,0:T(8,128)(2,1)S(1)}, u32[]{:S(2)}, u32[]{:S(2)}) %collective-permute-start.15) | collective-permute-done | bytes 204832 | tf_op jit(solution)/shard_map/ppermute | solution.py:327
  117.3 3.6 %collective-permute-start.18 = (bf16[400,256]{1,0:T(8,128)(2,1)S(1)}, bf16[400,256]{1,0:T(8,128)(2,1)S(1)}, u32[]{:S(2)}, u32[]{:S(2)}) collective-permute-start(bf16[400,256]{1,0:T(8,128)(2,1)S(1)} %get-tuple-element.73), channel_id=1, source_target_pairs={{0,24},{4,28},{8,16},{12,20},{16,8},{20,12},{24,0},{28,4},{1,25},{... | collective-permute-start | bytes 614408 | tf_op jit(solution)/shard_map/ppermute | solution.py:327
  120.9 3.8 %collective-permute-done.17.refs_13_ = bf16[400,256]{1,0:T(8,128)(2,1)S(1)} collective-permute-done((bf16[400,256]{1,0:T(8,128)(2,1)S(1)}, bf16[400,256]{1,0:T(8,128)(2,1)S(1)}, u32[]{:S(2)}, u32[]{:S(2)}) %collective-permute-start.17) | collective-permute-done | bytes 204832 | tf_op jit(solution)/shard_map/ppermute | solution.py:327
  125.4 18.8 %collective-permute-done.18.refs_14_ = bf16[400,256]{1,0:T(8,128)(2,1)S(1)} collective-permute-done((bf16[400,256]{1,0:T(8,128)(2,1)S(1)}, bf16[400,256]{1,0:T(8,128)(2,1)S(1)}, u32[]{:S(2)}, u32[]{:S(2)}) %collective-permute-start.18) | collective-permute-done | bytes 204832 | tf_op jit(solution)/shard_map/ppermute | solution.py:327
  144.9 3.2 collective-permute-done.19.refs_15_
  148.2 10.8 %collective-permute-start.9 = (bf16[416,256]{1,0:T(8,128)(2,1)S(1)}, bf16[416,256]{1,0:T(8,128)(2,1)}, u32[]{:S(2)}, u32[]{:S(2)}) collective-permute-start(bf16[416,256]{1,0:T(8,128)(2,1)S(1)} %get-tuple-element.62), channel_id=1, source_target_pairs={{0,28},{4,24},{8,20},{12,16},{16,12},{20,8},{24,4},{28,0},{1,29},{... | collective-permute-start | bytes 638984 | tf_op jit(solution)/shard_map/ppermute | solution.py:327
  159.0 2.4 collective-permute-done.6.refs_4_
  161.5 11.4 %collective-permute-done.7.refs_5_ = bf16[416,256]{1,0:T(8,128)(2,1)S(1)} collective-permute-done((bf16[416,256]{1,0:T(8,128)(2,1)S(1)}, bf16[416,256]{1,0:T(8,128)(2,1)S(1)}, u32[]{:S(2)}, u32[]{:S(2)}) %collective-permute-start.7) | collective-permute-done | bytes 213024 | tf_op jit(solution)/shard_map/ppermute | solution.py:327
  172.9 7.7 %collective-permute-done.8.refs_6_ = bf16[416,256]{1,0:T(8,128)(2,1)S(1)} collective-permute-done((bf16[416,256]{1,0:T(8,128)(2,1)S(1)}, bf16[416,256]{1,0:T(8,128)(2,1)S(1)}, u32[]{:S(2)}, u32[]{:S(2)}) %collective-permute-start.8) | collective-permute-done | bytes 213024 | tf_op jit(solution)/shard_map/ppermute | solution.py:327
  181.3 3.4 %collective-permute-done.9.refs_7_ = bf16[416,256]{1,0:T(8,128)(2,1)} collective-permute-done((bf16[416,256]{1,0:T(8,128)(2,1)S(1)}, bf16[416,256]{1,0:T(8,128)(2,1)}, u32[]{:S(2)}, u32[]{:S(2)}) %collective-permute-start.9) | collective-permute-done | bytes 213024 | tf_op jit(solution)/shard_map/ppermute | solution.py:327
  184.7 24.5 %shard_map.91 = (bf16[416,256]{1,0:T(8,128)(2,1)}, bf16[416,256]{1,0:T(8,128)(2,1)}, bf16[416,256]{1,0:T(8,128)(2,1)}, bf16[416,256]{1,0:T(8,128)(2,1)}, bf16[41...) custom-call(s32[2]{0:T(128)} %copy-done.9, ...), custom_call_target="tpu_custom_call" | custom-call | flops 10485760000 | bytes 18612232 | tf_op jit(solution)/shard_map/pallas_call | solution.py:43
  209.4 1.7 collective-permute-start.32
  211.1 2.7 collective-permute-start.34
  213.8 8.1 %collective-permute-done.31.refs_2_ = bf16[400,256]{1,0:T(8,128)(2,1)S(1)} collective-permute-done((bf16[400,256]{1,0:T(8,128)(2,1)}, bf16[400,256]{1,0:T(8,128)(2,1)S(1)}, u32[]{:S(2)}, u32[]{:S(2)}) %collective-permute-start.31) | collective-permute-done | bytes 204832 | tf_op jit(solution)/shard_map/ppermute | solution.py:327
  221.9 4.1 %collective-permute-done.32.refs_3_ = bf16[400,256]{1,0:T(8,128)(2,1)S(1)} collective-permute-done((bf16[400,256]{1,0:T(8,128)(2,1)}, bf16[400,256]{1,0:T(8,128)(2,1)S(1)}, u32[]{:S(2)}, u32[]{:S(2)}) %collective-permute-start.32) | collective-permute-done | bytes 204832 | tf_op jit(solution)/shard_map/ppermute | solution.py:327
  226.0 2.5 collective-permute-start.21
  228.5 10.2 %collective-permute-done.34.refs_5_ = bf16[400,256]{1,0:T(8,128)(2,1)S(1)} collective-permute-done((bf16[400,256]{1,0:T(8,128)(2,1)}, bf16[400,256]{1,0:T(8,128)(2,1)S(1)}, u32[]{:S(2)}, u32[]{:S(2)}) %collective-permute-start.34) | collective-permute-done | bytes 204832 | tf_op jit(solution)/shard_map/ppermute | solution.py:327
  238.7 3.2 collective-permute-start.22
  241.9 3.5 %collective-permute-done.35.refs_6_ = bf16[400,256]{1,0:T(8,128)(2,1)S(1)} collective-permute-done((bf16[400,256]{1,0:T(8,128)(2,1)}, bf16[400,256]{1,0:T(8,128)(2,1)S(1)}, u32[]{:S(2)}, u32[]{:S(2)}) %collective-permute-start.35) | collective-permute-done | bytes 204832 | tf_op jit(solution)/shard_map/ppermute | solution.py:327
  245.4 2.8 collective-permute-done.36.refs_7_
  248.2 0.9 copy-done.14
  249.2 2.8 shard_map.94
  252.0 1.7 collective-permute-start.37
  253.8 2.6 collective-permute-start.24
  258.2 19.5 %collective-permute-done.23.refs_4_ = bf16[416,256]{1,0:T(8,128)(2,1)S(1)} collective-permute-done((bf16[416,256]{1,0:T(8,128)(2,1)S(1)}, bf16[416,256]{1,0:T(8,128)(2,1)S(1)}, u32[]{:S(2)}, u32[]{:S(2)}) %collective-permute-start.23) | collective-permute-done | bytes 213024 | tf_op jit(solution)/shard_map/ppermute | solution.py:327
  277.6 1.5 collective-permute-start.38
  279.1 3.1 collective-permute-done.24.refs_5_
  282.2 1.3 collective-permute-start.39
  283.6 5.1 %collective-permute-done.25.refs_6_ = bf16[416,256]{1,0:T(8,128)(2,1)S(1)} collective-permute-done((bf16[416,256]{1,0:T(8,128)(2,1)S(1)}, bf16[416,256]{1,0:T(8,128)(2,1)S(1)}, u32[]{:S(2)}, u32[]{:S(2)}) %collective-permute-start.25) | collective-permute-done | bytes 213024 | tf_op jit(solution)/shard_map/ppermute | solution.py:327
  288.6 2.9 collective-permute-done.26.refs_7_
  291.5 1.2 shard_map.92
  293.2 1.5 collective-permute-start.28
  294.7 1.6 collective-permute-start.29
  296.3 1.7 collective-permute-done.38.refs_2_
  298.0 4.3 %shard_map.95 = f32[400,2048]{1,0:T(8,128)} custom-call(s32[2]{0:T(128)S(1)} %copy-done.10, bf16[400,512]{1,0:T(8,128)(2,1)S(1)} %get-tuple-element.96.refs_0_, bf16[400,512]{1,0:T(8,128)(2,1)S(1)} %collective-permute-done.37.refs_1_, bf16[400,512]{1,0:T(8,128)(2,1)S(1)} %collective-permute-done.38.refs_2_, ...), custom_call_target="tpu_custom_call" | custom-call | flops 1677721600 | bytes 5963784 | tf_op jit(solution)/shard_map/pallas_call | solution.py:43
  302.3 3.2 collective-permute-done.27.refs_1_
  305.5 9.0 %collective-permute-done.28.refs_2_ = bf16[416,512]{1,0:T(8,128)(2,1)S(1)} collective-permute-done((bf16[416,512]{1,0:T(8,128)(2,1)S(1)}, bf16[416,512]{1,0:T(8,128)(2,1)S(1)}, u32[]{:S(2)}, u32[]{:S(2)}) %collective-permute-start.28) | collective-permute-done | bytes 426016 | tf_op jit(solution)/shard_map/ppermute | solution.py:327
  314.5 1.0 collective-permute-done.29.refs_3_
  315.5 6.6 %shard_map.93 = f32[400,2048]{1,0:T(8,128)} custom-call(s32[2]{0:T(128)S(1)} %copy-done.10, bf16[416,512]{1,0:T(8,128)(2,1)S(1)} %get-tuple-element.84.refs_0_, bf16[416,512]{1,0:T(8,128)(2,1)S(1)} %collective-permute-done.27.refs_1_, bf16[416,512]{1,0:T(8,128)(2,1)S(1)} %collective-permute-done.28.refs_2_, ...), custom_call_target="tpu_custom_call" | custom-call | flops 1677721600 | bytes 10878984 | tf_op jit(solution)/shard_map/pallas_call | solution.py:43
  (131 shorter events, 10.9 us)
Async XLA Ops:
  7.2 17.8 %copy-start = (s32[128,64]{0,1:T(8,128)S(1)}, s32[128,64]{0,1:T(8,128)}, u32[]{:S(2)}) copy-start(s32[128,64]{0,1:T(8,128)} %param.12) | copy-start | bytes 98308
  7.2 177.5 %all-gather.3.cloned.1.call-start = ((), (), s32[]{:S(2)}) async-start(), calls=%async_computation | async-start | bytes 12300288 | tf_op jit(solution)/shard_map/all_gather | solution.py:366
  7.3 73.8 %copy-start.9 = (s32[2]{0:T(128)}, s32[2]{0:T(128)S(1)}, u32[]{:S(2)}) copy-start(s32[2]{0:T(128)S(1)} %pad_add_fusion.at) | copy-start | bytes 28
  13.4 7.3 %copy-start.4 = (bf16[512,512]{1,0:T(8,128)(2,1)}, bf16[512,512]{1,0:T(8,128)(2,1)S(1)}, u32[]{:S(2)}) copy-start(bf16[512,512]{1,0:T(8,128)(2,1)S(1)} %get-tuple-element.103.first.refs_4_) | copy-start | bytes 1572868
  21.4 55.7 %collective-permute-start = (s16[400,512]{1,0:T(8,128)(2,1)}, s16[400,512]{1,0:T(8,128)(2,1)}, u32[]{:S(2)}, u32[]{:S(2)}) collective-permute-start(s16[400,512]{1,0:T(8,128)(2,1)} %get-tuple-element.52), channel_id=1, source_target_pairs={{0,1},{1,0},{2,3},{3,2},{4,5},{5,4},{6,7},{7,6},{8,9},{9,8},{10,11... | collective-permute-start | bytes 1228808 | tf_op jit(solution)/shard_map/ppermute | solution.py:327
  22.9 55.5 %collective-permute-start.1 = (s16[400,512]{1,0:T(8,128)(2,1)}, s16[400,512]{1,0:T(8,128)(2,1)}, u32[]{:S(2)}, u32[]{:S(2)}) collective-permute-start(s16[400,512]{1,0:T(8,128)(2,1)} %get-tuple-element.53), channel_id=1, source_target_pairs={{0,2},{1,3},{2,0},{3,1},{4,6},{5,7},{6,4},{7,5},{8,10},{9,11},{10,... | collective-permute-start | bytes 1228808 | tf_op jit(solution)/shard_map/ppermute | solution.py:327
  24.5 56.6 %collective-permute-start.2 = (s16[400,512]{1,0:T(8,128)(2,1)}, s16[400,512]{1,0:T(8,128)(2,1)}, u32[]{:S(2)}, u32[]{:S(2)}) collective-permute-start(s16[400,512]{1,0:T(8,128)(2,1)} %get-tuple-element.54), channel_id=1, source_target_pairs={{0,3},{1,2},{2,1},{3,0},{4,7},{5,6},{6,5},{7,4},{8,11},{9,10},{10,... | collective-permute-start | bytes 1228808 | tf_op jit(solution)/shard_map/ppermute | solution.py:327
  25.9 9.2 %copy-start.18 = (f32[128,128]{1,0:T(8,128)S(1)}, f32[128,128]{1,0:T(8,128)}, u32[]{:S(2)}) copy-start(f32[128,128]{1,0:T(8,128)} %param.11) | copy-start | bytes 196612
  32.0 14.1 %copy-start.12 = (bf16[400,512]{1,0:T(8,128)(2,1)}, bf16[400,512]{1,0:T(8,128)(2,1)S(1)}, u32[]{:S(2)}) copy-start(bf16[400,512]{1,0:T(8,128)(2,1)S(1)} %get-tuple-element.66) | copy-start | bytes 1228804
  32.0 29.7 %collective-permute-start.10 = (bf16[400,512]{1,0:T(8,128)(2,1)}, bf16[400,512]{1,0:T(8,128)(2,1)}, u32[]{:S(2)}, u32[]{:S(2)}) collective-permute-start(bf16[400,512]{1,0:T(8,128)(2,1)} %get-tuple-element.64), channel_id=1, source_target_pairs={{0,1},{1,0},{2,3},{3,2},{4,5},{5,4},{6,7},{7,6},{8,9},{9,8},{10,11... | collective-permute-start | bytes 1228808 | tf_op jit(solution)/shard_map/ppermute | solution.py:327
  33.5 32.2 %collective-permute-start.11 = (bf16[400,512]{1,0:T(8,128)(2,1)}, bf16[400,512]{1,0:T(8,128)(2,1)}, u32[]{:S(2)}, u32[]{:S(2)}) collective-permute-start(bf16[400,512]{1,0:T(8,128)(2,1)} %get-tuple-element.65), channel_id=1, source_target_pairs={{0,2},{1,3},{2,0},{3,1},{4,6},{5,7},{6,4},{7,5},{8,10},{9,11},{10,... | collective-permute-start | bytes 1228808 | tf_op jit(solution)/shard_map/ppermute | solution.py:327
  40.0 24.2 %copy-start.19 = (s32[400]{0:T(512)S(1)}, s32[400]{0:T(512)}, u32[]{:S(2)}) copy-start(s32[400]{0:T(512)} %param.10) | copy-start | bytes 4804
  61.8 11.8 %collective-permute-start.12 = (bf16[400,512]{1,0:T(8,128)(2,1)}, bf16[400,512]{1,0:T(8,128)(2,1)}, u32[]{:S(2)}, u32[]{:S(2)}) collective-permute-start(bf16[400,512]{1,0:T(8,128)(2,1)} %copy-done.12), channel_id=1, source_target_pairs={{0,3},{1,2},{2,1},{3,0},{4,7},{5,6},{6,5},{7,4},{8,11},{9,10},{10,... | collective-permute-start | bytes 1228808 | tf_op jit(solution)/shard_map/ppermute | solution.py:327
  65.8 21.9 %copy-start.2 = (bf16[512,512]{1,0:T(8,128)(2,1)}, bf16[512,512]{1,0:T(8,128)(2,1)S(1)}, u32[]{:S(2)}) copy-start(bf16[512,512]{1,0:T(8,128)(2,1)S(1)} %reduce-precision_convert_fusion.refs_4_.refs_8_) | copy-start | bytes 1572868
  76.5 11.2 %copy-start.13 = (bf16[400,256]{1,0:T(8,128)(2,1)}, bf16[400,256]{1,0:T(8,128)(2,1)S(1)}, u32[]{:S(2)}) copy-start(bf16[400,256]{1,0:T(8,128)(2,1)S(1)} %get-tuple-element.67.refs_8_) | copy-start | bytes 614404
  76.5 11.9 %collective-permute-start.13 = (bf16[400,256]{1,0:T(8,128)(2,1)S(1)}, bf16[400,256]{1,0:T(8,128)(2,1)S(1)}, u32[]{:S(2)}, u32[]{:S(2)}) collective-permute-start(bf16[400,256]{1,0:T(8,128)(2,1)S(1)} %get-tuple-element.68), channel_id=1, source_target_pairs={{0,4},{4,0},{8,12},{12,8},{16,20},{20,16},{24,28},{28,24},{1,5},{5... | collective-permute-start | bytes 614408 | tf_op jit(solution)/shard_map/ppermute | solution.py:327
  76.6 22.4 %collective-permute-start.14 = (bf16[400,256]{1,0:T(8,128)(2,1)S(1)}, bf16[400,256]{1,0:T(8,128)(2,1)S(1)}, u32[]{:S(2)}, u32[]{:S(2)}) collective-permute-start(bf16[400,256]{1,0:T(8,128)(2,1)S(1)} %get-tuple-element.69), channel_id=1, source_target_pairs={{0,8},{4,12},{8,0},{12,4},{16,24},{20,28},{24,16},{28,20},{1,9},{5... | collective-permute-start | bytes 614408 | tf_op jit(solution)/shard_map/ppermute | solution.py:327
  77.1 40.1 %collective-permute-start.15 = (bf16[400,256]{1,0:T(8,128)(2,1)S(1)}, bf16[400,256]{1,0:T(8,128)(2,1)S(1)}, u32[]{:S(2)}, u32[]{:S(2)}) collective-permute-start(bf16[400,256]{1,0:T(8,128)(2,1)S(1)} %get-tuple-element.70), channel_id=1, source_target_pairs={{0,12},{4,8},{8,4},{12,0},{16,28},{20,24},{24,20},{28,16},{1,13},{... | collective-permute-start | bytes 614408 | tf_op jit(solution)/shard_map/ppermute | solution.py:327
  78.5 42.4 %collective-permute-start.16 = (bf16[400,256]{1,0:T(8,128)(2,1)S(1)}, bf16[400,256]{1,0:T(8,128)(2,1)S(1)}, u32[]{:S(2)}, u32[]{:S(2)}) collective-permute-start(bf16[400,256]{1,0:T(8,128)(2,1)S(1)} %get-tuple-element.71), channel_id=1, source_target_pairs={{0,16},{4,20},{8,24},{12,28},{16,0},{20,4},{24,8},{28,12},{1,17},{... | collective-permute-start | bytes 614408 | tf_op jit(solution)/shard_map/ppermute | solution.py:327
  88.4 59.7 %collective-permute-start.3 = (bf16[416,256]{1,0:T(8,128)(2,1)S(1)}, bf16[416,256]{1,0:T(8,128)(2,1)S(1)}, u32[]{:S(2)}, u32[]{:S(2)}) collective-permute-start(bf16[416,256]{1,0:T(8,128)(2,1)S(1)} %get-tuple-element.56), channel_id=1, source_target_pairs={{0,4},{4,0},{8,12},{12,8},{16,20},{20,16},{24,28},{28,24},{1,5},{5... | collective-permute-start | bytes 638984 | tf_op jit(solution)/shard_map/ppermute | solution.py:327
  88.5 92.1 %copy-start.30 = (bf16[400,256]{1,0:T(8,128)(2,1)}, bf16[400,256]{1,0:T(8,128)(2,1)S(1)}, u32[]{:S(2)}) copy-start(bf16[400,256]{1,0:T(8,128)(2,1)S(1)} %collective-permute-done.13.refs_9_) | copy-start | bytes 614404
  88.5 59.7 %collective-permute-start.4 = (bf16[416,256]{1,0:T(8,128)(2,1)S(1)}, bf16[416,256]{1,0:T(8,128)(2,1)S(1)}, u32[]{:S(2)}, u32[]{:S(2)}) collective-permute-start(bf16[416,256]{1,0:T(8,128)(2,1)S(1)} %get-tuple-element.57), channel_id=1, source_target_pairs={{0,8},{4,12},{8,0},{12,4},{16,24},{20,28},{24,16},{28,20},{1,9},{5... | collective-permute-start | bytes 638984 | tf_op jit(solution)/shard_map/ppermute | solution.py:327
  99.0 81.6 %copy-start.31 = (bf16[400,256]{1,0:T(8,128)(2,1)}, bf16[400,256]{1,0:T(8,128)(2,1)S(1)}, u32[]{:S(2)}) copy-start(bf16[400,256]{1,0:T(8,128)(2,1)S(1)} %collective-permute-done.14.refs_10_) | copy-start | bytes 614404
  99.0 25.8 %collective-permute-start.17 = (bf16[400,256]{1,0:T(8,128)(2,1)S(1)}, bf16[400,256]{1,0:T(8,128)(2,1)S(1)}, u32[]{:S(2)}, u32[]{:S(2)}) collective-permute-start(bf16[400,256]{1,0:T(8,128)(2,1)S(1)} %get-tuple-element.72), channel_id=1, source_target_pairs={{0,20},{4,16},{8,28},{12,24},{16,4},{20,0},{24,12},{28,8},{1,21},{... | collective-permute-start | bytes 614408 | tf_op jit(solution)/shard_map/ppermute | solution.py:327
  117.3 63.3 %copy-start.32 = (bf16[400,256]{1,0:T(8,128)(2,1)}, bf16[400,256]{1,0:T(8,128)(2,1)S(1)}, u32[]{:S(2)}) copy-start(bf16[400,256]{1,0:T(8,128)(2,1)S(1)} %collective-permute-done.15.refs_11_) | copy-start | bytes 614404
  117.3 26.9 %collective-permute-start.18 = (bf16[400,256]{1,0:T(8,128)(2,1)S(1)}, bf16[400,256]{1,0:T(8,128)(2,1)S(1)}, u32[]{:S(2)}, u32[]{:S(2)}) collective-permute-start(bf16[400,256]{1,0:T(8,128)(2,1)S(1)} %get-tuple-element.73), channel_id=1, source_target_pairs={{0,24},{4,28},{8,16},{12,20},{16,8},{20,12},{24,0},{28,4},{1,25},{... | collective-permute-start | bytes 614408 | tf_op jit(solution)/shard_map/ppermute | solution.py:327
  120.9 59.7 %copy-start.33 = (bf16[400,256]{1,0:T(8,128)(2,1)}, bf16[400,256]{1,0:T(8,128)(2,1)S(1)}, u32[]{:S(2)}) copy-start(bf16[400,256]{1,0:T(8,128)(2,1)S(1)} %collective-permute-done.16.refs_12_) | copy-start | bytes 614404
  120.9 27.2 %collective-permute-start.19 = (bf16[400,256]{1,0:T(8,128)(2,1)S(1)}, bf16[400,256]{1,0:T(8,128)(2,1)S(1)}, u32[]{:S(2)}, u32[]{:S(2)}) collective-permute-start(bf16[400,256]{1,0:T(8,128)(2,1)S(1)} %get-tuple-element.74), channel_id=1, source_target_pairs={{0,28},{4,24},{8,20},{12,16},{16,12},{20,8},{24,4},{28,0},{1,29},{... | collective-permute-start | bytes 614408 | tf_op jit(solution)/shard_map/ppermute | solution.py:327
  125.4 33.6 %collective-permute-start.5 = (bf16[416,256]{1,0:T(8,128)(2,1)S(1)}, bf16[416,256]{1,0:T(8,128)(2,1)S(1)}, u32[]{:S(2)}, u32[]{:S(2)}) collective-permute-start(bf16[416,256]{1,0:T(8,128)(2,1)S(1)} %get-tuple-element.58), channel_id=1, source_target_pairs={{0,12},{4,8},{8,4},{12,0},{16,28},{20,24},{24,20},{28,16},{1,13},{... | collective-permute-start | bytes 638984 | tf_op jit(solution)/shard_map/ppermute | solution.py:327
  144.9 16.5 %collective-permute-start.6 = (bf16[416,256]{1,0:T(8,128)(2,1)S(1)}, bf16[416,256]{1,0:T(8,128)(2,1)S(1)}, u32[]{:S(2)}, u32[]{:S(2)}) collective-permute-start(bf16[416,256]{1,0:T(8,128)(2,1)S(1)} %get-tuple-element.59), channel_id=1, source_target_pairs={{0,16},{4,20},{8,24},{12,28},{16,0},{20,4},{24,8},{28,12},{1,17},{... | collective-permute-start | bytes 638984 | tf_op jit(solution)/shard_map/ppermute | solution.py:327
  148.1 32.5 %copy-start.36 = (bf16[400,256]{1,0:T(8,128)(2,1)}, bf16[400,256]{1,0:T(8,128)(2,1)S(1)}, u32[]{:S(2)}) copy-start(bf16[400,256]{1,0:T(8,128)(2,1)S(1)} %collective-permute-done.19.refs_15_) | copy-start | bytes 614404
  148.1 24.8 %collective-permute-start.7 = (bf16[416,256]{1,0:T(8,128)(2,1)S(1)}, bf16[416,256]{1,0:T(8,128)(2,1)S(1)}, u32[]{:S(2)}, u32[]{:S(2)}) collective-permute-start(bf16[416,256]{1,0:T(8,128)(2,1)S(1)} %get-tuple-element.60), channel_id=1, source_target_pairs={{0,20},{4,16},{8,28},{12,24},{16,4},{20,0},{24,12},{28,8},{1,21},{... | collective-permute-start | bytes 638984 | tf_op jit(solution)/shard_map/ppermute | solution.py:327
  148.1 36.6 %copy-start.24 = (bf16[416,256]{1,0:T(8,128)(2,1)}, bf16[416,256]{1,0:T(8,128)(2,1)S(1)}, u32[]{:S(2)}) copy-start(bf16[416,256]{1,0:T(8,128)(2,1)S(1)} %collective-permute-done.3.refs_1_) | copy-start | bytes 638980
  148.1 32.5 %collective-permute-start.8 = (bf16[416,256]{1,0:T(8,128)(2,1)S(1)}, bf16[416,256]{1,0:T(8,128)(2,1)S(1)}, u32[]{:S(2)}, u32[]{:S(2)}) collective-permute-start(bf16[416,256]{1,0:T(8,128)(2,1)S(1)} %get-tuple-element.61), channel_id=1, source_target_pairs={{0,24},{4,28},{8,16},{12,20},{16,8},{20,12},{24,0},{28,4},{1,25},{... | collective-permute-start | bytes 638984 | tf_op jit(solution)/shard_map/ppermute | solution.py:327
  148.2 32.4 %copy-start.25 = (bf16[416,256]{1,0:T(8,128)(2,1)}, bf16[416,256]{1,0:T(8,128)(2,1)S(1)}, u32[]{:S(2)}) copy-start(bf16[416,256]{1,0:T(8,128)(2,1)S(1)} %collective-permute-done.4.refs_2_) | copy-start | bytes 638980
  148.2 36.5 %collective-permute-start.9 = (bf16[416,256]{1,0:T(8,128)(2,1)S(1)}, bf16[416,256]{1,0:T(8,128)(2,1)}, u32[]{:S(2)}, u32[]{:S(2)}) collective-permute-start(bf16[416,256]{1,0:T(8,128)(2,1)S(1)} %get-tuple-element.62), channel_id=1, source_target_pairs={{0,28},{4,24},{8,20},{12,16},{16,12},{20,8},{24,4},{28,0},{1,29},{... | collective-permute-start | bytes 638984 | tf_op jit(solution)/shard_map/ppermute | solution.py:327
  159.0 21.6 %copy-start.26 = (bf16[416,256]{1,0:T(8,128)(2,1)}, bf16[416,256]{1,0:T(8,128)(2,1)S(1)}, u32[]{:S(2)}) copy-start(bf16[416,256]{1,0:T(8,128)(2,1)S(1)} %collective-permute-done.5.refs_3_) | copy-start | bytes 638980
  161.5 19.2 %copy-start.27 = (bf16[416,256]{1,0:T(8,128)(2,1)}, bf16[416,256]{1,0:T(8,128)(2,1)S(1)}, u32[]{:S(2)}) copy-start(bf16[416,256]{1,0:T(8,128)(2,1)S(1)} %collective-permute-done.6.refs_4_) | copy-start | bytes 638980
  172.9 7.8 %copy-start.28 = (bf16[416,256]{1,0:T(8,128)(2,1)}, bf16[416,256]{1,0:T(8,128)(2,1)S(1)}, u32[]{:S(2)}) copy-start(bf16[416,256]{1,0:T(8,128)(2,1)S(1)} %collective-permute-done.7.refs_5_) | copy-start | bytes 638980
  184.7 63.5 %copy-start.3 = (bf16[512,512]{1,0:T(8,128)(2,1)S(1)}, bf16[512,512]{1,0:T(8,128)(2,1)}, u32[]{:S(2)}) copy-start(bf16[512,512]{1,0:T(8,128)(2,1)} %copy-done.2) | copy-start | bytes 1572868
  184.7 63.5 %copy-start.10 = (s32[2]{0:T(128)S(1)}, s32[2]{0:T(128)}, u32[]{:S(2)}) copy-start(s32[2]{0:T(128)} %copy-done.9) | copy-start | bytes 28
  209.2 82.3 %copy-start.8 = (bf16[416,256]{1,0:T(8,128)(2,1)S(1)}, bf16[416,256]{1,0:T(8,128)(2,1)}, u32[]{:S(2)}) copy-start(bf16[416,256]{1,0:T(8,128)(2,1)} %get-tuple-element.76.refs_0_) | copy-start | bytes 638980
  209.2 4.6 %collective-permute-start.30 = (bf16[400,256]{1,0:T(8,128)(2,1)}, bf16[400,256]{1,0:T(8,128)(2,1)S(1)}, u32[]{:S(2)}, u32[]{:S(2)}) collective-permute-start(bf16[400,256]{1,0:T(8,128)(2,1)} %get-tuple-element.89), channel_id=1, source_target_pairs={{0,4},{4,0},{8,12},{12,8},{16,20},{20,16},{24,28},{28,24},{1,5},{5... | collective-permute-start | bytes 614408 | tf_op jit(solution)/shard_map/ppermute | solution.py:327
  209.4 12.5 %collective-permute-start.31 = (bf16[400,256]{1,0:T(8,128)(2,1)}, bf16[400,256]{1,0:T(8,128)(2,1)S(1)}, u32[]{:S(2)}, u32[]{:S(2)}) collective-permute-start(bf16[400,256]{1,0:T(8,128)(2,1)} %get-tuple-element.90), channel_id=1, source_target_pairs={{0,8},{4,12},{8,0},{12,4},{16,24},{20,28},{24,16},{28,20},{1,9},{5... | collective-permute-start | bytes 614408 | tf_op jit(solution)/shard_map/ppermute | solution.py:327
  209.4 16.6 %collective-permute-start.32 = (bf16[400,256]{1,0:T(8,128)(2,1)}, bf16[400,256]{1,0:T(8,128)(2,1)S(1)}, u32[]{:S(2)}, u32[]{:S(2)}) collective-permute-start(bf16[400,256]{1,0:T(8,128)(2,1)} %get-tuple-element.91), channel_id=1, source_target_pairs={{0,12},{4,8},{8,4},{12,0},{16,28},{20,24},{24,20},{28,16},{1,13},{... | collective-permute-start | bytes 614408 | tf_op jit(solution)/shard_map/ppermute | solution.py:327
  211.1 14.9 %collective-permute-start.33 = (bf16[400,256]{1,0:T(8,128)(2,1)}, bf16[400,256]{1,0:T(8,128)(2,1)S(1)}, u32[]{:S(2)}, u32[]{:S(2)}) collective-permute-start(bf16[400,256]{1,0:T(8,128)(2,1)} %get-tuple-element.92), channel_id=1, source_target_pairs={{0,16},{4,20},{8,24},{12,28},{16,0},{20,4},{24,8},{28,12},{1,17},{... | collective-permute-start | bytes 614408 | tf_op jit(solution)/shard_map/ppermute | solution.py:327
  211.1 27.6 %collective-permute-start.34 = (bf16[400,256]{1,0:T(8,128)(2,1)}, bf16[400,256]{1,0:T(8,128)(2,1)S(1)}, u32[]{:S(2)}, u32[]{:S(2)}) collective-permute-start(bf16[400,256]{1,0:T(8,128)(2,1)} %get-tuple-element.93), channel_id=1, source_target_pairs={{0,20},{4,16},{8,28},{12,24},{16,4},{20,0},{24,12},{28,8},{1,21},{... | collective-permute-start | bytes 614408 | tf_op jit(solution)/shard_map/ppermute | solution.py:327
  213.8 31.6 %collective-permute-start.35 = (bf16[400,256]{1,0:T(8,128)(2,1)}, bf16[400,256]{1,0:T(8,128)(2,1)S(1)}, u32[]{:S(2)}, u32[]{:S(2)}) collective-permute-start(bf16[400,256]{1,0:T(8,128)(2,1)} %get-tuple-element.94), channel_id=1, source_target_pairs={{0,24},{4,28},{8,16},{12,20},{16,8},{20,12},{24,0},{28,4},{1,25},{... | collective-permute-start | bytes 614408 | tf_op jit(solution)/shard_map/ppermute | solution.py:327
  221.9 26.3 %collective-permute-start.36 = (bf16[400,256]{1,0:T(8,128)(2,1)}, bf16[400,256]{1,0:T(8,128)(2,1)S(1)}, u32[]{:S(2)}, u32[]{:S(2)}) collective-permute-start(bf16[400,256]{1,0:T(8,128)(2,1)} %get-tuple-element.95), channel_id=1, source_target_pairs={{0,28},{4,24},{8,20},{12,16},{16,12},{20,8},{24,4},{28,0},{1,29},{... | collective-permute-start | bytes 614408 | tf_op jit(solution)/shard_map/ppermute | solution.py:327
  226.0 27.8 %collective-permute-start.20 = (bf16[416,256]{1,0:T(8,128)(2,1)}, bf16[416,256]{1,0:T(8,128)(2,1)S(1)}, u32[]{:S(2)}, u32[]{:S(2)}) collective-permute-start(bf16[416,256]{1,0:T(8,128)(2,1)} %get-tuple-element.77), channel_id=1, source_target_pairs={{0,4},{4,0},{8,12},{12,8},{16,20},{20,16},{24,28},{28,24},{1,5},{5... | collective-permute-start | bytes 638984 | tf_op jit(solution)/shard_map/ppermute | solution.py:327
  226.0 30.4 %collective-permute-start.21 = (bf16[416,256]{1,0:T(8,128)(2,1)}, bf16[416,256]{1,0:T(8,128)(2,1)S(1)}, u32[]{:S(2)}, u32[]{:S(2)}) collective-permute-start(bf16[416,256]{1,0:T(8,128)(2,1)} %get-tuple-element.78), channel_id=1, source_target_pairs={{0,8},{4,12},{8,0},{12,4},{16,24},{20,28},{24,16},{28,20},{1,9},{5... | collective-permute-start | bytes 638984 | tf_op jit(solution)/shard_map/ppermute | solution.py:327
  238.7 18.5 %collective-permute-start.22 = (bf16[416,256]{1,0:T(8,128)(2,1)}, bf16[416,256]{1,0:T(8,128)(2,1)S(1)}, u32[]{:S(2)}, u32[]{:S(2)}) collective-permute-start(bf16[416,256]{1,0:T(8,128)(2,1)} %get-tuple-element.79), channel_id=1, source_target_pairs={{0,12},{4,8},{8,4},{12,0},{16,28},{20,24},{24,20},{28,16},{1,13},{... | collective-permute-start | bytes 638984 | tf_op jit(solution)/shard_map/ppermute | solution.py:327
  249.1 8.1 %copy-start.20 = (bf16[416,256]{1,0:T(8,128)(2,1)S(1)}, bf16[416,256]{1,0:T(8,128)(2,1)}, u32[]{:S(2)}) copy-start(bf16[416,256]{1,0:T(8,128)(2,1)} %get-tuple-element.83) | copy-start | bytes 638980
  249.1 48.9 %copy-start.5 = (bf16[512,512]{1,0:T(8,128)(2,1)S(1)}, bf16[512,512]{1,0:T(8,128)(2,1)}, u32[]{:S(2)}) copy-start(bf16[512,512]{1,0:T(8,128)(2,1)} %copy-done.4) | copy-start | bytes 1572868
  252.0 42.7 %collective-permute-start.37 = (bf16[400,512]{1,0:T(8,128)(2,1)S(1)}, bf16[400,512]{1,0:T(8,128)(2,1)S(1)}, u32[]{:S(2)}, u32[]{:S(2)}) collective-permute-start(bf16[400,512]{1,0:T(8,128)(2,1)S(1)} %get-tuple-element.97), channel_id=1, source_target_pairs={{0,1},{1,0},{2,3},{3,2},{4,5},{5,4},{6,7},{7,6},{8,9},{9,8},{10,11... | collective-permute-start | bytes 1228808 | tf_op jit(solution)/shard_map/ppermute | solution.py:327
  253.7 23.9 %collective-permute-start.23 = (bf16[416,256]{1,0:T(8,128)(2,1)S(1)}, bf16[416,256]{1,0:T(8,128)(2,1)S(1)}, u32[]{:S(2)}, u32[]{:S(2)}) collective-permute-start(bf16[416,256]{1,0:T(8,128)(2,1)S(1)} %copy-done.23), channel_id=1, source_target_pairs={{0,16},{4,20},{8,24},{12,28},{16,0},{20,4},{24,8},{28,12},{1,17},{... | collective-permute-start | bytes 638984 | tf_op jit(solution)/shard_map/ppermute | solution.py:327
  253.8 28.4 %collective-permute-start.24 = (bf16[416,256]{1,0:T(8,128)(2,1)S(1)}, bf16[416,256]{1,0:T(8,128)(2,1)S(1)}, u32[]{:S(2)}, u32[]{:S(2)}) collective-permute-start(bf16[416,256]{1,0:T(8,128)(2,1)S(1)} %copy-done.22), channel_id=1, source_target_pairs={{0,20},{4,16},{8,28},{12,24},{16,4},{20,0},{24,12},{28,8},{1,21},{... | collective-permute-start | bytes 638984 | tf_op jit(solution)/shard_map/ppermute | solution.py:327
  256.4 32.3 %collective-permute-start.25 = (bf16[416,256]{1,0:T(8,128)(2,1)S(1)}, bf16[416,256]{1,0:T(8,128)(2,1)S(1)}, u32[]{:S(2)}, u32[]{:S(2)}) collective-permute-start(bf16[416,256]{1,0:T(8,128)(2,1)S(1)} %copy-done.21), channel_id=1, source_target_pairs={{0,24},{4,28},{8,16},{12,20},{16,8},{20,12},{24,0},{28,4},{1,25},{... | collective-permute-start | bytes 638984 | tf_op jit(solution)/shard_map/ppermute | solution.py:327
  257.3 34.3 %collective-permute-start.26 = (bf16[416,256]{1,0:T(8,128)(2,1)S(1)}, bf16[416,256]{1,0:T(8,128)(2,1)S(1)}, u32[]{:S(2)}, u32[]{:S(2)}) collective-permute-start(bf16[416,256]{1,0:T(8,128)(2,1)S(1)} %copy-done.20), channel_id=1, source_target_pairs={{0,28},{4,24},{8,20},{12,16},{16,12},{20,8},{24,4},{28,0},{1,29},{... | collective-permute-start | bytes 638984 | tf_op jit(solution)/shard_map/ppermute | solution.py:327
  277.6 20.3 %collective-permute-start.38 = (bf16[400,512]{1,0:T(8,128)(2,1)S(1)}, bf16[400,512]{1,0:T(8,128)(2,1)S(1)}, u32[]{:S(2)}, u32[]{:S(2)}) collective-permute-start(bf16[400,512]{1,0:T(8,128)(2,1)S(1)} %get-tuple-element.98), channel_id=1, source_target_pairs={{0,2},{1,3},{2,0},{3,1},{4,6},{5,7},{6,4},{7,5},{8,10},{9,11},{10,... | collective-permute-start | bytes 1228808 | tf_op jit(solution)/shard_map/ppermute | solution.py:327
  282.2 15.8 %collective-permute-start.39 = (bf16[400,512]{1,0:T(8,128)(2,1)S(1)}, bf16[400,512]{1,0:T(8,128)(2,1)S(1)}, u32[]{:S(2)}, u32[]{:S(2)}) collective-permute-start(bf16[400,512]{1,0:T(8,128)(2,1)S(1)} %get-tuple-element.99), channel_id=1, source_target_pairs={{0,3},{1,2},{2,1},{3,0},{4,7},{5,6},{6,5},{7,4},{8,11},{9,10},{10,... | collective-permute-start | bytes 1228808 | tf_op jit(solution)/shard_map/ppermute | solution.py:327
  292.7 12.8 %collective-permute-start.27 = (bf16[416,512]{1,0:T(8,128)(2,1)S(1)}, bf16[416,512]{1,0:T(8,128)(2,1)S(1)}, u32[]{:S(2)}, u32[]{:S(2)}) collective-permute-start(bf16[416,512]{1,0:T(8,128)(2,1)S(1)} %get-tuple-element.85), channel_id=1, source_target_pairs={{0,1},{1,0},{2,3},{3,2},{4,5},{5,4},{6,7},{7,6},{8,9},{9,8},{10,11... | collective-permute-start | bytes 1277960 | tf_op jit(solution)/shard_map/ppermute | solution.py:327
  293.2 21.3 %collective-permute-start.28 = (bf16[416,512]{1,0:T(8,128)(2,1)S(1)}, bf16[416,512]{1,0:T(8,128)(2,1)S(1)}, u32[]{:S(2)}, u32[]{:S(2)}) collective-permute-start(bf16[416,512]{1,0:T(8,128)(2,1)S(1)} %get-tuple-element.86), channel_id=1, source_target_pairs={{0,2},{1,3},{2,0},{3,1},{4,6},{5,7},{6,4},{7,5},{8,10},{9,11},{10,... | collective-permute-start | bytes 1277960 | tf_op jit(solution)/shard_map/ppermute | solution.py:327
  294.7 20.8 %collective-permute-start.29 = (bf16[416,512]{1,0:T(8,128)(2,1)S(1)}, bf16[416,512]{1,0:T(8,128)(2,1)S(1)}, u32[]{:S(2)}, u32[]{:S(2)}) collective-permute-start(bf16[416,512]{1,0:T(8,128)(2,1)S(1)} %get-tuple-element.87), channel_id=1, source_target_pairs={{0,3},{1,2},{2,1},{3,0},{4,7},{5,6},{6,5},{7,4},{8,11},{9,10},{10,... | collective-permute-start | bytes 1277960 | tf_op jit(solution)/shard_map/ppermute | solution.py:327
  (14 other events, 32.4 us)
Sparse Core Ops, SparseCore 0:
  12.2 132.4 all-gather.2

commit v2 on v1

v2 whole, which is shorter than its diff:
```python
import functools
import math

import jax
import jax.numpy as jnp
from jax import lax
from jax.experimental import pallas as pl
from jax.experimental.pallas import tpu as pltpu
from jax.sharding import PartitionSpec as P

DISCOUNT = 0.96
LANES = 128
TILE = 16
VALUE_LOW = -4.0
VALUE_HIGH = 252.0
STEP = (VALUE_HIGH - VALUE_LOW) / 65535.0
HALF = 32768.0
LN2 = math.log(2.0)
SCORE_STEP = DISCOUNT * STEP / LN2
SCORE_SHIFT = DISCOUNT * (HALF * STEP + VALUE_LOW)

BF = jnp.bfloat16
F32 = jnp.float32
VMEM = pl.BlockSpec(memory_space=pltpu.VMEM)
SMEM = pl.BlockSpec(memory_space=pltpu.SMEM)
ANY = pl.BlockSpec(memory_space=pl.ANY)


def dot(a, b):
    return lax.dot_general(a, b, (((1,), (0,)), ((), ())), preferred_element_type=F32)


def dot_nt(a, b):
    return lax.dot_general(a, b, (((1,), (1,)), ((), ())), preferred_element_type=F32)


def lanes_at(start, size):
    return pl.ds(pl.multiple_of(start, LANES), size)


def call(kernel, outs, ins, scratch=(), flops=0, specs=None, out_specs=None, vmem=48):
    moved = sum(math.prod(x.shape) * x.dtype.itemsize for x in list(ins) + list(outs))
    return pl.pallas_call(
        kernel,
        out_shape=tuple(outs),
        in_specs=specs or [SMEM] + [VMEM] * (len(ins) - 1),
        out_specs=tuple(out_specs or [VMEM] * len(outs)),
        scratch_shapes=list(scratch),
        compiler_params=pltpu.CompilerParams(vmem_limit_bytes=vmem * 1024 * 1024),
        cost_estimate=pl.CostEstimate(flops=flops, bytes_accessed=moved, transcendentals=0),
    )(*ins)


class Plan:
    def __init__(self, n_loc, n_inc, counties, rows, columns, incomes, assets):
        self.n_loc, self.n_inc, self.n_z = n_loc, n_inc, n_loc // 2
        self.counties, self.rows, self.columns = counties, rows, columns
        self.incomes, self.assets = incomes, assets
        self.own_incomes = incomes // n_inc
        self.own_assets = assets // n_inc
        self.group_assets = LANES // self.own_incomes
        self.wide = n_inc * LANES
        self.packed = rows + TILE
        self.half = counties // 2
        self.block_rows = counties // LANES
        self.window = (self.block_rows // 2 + 1) * LANES
        self.stride = rows // n_inc // TILE * TILE
        self.quarter = rows - self.stride * (n_inc - 1)
        self.cut = (self.window // LANES + 1) // 2 * LANES

    def fits(self):
        power = lambda n: n > 1 and n & (n - 1) == 0
        return (
            power(self.n_loc)
            and power(self.n_z)
            and power(self.n_inc)
            and self.incomes == LANES
            and self.own_incomes * self.group_assets == LANES
            and self.columns == self.n_z * self.wide
            and self.n_z == self.n_inc == 4
            and self.own_assets == self.n_z * self.group_assets
            and self.rows % TILE == 0
            and self.counties == self.rows * self.n_loc
            and self.counties % LANES == 0
            and self.block_rows % 2 == 1
        )


def order_maps(plan):
    w, oa, oi = plan.wide, plan.own_assets, plan.own_incomes
    r = lax.broadcasted_iota(jnp.int32, (w, w), 0)
    c = lax.broadcasted_iota(jnp.int32, (w, w), 1)
    a = plan.assets
    spot = (r % a) // oa * LANES + r // a * oa + r % oa
    first = (c == spot).astype(BF)
    second = (c == r % oa * oi + r // oa).astype(BF)
    return first, second


def encode_kernel(plan, at, value, first, second, *refs):
    outs, (high, low) = refs[: plan.n_inc], refs[plan.n_inc :]
    inc, w = at[1], plan.wide
    for t in range(plan.n_inc):
        x = value[:, t * w : (t + 1) * w]
        code = jnp.clip(jnp.round((x - VALUE_LOW) * (1.0 / STEP)) - HALF, -HALF, HALF - 1.0)
        top = jnp.floor(code * (1.0 / 256.0))
        rest = code - 256.0 * top
        moved_top = dot(top.astype(BF), first[...]).astype(BF)
        moved_rest = dot(rest.astype(BF), first[...]).astype(BF)
        for q in range(plan.n_inc):
            high[q, :, t * LANES : (t + 1) * LANES] = moved_top[:, q * LANES : (q + 1) * LANES]
            low[q, :, t * LANES : (t + 1) * LANES] = moved_rest[:, q * LANES : (q + 1) * LANES]
    for k in range(plan.n_inc):
        q = inc ^ k
        code = dot(high[q], second[...]) * 256.0 + dot(low[q], second[...])
        outs[k][...] = code.astype(jnp.int32).astype(jnp.int16)


def weight_kernel(plan, at, *refs):
    ni, nz, rows = plan.n_inc, plan.n_z, plan.rows
    codes, (mix_a, mix_b, live), refs = refs[:ni], refs[ni : ni + 3], refs[ni + 3 :]
    weights, held = refs
    inc, w = at[1], plan.wide
    alive = live[...] > 0.0
    for g in range(nz):
        for k in range(ni):
            held[:, lanes_at((inc ^ k) * LANES, LANES)] = codes[k][
                :, g * LANES : (g + 1) * LANES
            ].astype(jnp.int32)
        code = held[...]
        top = (code >> 8).astype(F32).astype(BF)
        rest = (code & 255).astype(F32).astype(BF)
        mixed = (dot(top, mix_a[...]) + dot(top, mix_b[...])) * 256.0 + dot(rest, mix_a[...])
        score = mixed * SCORE_STEP
        peak = jnp.max(jnp.where(alive, score, -512.0), axis=0, keepdims=True)
        peak = jnp.ceil(peak)
        weights[g, 0:rows, :] = jnp.where(alive, jnp.exp2(score - peak), 0.0).astype(BF)
        weights[g, rows:, :] = jnp.broadcast_to(peak, (TILE, w)).astype(BF)


def mass_kernel(plan, at, mass, hit, second, *refs):
    outs, (held,) = refs[: plan.n_inc], refs[plan.n_inc :]
    inc, w = at[1], plan.wide
    for t in range(plan.n_inc):
        x = mass[:, t * w : (t + 1) * w]
        top = x.astype(BF)
        rest = (x - top.astype(F32)).astype(BF)
        moved = (dot(top, hit[t]) + dot(rest, hit[t])).astype(BF)
        for q in range(plan.n_inc):
            held[q, :, t * LANES : (t + 1) * LANES] = moved[:, q * LANES : (q + 1) * LANES]
    for k in range(plan.n_inc):
        outs[k][...] = dot(held[inc ^ k], second[...]).astype(BF)


def spread_kernel(plan, at, *refs):
    *ins, out = refs
    for k in range(plan.n_inc):
        for g in range(plan.n_z):
            out[g, :, lanes_at((at[1] ^ k) * LANES, LANES)] = ins[k][
                :, g * LANES : (g + 1) * LANES
            ]


def collect_kernel(plan, at, *refs):
    blocks, *outs = refs
    for k in range(plan.n_inc):
        for g in range(plan.n_z):
            outs[k][:, g * LANES : (g + 1) * LANES] = blocks[
                g, :, lanes_at((at[1] ^ k) * LANES, LANES)
            ]


def windows(plan, start, count, near, held, out):
    n = plan.counties
    held[:, :n] = near
    held[:, n:] = near[:, : plan.window - LANES]
    for g in range(count // TILE):
        block = (start + g * TILE) // LANES
        out[g * TILE : (g + 1) * TILE, :] = held[
            g * TILE : (g + 1) * TILE, lanes_at(block * LANES, plan.window)
        ]


def quarter_kernel(plan, at, cost, out, part, held, sem):
    start = pl.multiple_of(at[1] * plan.stride, TILE)
    copy = pltpu.make_async_copy(cost.at[pl.ds(start, plan.quarter)], part, sem)
    copy.start()
    copy.wait()
    near = jnp.exp(-part[...]).astype(BF)
    windows(plan, at[0] * plan.rows + start, plan.quarter, near, held, out)


def window_kernel(plan, at, cost, out, held):
    near = jnp.exp(-cost[...]).astype(BF)
    windows(plan, at[0] * plan.rows, plan.rows, near, held, out)


def county_rows(plan, at, z, side):
    start = (2 * z + ((at[0] % 2) ^ side)) * plan.rows
    return pl.ds(pl.multiple_of(start, TILE), plan.rows)


def near_copies(plan, near, held, sems):
    blocks = [pl.ds(j * plan.rows, plan.rows) for j in range(plan.n_z)]
    return [
        pltpu.make_async_copy(near.at[b], held.at[b], sems.at[j]) for j, b in enumerate(blocks)
    ]


def total_kernel(plan, at, *refs):
    nz, rows, cut = plan.n_z, plan.rows, plan.cut
    own_weights, other_weights, refs = refs[0], refs[1], refs[2:]
    both, (sent, scaled, near, weight, strip, full, sums, sem) = refs[:10], refs[10:]
    z, core, inc = at[0] // 2, at[0] % 2, at[1]
    left, right = pl.ds(0, cut), pl.ds(cut, plan.window - cut)
    always, last = [], []
    for side in range(2):
        own, *parts = both[side * 5 : side * 5 + 5]
        first_row = lambda j: (2 * (z ^ j) + (core ^ side)) * rows
        always.append((own, strip.at[pl.ds(pl.multiple_of(first_row(0), TILE), rows)]))
        places = ((0, 1), left), ((2, 3), left), ((0, 2), right), ((1, 3), right)
        for part, (steps, lanes) in zip(parts, places):
            for h, k in enumerate(steps):
                q = inc ^ k
                for j in range(1, nz):
                    base = (h * (nz - 1) + j - 1) * plan.quarter
                    start = first_row(j) + q * plan.stride
                    rest = plan.quarter - plan.stride
                    to = lambda r, size: strip.at[pl.ds(pl.multiple_of(r, TILE), size), lanes]
                    always.append((part.at[pl.ds(base, plan.stride)], to(start, plan.stride)))
                    extra = part.at[pl.ds(base + plan.stride, rest)]
                    last.append((q == plan.n_inc - 1, extra, to(start + plan.stride, rest)))
    copies = [pltpu.make_async_copy(a, b, sem) for a, b in always]
    more = [(c, pltpu.make_async_copy(a, b, sem)) for c, a, b in last]
    for c in copies:
        c.start()
    for when, c in more:
        pl.when(when)(c.start)

    places = [(x, g) for x in (own_weights, other_weights) for g in range(nz)]
    peaks = [x[g, rows : rows + 1, :].astype(F32) for x, g in places]
    peak = functools.reduce(jnp.maximum, peaks)
    for i, (x, g) in enumerate(places):
        part = (x[g, :rows, :].astype(F32) * jnp.exp2(peaks[i] - peak)).astype(BF)
        weight[county_rows(plan, at, g, i // nz), :] = part
        if i < nz:
            scaled[g] = part

    for c in copies:
        c.wait()
    for when, c in more:
        pl.when(when)(c.wait)
    blocks = plan.block_rows
    for i in range(blocks):
        for k in range(plan.window // LANES):
            j = (i + k) % blocks
            tile = strip[i * LANES : (i + 1) * LANES, k * LANES : (k + 1) * LANES]
            full[i * LANES : (i + 1) * LANES, j * LANES : (j + 1) * LANES] = tile
            if k:
                full[j * LANES : (j + 1) * LANES, i * LANES : (i + 1) * LANES] = tile.T
    copies = []
    for j in range(nz):
        out = near.at[pl.ds(j * rows, rows)]
        copies.append(pltpu.make_async_copy(full.at[county_rows(plan, at, j, 0)], out, sem))
    for c in copies:
        c.start()
    def product(j, carry):
        sums[j] = dot(full[county_rows(plan, at, j, 0), :], weight[...])
        return carry

    lax.fori_loop(0, nz, product, 0)
    sent[:, :rows, :] = sums[...].astype(BF)
    sent[:, rows:, :] = jnp.broadcast_to(peak[None], (nz, TILE, plan.wide)).astype(BF)
    for c in copies:
        c.wait()


def share_kernel(plan, masses, totals, out):
    for g in range(plan.n_z):
        total = totals[g, : plan.rows, :].astype(F32)
        out[g] = (masses[g].astype(F32) / total).astype(BF)


def mover_kernel(plan, at, own, other, near, scaled, *refs):
    nz, rows = plan.n_z, plan.rows
    outs, (movers, share, held, sems) = refs[:nz], refs[nz:]
    copies = near_copies(plan, near, held, sems)
    for c in copies:
        c.start()
    for side, x in enumerate((own, other)):
        for g in range(nz):
            share[county_rows(plan, at, g, side), :] = x[g]
    for g in range(nz):
        copies[g].wait()
        arrived = dot(held[g * rows : (g + 1) * rows, :], share[...])
        movers[g] = (scaled[g].astype(F32) * arrived).astype(BF)
    for j in range(nz):
        outs[j][...] = movers[(at[0] // 2) ^ j]


def tail_kernel(plan, at, *refs):
    ni, rows, w = plan.n_inc, plan.rows, plan.wide
    mix_a, mix_b, *refs = refs
    ins, outs, mixed = refs[: -1 - ni], refs[-1 - ni : -1], refs[-1]
    for i, part in enumerate(ins):
        x = part[...]
        new = dot_nt(x, mix_a[...]) + dot_nt(x, mix_b[...])
        most = jnp.maximum(jnp.max(new, axis=0, keepdims=True), 1e-30)
        power = jnp.ceil(jnp.log2(most))
        code = jnp.minimum(jnp.round(new * jnp.exp2(15.0 - power)), HALF - 1.0)
        mixed[:rows, :] = code.astype(jnp.int32)
        mixed[rows:, :] = jnp.broadcast_to(power, (TILE, w)).astype(jnp.int32)
        for k in range(ni):
            outs[k][:, i * LANES : (i + 1) * LANES] = mixed[
                :, lanes_at((at[1] ^ k) * LANES, LANES)
            ].astype(jnp.int16)


def next_mass_kernel(plan, at, *refs):
    ni, w, rows = plan.n_inc, plan.wide, plan.rows
    close, far, refs = refs[:ni], refs[ni : 2 * ni], refs[2 * ni :]
    first, second, out, held, high, low = refs
    z, inc = at[0] // 2, at[1]
    for k in range(ni):
        j = 0
        for part in (close[k], far[k]):
            for i in range(part.shape[1] // LANES):
                held[:, lanes_at((z ^ j) * LANES, LANES)] = part[
                    :, i * LANES : (i + 1) * LANES
                ].astype(jnp.int32)
                j += 1
        code = held[...]
        for part, into in ((code >> 8, high), (code & 255, low)):
            back = dot_nt(part.astype(F32).astype(BF), second[...]).astype(BF)
            for t in range(ni):
                into[t, :, lanes_at((inc ^ k) * LANES, LANES)] = back[:, t * LANES : (t + 1) * LANES]
    for t in range(ni):
        code = dot_nt(high[t], first[...]) * 256.0 + dot_nt(low[t], first[...])
        out[:, t * w : (t + 1) * w] = code[:rows, :] * jnp.exp2(code[rows : rows + 1, :] - 15.0)


def value_kernel(plan, at, *refs):
    ni, w, rows = plan.n_inc, plan.wide, plan.rows
    ins, (hit, second, flow), (out, held) = refs[:ni], refs[ni : ni + 3], refs[ni + 3 :]
    inc = at[1]
    for k in range(ni):
        back = dot_nt(ins[k][...], second[...]).astype(BF)
        for t in range(ni):
            held[t, :, lanes_at((inc ^ k) * LANES, LANES)] = back[:, t * LANES : (t + 1) * LANES]
    for t in range(ni):
        got = dot_nt(held[t], hit[t])
        peak = got[rows : rows + 1, :] * LN2 + SCORE_SHIFT
        out[:, t * w : (t + 1) * w] = flow[:, t * w : (t + 1) * w] + (peak + jnp.log(got[:rows, :]))


def mix_kernel(plan, trans, out_a, out_b):
    e, oi, ga, w = plan.incomes, plan.own_incomes, plan.group_assets, plan.wide
    grid = lambda shape, axis: lax.broadcasted_iota(jnp.int32, shape, axis)
    raised = trans[...] + jnp.where(grid((e, e), 0) == grid((e, e), 1), 16.0, 0.0)
    prob = (raised / jnp.sum(raised, axis=1, keepdims=True)).T
    lane = grid((e, w), 1)
    place = (grid((e, w), 0) == lane // LANES * oi + lane % oi).astype(BF)
    same = grid((w, w), 0) // oi % ga == grid((w, w), 1) // oi % ga
    top = prob.astype(BF)
    for part, out in ((top, out_a), ((prob - top.astype(F32)).astype(BF), out_b)):
        wide = dot(part, place)
        blocks = [wide[i * oi : (i + 1) * oi] for i in range(plan.n_inc) for _ in range(ga)]
        out[...] = jnp.where(same, jnp.concatenate(blocks, axis=0), 0.0).astype(BF)


def policy_maps(plan, asset_policy, inc):
    ni, oa, a, w = plan.n_inc, plan.own_assets, plan.assets, plan.wide
    own = lax.dynamic_slice_in_dim(asset_policy, inc * plan.own_incomes, plan.own_incomes, 0)
    group = w // a
    row_income = jnp.arange(group, dtype=jnp.int32)[None, :, None]
    own = own.reshape(ni, group, a)
    lane = own // oa * LANES + row_income * oa + own % oa
    lane = lane.reshape(ni, w, 1)
    return (lane == lax.broadcasted_iota(jnp.int32, (ni, w, w), 2)).astype(BF)


def swap(x, axis, n, k):
    return lax.ppermute(x, axis, [(s, s ^ k) for s in range(n)]) if k else x


def exchange(blocks, axis, n, unit=1):
    got = {k: swap(blocks[k], axis, n, k * unit) for k in reversed(range(len(blocks)))}
    return [got[k] for k in range(len(blocks))]


def after(x, y):
    return lax.optimization_barrier((x, y))


def state_split(plan, cont_value, flow_util, move_cost, live_mask, trans_weight, asset_policy, mass):
    ni, nl, nz, rows, n = plan.n_inc, plan.n_loc, plan.n_z, plan.rows, plan.counties
    w, packed, half = plan.wide, plan.packed, plan.half
    S = jax.ShapeDtypeStruct
    loc, inc = lax.axis_index("loc"), lax.axis_index("inc")
    at = jnp.stack([loc, inc]).astype(jnp.int32)
    bind = lambda f: functools.partial(f, plan)
    pass_flops = 2 * rows * plan.columns * w
    solve_flops = 2 * half * n * w
    swap_core = lambda x: swap(x, "loc", nl, 1)
    lines = [list(range(core, nl, 2)) for core in range(2)]
    along_z = lambda x: lax.all_to_all(x, "loc", 0, 0, axis_index_groups=lines)
    ring = n + plan.window - LANES

    (quarter,) = call(
        bind(quarter_kernel),
        [S((plan.quarter, plan.window), BF)],
        [at, move_cost],
        [
            pltpu.VMEM((plan.quarter, n), F32),
            pltpu.VMEM((plan.quarter, ring), BF),
            pltpu.SemaphoreType.DMA,
        ],
        specs=[SMEM, ANY],
    )
    pieces = [swap(quarter, "loc", nl, 2 * j) for j in range(2, nz)]

    first, second = order_maps(plan)
    codes = call(
        bind(encode_kernel),
        [S((rows, w), jnp.int16)] * ni,
        [at, cont_value, first, second],
        [pltpu.VMEM((ni, rows, w), BF)] * 2,
        4 * pass_flops,
    )
    codes = exchange(codes, "inc", ni)
    quarter, _ = after(quarter, codes[1])
    pieces.insert(0, swap(quarter, "loc", nl, 2))

    hit = policy_maps(plan, asset_policy, inc)
    masses = call(
        bind(mass_kernel),
        [S((rows, w), BF)] * ni,
        [at, mass, hit, second],
        [pltpu.VMEM((ni, rows, w), BF)],
        3 * pass_flops,
    )
    mix_a, mix_b = call(
        bind(mix_kernel), [S((w, w), BF)] * 2, [trans_weight], specs=[VMEM]
    )
    (own_near,) = call(
        bind(window_kernel),
        [S((rows, plan.window), BF)],
        [at, move_cost],
        [pltpu.VMEM((rows, ring), BF)],
    )
    masses, codes = after(masses, codes)
    masses = exchange(masses, "inc", ni)
    codes, _ = after(codes, pieces)

    live = (live_mask > 0).astype(F32)[:, None]
    weights = call(
        bind(weight_kernel),
        [S((nz, packed, w), BF)],
        [at, *codes, mix_a, mix_b, live],
        [pltpu.VMEM((rows, w), jnp.int32)],
        3 * pass_flops,
    )
    weights = along_z(weights[0])
    others = swap_core(weights)

    strip, _ = after(jnp.concatenate(pieces), masses)
    left, right = strip[:, : plan.cut], strip[:, plan.cut :]
    left = jnp.concatenate([left, swap(left, "inc", ni, 1)])
    right = jnp.concatenate([right, swap(right, "inc", ni, 2)])
    near = [own_near, left, swap(left, "inc", ni, 2), right, swap(right, "inc", ni, 1)]
    near = near + [swap_core(x) for x in near]

    masses = call(bind(spread_kernel), [S((nz, rows, w), BF)], [at, *masses])
    masses, weights = after(masses[0], weights)
    masses = along_z(masses)

    totals, scaled, near = call(
        bind(total_kernel),
        [S((nz, packed, w), BF), S((nz, rows, w), BF), S((half, n), BF)],
        [at, weights, others, *near],
        [
            pltpu.VMEM((n, w), BF),
            pltpu.VMEM((n, plan.window), BF),
            pltpu.VMEM((n, n), BF),
            pltpu.VMEM((nz, rows, w), F32),
            pltpu.SemaphoreType.DMA,
        ],
        solve_flops,
        specs=[SMEM, VMEM, VMEM] + [ANY] * len(near),
        out_specs=[VMEM, VMEM, ANY],
        vmem=60,
    )
    sent = along_z(totals)
    (share,) = call(
        bind(share_kernel), [S((nz, rows, w), BF)], [masses, totals], specs=[VMEM] * 2
    )
    movers = call(
        bind(mover_kernel),
        [S((rows, w), BF)] * nz,
        [at, share, swap_core(share), near, scaled],
        [
            pltpu.VMEM((nz, rows, w), BF),
            pltpu.VMEM((n, w), BF),
            pltpu.VMEM((half, n), BF),
            pltpu.SemaphoreType.DMA((nz,)),
        ],
        solve_flops,
        specs=[SMEM, VMEM, VMEM, ANY, VMEM],
    )
    far, _ = after(movers[2:], sent)
    close = [movers[0], swap(movers[1], "loc", nl, 2)]
    far = [swap(x, "loc", nl, 2 * (j + 2)) for j, x in enumerate(far)]

    moved = []
    for part in (close, far):
        blocks = call(
            bind(tail_kernel),
            [S((packed, len(part) * LANES), jnp.int16)] * ni,
            [at, mix_a, mix_b, *part],
            [pltpu.VMEM((packed, w), jnp.int32)],
            pass_flops,
        )
        moved += exchange(blocks, "inc", ni)
    sent = call(bind(collect_kernel), [S((packed, w), BF)] * ni, [at, sent])
    sent = exchange(sent, "inc", ni)

    (new_mass,) = call(
        bind(next_mass_kernel),
        [S((rows, plan.columns), F32)],
        [at, *moved, first, second],
        [pltpu.VMEM((packed, w), jnp.int32)] + [pltpu.VMEM((ni, packed, w), BF)] * 2,
        4 * pass_flops,
    )
    (new_value,) = call(
        bind(value_kernel),
        [S((rows, plan.columns), F32)],
        [at, *sent, hit, second, flow_util],
        [pltpu.VMEM((ni, packed, w), BF)],
        2 * pass_flops,
    )
    return new_value, new_mass


def gathered(cont_value, flow_util, move_cost, live_mask, trans_weight, asset_policy, mass):
    high = lax.Precision.HIGHEST
    e, a = asset_policy.shape
    raised = trans_weight + 16.0 * jnp.eye(e, dtype=F32)
    trans_prob = raised / jnp.sum(raised, axis=1, keepdims=True)
    onehot = (asset_policy[:, :, None] == jnp.arange(a, dtype=jnp.int32)[None, None, :]).astype(F32)
    moved_rows = lax.all_to_all(cont_value, "inc", split_axis=0, concat_axis=1, tiled=True)
    expect = jnp.einsum("ef,jfb->jeb", trans_prob, moved_rows.reshape(-1, e, a), precision=high)
    chosen_all = jnp.einsum("jeb,eab->jea", expect, onehot, precision=high).reshape(-1, e * a)
    chosen = lax.all_to_all(chosen_all, "inc", split_axis=1, concat_axis=0, tiled=True)
    scores = DISCOUNT * chosen
    live_rows = live_mask[:, None] > 0
    local_max = jnp.max(jnp.where(live_rows, scores, F32(-1e30)), axis=0)
    column_max = lax.pmax(local_max, "loc")
    dest_weight = jnp.where(live_rows, jnp.exp(scores - column_max[None, :]), F32(0.0)).astype(BF)
    kernel = jnp.exp(-move_cost).astype(BF)
    totals = dot(kernel, lax.all_gather(dest_weight, "loc", axis=0, tiled=True))
    new_value = flow_util + column_max[None, :] + jnp.log(totals)
    shares = (mass / totals).astype(BF)
    arrived = lax.psum_scatter(
        lax.dot_general(
            kernel, shares, (((0,), (0,)), ((), ())), preferred_element_type=F32
        ).astype(BF),
        "loc",
        scatter_dimension=0,
        tiled=True,
    ).astype(F32)
    movers = dest_weight.astype(F32) * arrived
    moved_mass = lax.all_to_all(movers, "inc", split_axis=0, concat_axis=1, tiled=True)
    shuffled = jnp.einsum("jea,eab->jeb", moved_mass.reshape(-1, e, a), onehot, precision=high)
    mixed_mass = jnp.einsum("ef,jeb->jfb", trans_prob, shuffled, precision=high).reshape(-1, e * a)
    new_mass = lax.all_to_all(mixed_mass, "inc", split_axis=1, concat_axis=0, tiled=True)
    return new_value, new_mass


def solution(mesh):
    n_loc, n_inc = mesh.shape["loc"], mesh.shape["inc"]

    def shards(*args):
        rows, columns = args[0].shape
        plan = Plan(n_loc, n_inc, args[2].shape[1], rows, columns, *args[5].shape)
        if plan.fits():
            return state_split(plan, *args)
        return gathered(*args)

    split = P("loc", "inc")
    return jax.shard_map(
        shards,
        mesh=mesh,
        in_specs=(split, split, P("loc", None), P("loc"), P(), P(), split),
        out_specs=(split, split),
        check_vma=False,
    )
```

time: 333 us -> 247 us (0.74)
  waiting for transfers between devices: 168 us -> 103 us
  between operations: 14.5 us -> 0.97 us
  Pallas kernels: 62.2 us -> 71.4 us
  starting transfers between devices: 57.4 us -> 50.4 us
  local copies, waits for them, and re-layouts: 20.8 us -> 14.5 us
    ppermute x40 -> x32, waiting for transfers between devices: 168 us -> 86.4 us  [swap(): return lax.ppermute(x, axis, [(s, s ^ k) for s in range(n)]) if k else x]
    ppermute x40 -> x32, starting transfers between devices: 57.4 us -> 31.9 us  [swap(): return lax.ppermute(x, axis, [(s, s ^ k) for s in range(n)]) if k else x]
    all_to_all x0 -> x3, starting transfers between devices: none -> 18.6 us  [state_split(): along_z = lambda x: lax.all_to_all(x, 'loc', 0, 0, axis_index_groups=lines)]
    all_to_all x0 -> x3, waiting for transfers between devices: none -> 16.4 us  [state_split(): along_z = lambda x: lax.all_to_all(x, 'loc', 0, 0, axis_index_groups=lines)]
    pallas_call x10 -> x15, Pallas kernels: 62.2 us -> 71.4 us  [call(): pl.pallas_call(kernel, out_shape=tuple(outs), in_specs=specs or [SMEM] +...]
    reshape x1 -> x0, local copies, waits for them, and re-layouts: 6.12 us -> none  [mix_maps(): jnp.broadcast_to(turned, (ni, ga, oi, ni, ga, oi))]
    broadcast_in_dim x3 -> x0, local copies, waits for them, and re-layouts: 4.74 us -> none  [mix_maps(): jnp.broadcast_to(turned, (ni, ga, oi, ni, ga, oi))]
    unnamed x74 -> x52, local copies, waits for them, and re-layouts: 9.44 us -> 13.2 us
  transfers between devices with their start and end apart: 41 -> 35, of which waited for: 24 -> 15; matrix products, arithmetic and copies ran while one was open for 5% -> 3% of each run, Pallas kernels for 8% -> 24%
where the time goes in v2:
time: 247 us; the launch traced here: 246 us
  waiting for transfers between devices  103 us (42%)
  Pallas kernels  71.4 us (29%)
  starting transfers between devices  50.4 us (20%)
  local copies, waits for them, and re-layouts  14.5 us (6%)
  other arithmetic  6.06 us (2%)
    ppermute x32, waiting for transfers between devices, swap(): return lax.ppermute(x, axis, [(s, s ^ k) for s in range(n)]) if k else x  86.4 us
    pallas_call x15, Pallas kernels, call(): pl.pallas_call(kernel, out_shape=tuple(outs), in_specs=specs or [SMEM] +...  71.4 us
    ppermute x32, starting transfers between devices, swap(): return lax.ppermute(x, axis, [(s, s ^ k) for s in range(n)]) if k else x  31.9 us
    all_to_all x3, starting transfers between devices, state_split(): along_z = lambda x: lax.all_to_all(x, 'loc', 0, 0, axis_index_groups=lines)  18.6 us
    all_to_all x3, waiting for transfers between devices, state_split(): along_z = lambda x: lax.all_to_all(x, 'loc', 0, 0, axis_index_groups=lines)  16.4 us
    unnamed x52, local copies, waits for them, and re-layouts  13.2 us
  transfers between devices with their start and end apart: 35, of which 15 were waited for; matrix products, arithmetic and copies ran while one was open for 3% of the time, Pallas kernels for 24%

profile of v2, /device:TPU:8, one launch (start us, length us, event | category | flops | bytes accessed | tf_op | source)
XLA Modules:
  0.0 246.2 jit_solution(10249780183429596468)
XLA Ops:
  0.7 2.4 copy-done.2
  3.2 1.1 shard_map.89
  4.2 1.6 collective-permute-start.8
  5.9 1.1 collective-permute-start.7
  7.0 1.2 fusion.12
  8.3 5.0 %shard_map.87 = (s16[400,512]{1,0:T(8,128)(2,1)S(1)}, s16[400,512]{1,0:T(8,128)(2,1)}, s16[400,512]{1,0:T(8,128)(2,1)}, s16[400,512]{1,0:T(8,128)(2,1)}) custom-call(s32[2]{0:T(128)S(1)} %pad_add_fusion.at, f32[400,2048]{1,0:T(8,128)S(1)} %copy-done.12, bf16[512,512]{1,0:T(8,128)(2,1)S(1)} %get-tuple-element.96.first.refs_8_, ...), custom_call_target="tpu_custom_call" | custom-call | flops 3355443200 | bytes 5963784 | tf_op jit(solution)/shard_map/pallas_call | solution.py:43
  13.3 0.8 copy-done.24
  14.1 1.6 collective-permute-start
  15.7 1.5 collective-permute-start.1
  18.5 8.3 %collective-permute-done.refs_1_ = s16[400,512]{1,0:T(8,128)(2,1)} collective-permute-done((s16[400,512]{1,0:T(8,128)(2,1)}, s16[400,512]{1,0:T(8,128)(2,1)}, u32[]{:S(2)}, u32[]{:S(2)}) %collective-permute-start) | collective-permute-done | bytes 409632 | tf_op jit(solution)/shard_map/ppermute | solution.py:383
  26.8 1.4 collective-permute-start.6
  28.9 0.8 copy.10.refs_6_
  29.7 0.8 copy-done.9
  31.0 5.2 %shard_map.86 = (bf16[400,512]{1,0:T(8,128)(2,1)S(1)}, bf16[400,512]{1,0:T(8,128)(2,1)S(1)}, bf16[400,512]{1,0:T(8,128)(2,1)S(1)}, bf16[400,512]{1,0:T(8,128)(2,1)S(1)}) custom-call(s32[2]{0:T(128)S(1)} %pad_add_fusion.at, f32[400,2048]{1,0:T(8,128)} %mass.1, bf16[4,512,512]{2,1,0:T(8,128)(2,1)S(1)} %fusion.hit.refs_4_, ...), custom_call_target="tpu_custom_call" | custom-call | flops 2516582400 | bytes 7536648 | tf_op jit(solution)/shard_map/pallas_call | solution.py:43
  36.2 0.8 copy-done.6
  39.3 2.2 collective-permute-done.6
  41.4 5.3 %shard_map.91 = bf16[4,416,512]{2,1,0:T(8,128)(2,1)S(1)} custom-call(s32[2]{0:T(128)S(1)} %pad_add_fusion.at, s16[400,512]{1,0:T(8,128)(2,1)S(1)} %copy-done.25, s16[400,512]{1,0:T(8,128)(2,1)} %collective-permute-done.refs_1_, s16[400,512]{1,0:T(8,128)(2,1)} %collective-permute-done.1.refs_2_, s16[400,512]{1,0:T(8,128)(2,1)} %collective-permute-done.2.refs_3_, ...), custom_call_target="tpu_custom_call" | custom-call | flops 2516582400 | bytes 4392520 | tf_op jit(solution)/shard_map/pallas_call | solution.py:43
  46.7 1.2 copy-done.5
  47.9 6.9 %all-to-all-start = ((bf16[4,416,512]{2,1,0:T(8,128)(2,1)}), bf16[4,416,512]{2,1,0:T(8,128)(2,1)}, u32[]{:S(2)}, u32[]{:S(2)}) async-start(bf16[4,416,512]{2,1,0:T(8,128)(2,1)} %copy-done.5), calls=%async_computation | async-start | bytes 3407872 | tf_op jit(solution)/shard_map/all_to_all | solution.py:406
  54.8 1.5 collective-permute-start.3
  56.3 1.5 collective-permute-start.4
  58.3 1.3 pad_maximum_fusion.1
  59.6 7.4 %collective-permute-done.3.refs_1_ = bf16[400,512]{1,0:T(8,128)(2,1)S(1)} collective-permute-done((bf16[400,512]{1,0:T(8,128)(2,1)}, bf16[400,512]{1,0:T(8,128)(2,1)S(1)}, u32[]{:S(2)}, u32[]{:S(2)}) %collective-permute-start.3) | collective-permute-done | bytes 409632 | tf_op jit(solution)/shard_map/ppermute | solution.py:383
  67.1 5.8 %collective-permute-done.4.refs_2_ = bf16[400,512]{1,0:T(8,128)(2,1)S(1)} collective-permute-done((bf16[400,512]{1,0:T(8,128)(2,1)}, bf16[400,512]{1,0:T(8,128)(2,1)S(1)}, u32[]{:S(2)}, u32[]{:S(2)}) %collective-permute-start.4) | collective-permute-done | bytes 409632 | tf_op jit(solution)/shard_map/ppermute | solution.py:383
  72.9 1.8 collective-permute-done.5.refs_3_
  74.7 1.5 collective-permute-start.10
  76.4 8.4 %collective-permute-done.10 = bf16[336,896]{1,0:T(8,128)(2,1)S(1)} collective-permute-done((bf16[336,896]{1,0:T(8,128)(2,1)S(1)}, bf16[336,896]{1,0:T(8,128)(2,1)S(1)}, u32[]{:S(2)}, u32[]{:S(2)}) %collective-permute-start.10) | collective-permute-done | bytes 602144 | tf_op jit(solution)/shard_map/ppermute | solution.py:383
  84.8 1.1 pad_maximum_fusion.refs_3_
  86.0 1.0 collective-permute-start.11
  87.0 4.6 %shard_map.92.refs_2_ = bf16[400,1664]{1,0:T(8,128)(2,1)} custom-call(s32[2]{0:T(128)S(1)} %pad_add_fusion.at, f32[400,3200]{1,0:T(8,128)} %cost.3), custom_call_target="tpu_custom_call" | custom-call | bytes 6451208 | tf_op jit(solution)/shard_map/pallas_call | solution.py:43
  91.6 1.1 pad_maximum_fusion.2.refs_5_
  92.7 1.5 collective-permute-start.13
  94.2 0.8 shard_map.88
  95.1 1.2 copy-done.4
  96.2 5.1 %all-to-all-start.2 = ((bf16[4,400,512]{2,1,0:T(8,128)(2,1)}), bf16[4,400,512]{2,1,0:T(8,128)(2,1)}, u32[]{:S(2)}, u32[]{:S(2)}) async-start(bf16[4,400,512]{2,1,0:T(8,128)(2,1)} %copy-done.4), calls=%async_computation.2 | async-start | bytes 3276800 | tf_op jit(solution)/shard_map/all_to_all | solution.py:406
  101.8 9.5 %collective-permute-done.11.refs_4_ = bf16[672,896]{1,0:T(8,128)(2,1)} collective-permute-done((bf16[672,896]{1,0:T(8,128)(2,1)}, bf16[672,896]{1,0:T(8,128)(2,1)}, u32[]{:S(2)}, u32[]{:S(2)}) %collective-permute-start.11) | collective-permute-done | bytes 1204256 | tf_op jit(solution)/shard_map/ppermute | solution.py:383
  111.9 6.4 %collective-permute-done.13.refs_6_ = bf16[672,768]{1,0:T(8,128)(2,1)} collective-permute-done((bf16[672,768]{1,0:T(8,128)(2,1)}, bf16[672,768]{1,0:T(8,128)(2,1)}, u32[]{:S(2)}, u32[]{:S(2)}) %collective-permute-start.13) | collective-permute-done | bytes 1032224 | tf_op jit(solution)/shard_map/ppermute | solution.py:383
  118.3 3.0 %collective-permute-done.18.refs_11_ = bf16[672,768]{1,0:T(8,128)(2,1)} collective-permute-done((bf16[672,768]{1,0:T(8,128)(2,1)}, bf16[672,768]{1,0:T(8,128)(2,1)}, u32[]{:S(2)}, u32[]{:S(2)}) %collective-permute-start.18) | collective-permute-done | bytes 1032224 | tf_op jit(solution)/shard_map/ppermute | solution.py:383
  121.2 16.8 %shard_map.93 = (bf16[4,416,512]{2,1,0:T(8,128)(2,1)}, bf16[4,400,512]{2,1,0:T(8,128)(2,1)}, bf16[1600,3200]{1,0:T(8,128)(2,1)}) custom-call(s32[2]{0:T(128)} %copy-done.10, bf16[4,416,512]{2,1,0:T(8,128)(2,1)} %all-to-all-done.refs_0_, bf16[4,416,512]{2,1,0:T(8,128)(2,1)} %collective-permute-done.9.refs_1_, bf16[400,1664]{1,0:T(8,128)(2,1)} %shard_map.92.refs_2_, ...), custom_call_target="tpu_custom_call" | custom-call | flops 5242880000 | bytes 28598280 | tf_op jit(solution)/shard_map/pallas_call | solution.py:43
  138.1 6.5 %all-to-all-start.1 = ((bf16[4,416,512]{2,1,0:T(8,128)(2,1)}), bf16[4,416,512]{2,1,0:T(8,128)(2,1)}, u32[]{:S(2)}, u32[]{:S(2)}) async-start(bf16[4,416,512]{2,1,0:T(8,128)(2,1)} %get-tuple-element.74.totals), calls=%async_computation.1 | async-start | bytes 3407872 | tf_op jit(solution)/shard_map/all_to_all | solution.py:406
  144.6 1.5 copy-done.3
  146.1 1.9 shard_map.96.own
  148.1 3.5 %collective-permute-done.22.other = bf16[4,400,512]{2,1,0:T(8,128)(2,1)S(1)} collective-permute-done((bf16[4,400,512]{2,1,0:T(8,128)(2,1)S(1)}, bf16[4,400,512]{2,1,0:T(8,128)(2,1)S(1)}, u32[]{:S(2)}, u32[]{:S(2)}) %collective-permute-start.22) | collective-permute-done | bytes 1638432 | tf_op jit(solution)/shard_map/ppermute | solution.py:383
  151.6 10.2 %shard_map.97 = (bf16[400,512]{1,0:T(8,128)(2,1)S(1)}, bf16[400,512]{1,0:T(8,128)(2,1)}, bf16[400,512]{1,0:T(8,128)(2,1)S(1)}, bf16[400,512]{1,0:T(8,128)(2,1)S(1)}) custom-call(s32[2]{0:T(128)S(1)} %copy-done.11, bf16[4,400,512]{2,1,0:T(8,128)(2,1)S(1)} %shard_map.96.own, bf16[4,400,512]{2,1,0:T(8,128)(2,1)S(1)} %collective-permute-done.22.other, ...), custom_call_target="tpu_custom_call" | custom-call | flops 5242880000 | bytes 16793608 | tf_op jit(solution)/shard_map/pallas_call | solution.py:43
  164.3 16.4 %all-to-all-done.1.refs_0_ = bf16[4,416,512]{2,1,0:T(8,128)(2,1)} async-done(((bf16[4,416,512]{2,1,0:T(8,128)(2,1)}), bf16[4,416,512]{2,1,0:T(8,128)(2,1)}, u32[]{:S(2)}, u32[]{:S(2)}) %all-to-all-start.1) | async-done | bytes 1703968 | tf_op jit(solution)/shard_map/all_to_all | solution.py:406
  180.8 3.4 %collective-permute-start.27 = (bf16[400,512]{1,0:T(8,128)(2,1)}, bf16[400,512]{1,0:T(8,128)(2,1)S(1)}, u32[]{:S(2)}, u32[]{:S(2)}) collective-permute-start(bf16[400,512]{1,0:T(8,128)(2,1)} %copy-done.20), channel_id=1, source_target_pairs={{0,16},{4,20},{8,24},{12,28},{16,0},{20,4},{24,8},{28,12},{1,17},{... | collective-permute-start | bytes 1228808 | tf_op jit(solution)/shard_map/ppermute | solution.py:383
  184.2 1.5 collective-permute-start.28
  185.7 1.8 shard_map.94
  187.4 0.9 collective-permute-start.19
  189.1 1.9 collective-permute-start.21
  191.0 2.7 %shard_map.98 = (s16[416,256]{1,0:T(8,128)(2,1)S(1)}, s16[416,256]{1,0:T(8,128)(2,1)S(1)}, s16[416,256]{1,0:T(8,128)(2,1)S(1)}, s16[416,256]{1,0:T(8,128)(2,1)S(1)}) custom-call(s32[2]{0:T(128)S(1)} %copy-done.11, bf16[512,512]{1,0:T(8,128)(2,1)S(1)} %copy-done.14, bf16[512,512]{1,0:T(8,128)(2,1)S(1)} %copy-done.16, bf16[400,512]{1,0:T(8,128)(2,1)S(1)} %copy-done.23, ...), custom_call_target="tpu_custom_call" | custom-call | flops 838860800 | bytes 2719752 | tf_op jit(solution)/shard_map/pallas_call | solution.py:43
  193.7 16.1 %collective-permute-done.27.refs_2_ = bf16[400,512]{1,0:T(8,128)(2,1)S(1)} collective-permute-done((bf16[400,512]{1,0:T(8,128)(2,1)}, bf16[400,512]{1,0:T(8,128)(2,1)S(1)}, u32[]{:S(2)}, u32[]{:S(2)}) %collective-permute-start.27) | collective-permute-done | bytes 409632 | tf_op jit(solution)/shard_map/ppermute | solution.py:383
  209.8 0.8 collective-permute-start.24
  210.6 8.0 %collective-permute-done.28.refs_3_ = bf16[400,512]{1,0:T(8,128)(2,1)S(1)} collective-permute-done((bf16[400,512]{1,0:T(8,128)(2,1)}, bf16[400,512]{1,0:T(8,128)(2,1)S(1)}, u32[]{:S(2)}, u32[]{:S(2)}) %collective-permute-start.28) | collective-permute-done | bytes 409632 | tf_op jit(solution)/shard_map/ppermute | solution.py:383
  218.6 1.0 collective-permute-start.25
  219.6 2.2 shard_map.99
  221.8 1.6 collective-permute-start.26
  223.4 0.9 collective-permute-start.29
  224.4 1.0 collective-permute-start.30
  225.4 1.6 collective-permute-start.31
  226.9 6.6 %shard_map.95 = f32[400,2048]{1,0:T(8,128)} custom-call(s32[2]{0:T(128)S(1)} %copy-done.11, bf16[416,512]{1,0:T(8,128)(2,1)S(1)} %get-tuple-element.75.refs_0_, bf16[416,512]{1,0:T(8,128)(2,1)S(1)} %collective-permute-done.19.refs_1_, bf16[416,512]{1,0:T(8,128)(2,1)S(1)} %collective-permute-done.20.refs_2_, ...), custom_call_target="tpu_custom_call" | custom-call | flops 1677721600 | bytes 10878984 | tf_op jit(solution)/shard_map/pallas_call | solution.py:43
  233.5 1.5 collective-permute-done.29.refs_5_
  235.0 4.4 %collective-permute-done.30.refs_6_ = s16[416,256]{1,0:T(8,128)(2,1)S(1)} collective-permute-done((s16[416,256]{1,0:T(8,128)(2,1)S(1)}, s16[416,256]{1,0:T(8,128)(2,1)S(1)}, u32[]{:S(2)}, u32[]{:S(2)}) %collective-permute-start.30) | collective-permute-done | bytes 213024 | tf_op jit(solution)/shard_map/ppermute | solution.py:383
  239.4 6.7 %shard_map.100 = f32[400,2048]{1,0:T(8,128)} custom-call(s32[2]{0:T(128)S(1)} %copy-done.11, s16[416,256]{1,0:T(8,128)(2,1)S(1)} %get-tuple-element.84.refs_0_, s16[416,256]{1,0:T(8,128)(2,1)S(1)} %collective-permute-done.24.refs_1_, s16[416,256]{1,0:T(8,128)(2,1)S(1)} %collective-permute-done.25.refs_2_, ...), custom_call_target="tpu_custom_call" | custom-call | flops 3355443200 | bytes 6029320 | tf_op jit(solution)/shard_map/pallas_call | solution.py:43
  (96 shorter events, 9.8 us)
Async XLA Ops:
  0.6 17.1 %copy-start = (s32[128,64]{0,1:T(8,128)S(1)}, s32[128,64]{0,1:T(8,128)}, u32[]{:S(2)}) copy-start(s32[128,64]{0,1:T(8,128)} %param.12) | copy-start | bytes 98308
  0.7 2.5 copy-start.2
  3.2 91.0 %copy-start.10 = (s32[2]{0:T(128)}, s32[2]{0:T(128)S(1)}, u32[]{:S(2)}) copy-start(s32[2]{0:T(128)S(1)} %pad_add_fusion.at) | copy-start | bytes 28
  3.2 5.1 %copy-start.12 = (f32[400,2048]{1,0:T(8,128)S(1)}, f32[400,2048]{1,0:T(8,128)}, u32[]{:S(2)}) copy-start(f32[400,2048]{1,0:T(8,128)} %value.1) | copy-start | bytes 9830404
  4.2 35.0 %collective-permute-start.8 = (bf16[112,1664]{1,0:T(8,128)(2,1)S(1)}, bf16[112,1664]{1,0:T(8,128)(2,1)}, u32[]{:S(2)}, u32[]{:S(2)}) collective-permute-start(bf16[112,1664]{1,0:T(8,128)(2,1)S(1)} %shard_map.89), channel_id=1, source_target_pairs={{0,24},{4,28},{8,16},{12,20},{16,8},{20,12},{24,0},{28,4},{1,25},{... | collective-permute-start | bytes 1118216 | tf_op jit(solution)/shard_map/ppermute | solution.py:383
  5.9 33.4 %collective-permute-start.7 = (bf16[112,1664]{1,0:T(8,128)(2,1)S(1)}, bf16[112,1664]{1,0:T(8,128)(2,1)}, u32[]{:S(2)}, u32[]{:S(2)}) collective-permute-start(bf16[112,1664]{1,0:T(8,128)(2,1)S(1)} %shard_map.89), channel_id=1, source_target_pairs={{0,16},{4,20},{8,24},{12,28},{16,0},{20,4},{24,8},{28,12},{1,17},{... | collective-permute-start | bytes 1118216 | tf_op jit(solution)/shard_map/ppermute | solution.py:383
  13.3 0.8 copy-start.24
  14.1 12.7 %collective-permute-start = (s16[400,512]{1,0:T(8,128)(2,1)}, s16[400,512]{1,0:T(8,128)(2,1)}, u32[]{:S(2)}, u32[]{:S(2)}) collective-permute-start(s16[400,512]{1,0:T(8,128)(2,1)} %get-tuple-element.54), channel_id=1, source_target_pairs={{0,1},{1,0},{2,3},{3,2},{4,5},{5,4},{6,7},{7,6},{8,9},{9,8},{10,11... | collective-permute-start | bytes 1228808 | tf_op jit(solution)/shard_map/ppermute | solution.py:383
  15.7 23.5 %collective-permute-start.1 = (s16[400,512]{1,0:T(8,128)(2,1)}, s16[400,512]{1,0:T(8,128)(2,1)}, u32[]{:S(2)}, u32[]{:S(2)}) collective-permute-start(s16[400,512]{1,0:T(8,128)(2,1)} %get-tuple-element.55), channel_id=1, source_target_pairs={{0,2},{1,3},{2,0},{3,1},{4,6},{5,7},{6,4},{7,5},{8,10},{9,11},{10,... | collective-permute-start | bytes 1228808 | tf_op jit(solution)/shard_map/ppermute | solution.py:383
  17.2 22.0 %collective-permute-start.2 = (s16[400,512]{1,0:T(8,128)(2,1)}, s16[400,512]{1,0:T(8,128)(2,1)}, u32[]{:S(2)}, u32[]{:S(2)}) collective-permute-start(s16[400,512]{1,0:T(8,128)(2,1)} %get-tuple-element.56), channel_id=1, source_target_pairs={{0,3},{1,2},{2,1},{3,0},{4,7},{5,6},{6,5},{7,4},{8,11},{9,10},{10,... | collective-permute-start | bytes 1228808 | tf_op jit(solution)/shard_map/ppermute | solution.py:383
  26.8 14.6 %collective-permute-start.6 = (bf16[112,1664]{1,0:T(8,128)(2,1)S(1)}, bf16[112,1664]{1,0:T(8,128)(2,1)}, u32[]{:S(2)}, u32[]{:S(2)}) collective-permute-start(bf16[112,1664]{1,0:T(8,128)(2,1)S(1)} %shard_map.89), channel_id=1, source_target_pairs={{0,8},{4,12},{8,0},{12,4},{16,24},{20,28},{24,16},{28,20},{1,9},{5... | collective-permute-start | bytes 1118216 | tf_op jit(solution)/shard_map/ppermute | solution.py:383
  29.7 0.8 copy-start.9
  31.0 10.5 %copy-start.13 = (bf16[512,512]{1,0:T(8,128)(2,1)}, bf16[512,512]{1,0:T(8,128)(2,1)S(1)}, u32[]{:S(2)}) copy-start(bf16[512,512]{1,0:T(8,128)(2,1)S(1)} %get-tuple-element.70.refs_4_.refs_0_) | copy-start | bytes 1572868
  31.0 10.5 %copy-start.15 = (bf16[512,512]{1,0:T(8,128)(2,1)}, bf16[512,512]{1,0:T(8,128)(2,1)S(1)}, u32[]{:S(2)}) copy-start(bf16[512,512]{1,0:T(8,128)(2,1)S(1)} %get-tuple-element.71.refs_5_.refs_1_) | copy-start | bytes 1572868
  31.0 10.4 %copy-start.8 = (f32[400,1]{1,0:T(8,128)S(1)}, f32[400,1]{1,0:T(8,128)}, u32[]{:S(2)}) copy-start(f32[400,1]{1,0:T(8,128)} %copy.10.refs_6_) | copy-start | bytes 4804
  31.0 10.4 %copy-start.25 = (s16[400,512]{1,0:T(8,128)(2,1)S(1)}, s16[400,512]{1,0:T(8,128)(2,1)}, u32[]{:S(2)}) copy-start(s16[400,512]{1,0:T(8,128)(2,1)} %copy-done.24) | copy-start | bytes 1228804
  36.2 0.8 copy-start.6
  37.0 0.7 copy-start.18
  37.7 0.8 copy-start.19
  38.5 0.8 copy-start.21
  46.7 1.2 copy-start.5
  47.9 48.3 %all-to-all-start = ((bf16[4,416,512]{2,1,0:T(8,128)(2,1)}), bf16[4,416,512]{2,1,0:T(8,128)(2,1)}, u32[]{:S(2)}, u32[]{:S(2)}) async-start(bf16[4,416,512]{2,1,0:T(8,128)(2,1)} %copy-done.5), calls=%async_computation | async-start | bytes 3407872 | tf_op jit(solution)/shard_map/all_to_all | solution.py:406
  54.8 12.2 %collective-permute-start.3 = (bf16[400,512]{1,0:T(8,128)(2,1)}, bf16[400,512]{1,0:T(8,128)(2,1)S(1)}, u32[]{:S(2)}, u32[]{:S(2)}) collective-permute-start(bf16[400,512]{1,0:T(8,128)(2,1)} %copy-done.21), channel_id=1, source_target_pairs={{0,1},{1,0},{2,3},{3,2},{4,5},{5,4},{6,7},{7,6},{8,9},{9,8},{10,11... | collective-permute-start | bytes 1228808 | tf_op jit(solution)/shard_map/ppermute | solution.py:383
  56.3 16.5 %collective-permute-start.4 = (bf16[400,512]{1,0:T(8,128)(2,1)}, bf16[400,512]{1,0:T(8,128)(2,1)S(1)}, u32[]{:S(2)}, u32[]{:S(2)}) collective-permute-start(bf16[400,512]{1,0:T(8,128)(2,1)} %copy-done.19), channel_id=1, source_target_pairs={{0,2},{1,3},{2,0},{3,1},{4,6},{5,7},{6,4},{7,5},{8,10},{9,11},{10,... | collective-permute-start | bytes 1228808 | tf_op jit(solution)/shard_map/ppermute | solution.py:383
  57.9 16.8 %collective-permute-start.5 = (bf16[400,512]{1,0:T(8,128)(2,1)}, bf16[400,512]{1,0:T(8,128)(2,1)S(1)}, u32[]{:S(2)}, u32[]{:S(2)}) collective-permute-start(bf16[400,512]{1,0:T(8,128)(2,1)} %copy-done.18), channel_id=1, source_target_pairs={{0,3},{1,2},{2,1},{3,0},{4,7},{5,6},{6,5},{7,4},{8,11},{9,10},{10,... | collective-permute-start | bytes 1228808 | tf_op jit(solution)/shard_map/ppermute | solution.py:383
  74.7 10.1 %collective-permute-start.10 = (bf16[336,896]{1,0:T(8,128)(2,1)S(1)}, bf16[336,896]{1,0:T(8,128)(2,1)S(1)}, u32[]{:S(2)}, u32[]{:S(2)}) collective-permute-start(bf16[336,896]{1,0:T(8,128)(2,1)S(1)} %slice.6), channel_id=1, source_target_pairs={{0,1},{1,0},{2,3},{3,2},{4,5},{5,4},{6,7},{7,6},{8,9},{9,8},{10,11... | collective-permute-start | bytes 1806344 | tf_op jit(solution)/shard_map/ppermute | solution.py:383
  76.3 15.3 %collective-permute-start.12 = (bf16[336,768]{1,0:T(8,128)(2,1)S(1)}, bf16[336,768]{1,0:T(8,128)(2,1)S(1)}, u32[]{:S(2)}, u32[]{:S(2)}) collective-permute-start(bf16[336,768]{1,0:T(8,128)(2,1)S(1)} %slice.7), channel_id=1, source_target_pairs={{0,2},{1,3},{2,0},{3,1},{4,6},{5,7},{6,4},{7,5},{8,10},{9,11},{10,... | collective-permute-start | bytes 1548296 | tf_op jit(solution)/shard_map/ppermute | solution.py:383
  86.0 25.4 %collective-permute-start.11 = (bf16[672,896]{1,0:T(8,128)(2,1)}, bf16[672,896]{1,0:T(8,128)(2,1)}, u32[]{:S(2)}, u32[]{:S(2)}) collective-permute-start(bf16[672,896]{1,0:T(8,128)(2,1)} %pad_maximum_fusion.refs_3_), channel_id=1, source_target_pairs={{0,2},{1,3},{2,0},{3,1},{4,6},{5,7},{6,4},{7,5},{8,10},{9,11},{10,... | collective-permute-start | bytes 3612680 | tf_op jit(solution)/shard_map/ppermute | solution.py:383
  91.6 2.6 %copy-start.7 = (bf16[400,512]{1,0:T(8,128)(2,1)S(1)}, bf16[400,512]{1,0:T(8,128)(2,1)}, u32[]{:S(2)}) copy-start(bf16[400,512]{1,0:T(8,128)(2,1)} %copy-done.6) | copy-start | bytes 1228804
  91.6 19.8 %collective-permute-start.14 = (bf16[400,1664]{1,0:T(8,128)(2,1)}, bf16[400,1664]{1,0:T(8,128)(2,1)}, u32[]{:S(2)}, u32[]{:S(2)}) collective-permute-start(bf16[400,1664]{1,0:T(8,128)(2,1)} %shard_map.92.refs_2_), channel_id=1, source_target_pairs={{0,4},{4,0},{8,12},{12,8},{16,20},{20,16},{24,28},{28,24},{1,5},{5... | collective-permute-start | bytes 3993608 | tf_op jit(solution)/shard_map/ppermute | solution.py:383
  92.7 25.5 %collective-permute-start.13 = (bf16[672,768]{1,0:T(8,128)(2,1)}, bf16[672,768]{1,0:T(8,128)(2,1)}, u32[]{:S(2)}, u32[]{:S(2)}) collective-permute-start(bf16[672,768]{1,0:T(8,128)(2,1)} %pad_maximum_fusion.2.refs_5_), channel_id=1, source_target_pairs={{0,1},{1,0},{2,3},{3,2},{4,5},{5,4},{6,7},{7,6},{8,9},{9,8},{10,11... | collective-permute-start | bytes 3096584 | tf_op jit(solution)/shard_map/ppermute | solution.py:383
  95.0 1.2 copy-start.4
  96.2 41.8 %all-to-all-start.2 = ((bf16[4,400,512]{2,1,0:T(8,128)(2,1)}), bf16[4,400,512]{2,1,0:T(8,128)(2,1)}, u32[]{:S(2)}, u32[]{:S(2)}) async-start(bf16[4,400,512]{2,1,0:T(8,128)(2,1)} %copy-done.4), calls=%async_computation.2 | async-start | bytes 3276800 | tf_op jit(solution)/shard_map/all_to_all | solution.py:406
  101.3 19.9 %collective-permute-start.9 = (bf16[4,416,512]{2,1,0:T(8,128)(2,1)}, bf16[4,416,512]{2,1,0:T(8,128)(2,1)}, u32[]{:S(2)}, u32[]{:S(2)}) collective-permute-start(bf16[4,416,512]{2,1,0:T(8,128)(2,1)} %all-to-all-done.refs_0_), channel_id=1, source_target_pairs={{0,4},{4,0},{8,12},{12,8},{16,20},{20,16},{24,28},{28,24},{1,5},{5... | collective-permute-start | bytes 5111816 | tf_op jit(solution)/shard_map/ppermute | solution.py:383
  101.3 16.9 %collective-permute-start.15 = (bf16[672,896]{1,0:T(8,128)(2,1)}, bf16[672,896]{1,0:T(8,128)(2,1)}, u32[]{:S(2)}, u32[]{:S(2)}) collective-permute-start(bf16[672,896]{1,0:T(8,128)(2,1)} %pad_maximum_fusion.refs_3_), channel_id=1, source_target_pairs={{0,4},{4,0},{8,12},{12,8},{16,20},{20,16},{24,28},{28,24},{1,5},{5... | collective-permute-start | bytes 3612680 | tf_op jit(solution)/shard_map/ppermute | solution.py:383
  111.4 9.9 %collective-permute-start.16 = (bf16[672,896]{1,0:T(8,128)(2,1)}, bf16[672,896]{1,0:T(8,128)(2,1)}, u32[]{:S(2)}, u32[]{:S(2)}) collective-permute-start(bf16[672,896]{1,0:T(8,128)(2,1)} %collective-permute-done.11.refs_4_), channel_id=1, source_target_pairs={{0,4},{4,0},{8,12},{12,8},{16,20},{20,16},{24,28},{28,24},{1,5},{5... | collective-permute-start | bytes 3612680 | tf_op jit(solution)/shard_map/ppermute | solution.py:383
  111.4 6.9 %collective-permute-start.17 = (bf16[672,768]{1,0:T(8,128)(2,1)}, bf16[672,768]{1,0:T(8,128)(2,1)}, u32[]{:S(2)}, u32[]{:S(2)}) collective-permute-start(bf16[672,768]{1,0:T(8,128)(2,1)} %pad_maximum_fusion.2.refs_5_), channel_id=1, source_target_pairs={{0,4},{4,0},{8,12},{12,8},{16,20},{20,16},{24,28},{28,24},{1,5},{5... | collective-permute-start | bytes 3096584 | tf_op jit(solution)/shard_map/ppermute | solution.py:383
  118.3 3.0 %collective-permute-start.18 = (bf16[672,768]{1,0:T(8,128)(2,1)}, bf16[672,768]{1,0:T(8,128)(2,1)}, u32[]{:S(2)}, u32[]{:S(2)}) collective-permute-start(bf16[672,768]{1,0:T(8,128)(2,1)} %collective-permute-done.13.refs_6_), channel_id=1, source_target_pairs={{0,4},{4,0},{8,12},{12,8},{16,20},{20,16},{24,28},{28,24},{1,5},{5... | collective-permute-start | bytes 3096584 | tf_op jit(solution)/shard_map/ppermute | solution.py:383
  138.1 42.7 %all-to-all-start.1 = ((bf16[4,416,512]{2,1,0:T(8,128)(2,1)}), bf16[4,416,512]{2,1,0:T(8,128)(2,1)}, u32[]{:S(2)}, u32[]{:S(2)}) async-start(bf16[4,416,512]{2,1,0:T(8,128)(2,1)} %get-tuple-element.74.totals), calls=%async_computation.1 | async-start | bytes 3407872 | tf_op jit(solution)/shard_map/all_to_all | solution.py:406
  144.6 1.5 copy-start.3
  146.1 5.5 %copy-start.11 = (s32[2]{0:T(128)S(1)}, s32[2]{0:T(128)}, u32[]{:S(2)}) copy-start(s32[2]{0:T(128)} %copy-done.10) | copy-start | bytes 28
  148.0 3.6 %collective-permute-start.22 = (bf16[4,400,512]{2,1,0:T(8,128)(2,1)S(1)}, bf16[4,400,512]{2,1,0:T(8,128)(2,1)S(1)}, u32[]{:S(2)}, u32[]{:S(2)}) collective-permute-start(bf16[4,400,512]{2,1,0:T(8,128)(2,1)S(1)} %shard_map.96.own), channel_id=1, source_target_pairs={{0,4},{4,0},{8,12},{12,8},{16,20},{20,16},{24,28},{28,24},{1,5},{5... | collective-permute-start | bytes 4915208 | tf_op jit(solution)/shard_map/ppermute | solution.py:383
  161.8 0.8 copy-start.17
  162.6 0.8 copy-start.20
  163.3 0.8 copy-start.22
  164.1 25.0 %collective-permute-start.23 = (bf16[400,512]{1,0:T(8,128)(2,1)}, bf16[400,512]{1,0:T(8,128)(2,1)}, u32[]{:S(2)}, u32[]{:S(2)}) collective-permute-start(bf16[400,512]{1,0:T(8,128)(2,1)} %get-tuple-element.83), channel_id=1, source_target_pairs={{0,8},{4,12},{8,0},{12,4},{16,24},{20,28},{24,16},{28,20},{1,9},{5... | collective-permute-start | bytes 1228808 | tf_op jit(solution)/shard_map/ppermute | solution.py:383
  180.8 10.2 %copy-start.14 = (bf16[512,512]{1,0:T(8,128)(2,1)S(1)}, bf16[512,512]{1,0:T(8,128)(2,1)}, u32[]{:S(2)}) copy-start(bf16[512,512]{1,0:T(8,128)(2,1)} %copy-done.13) | copy-start | bytes 1572868
  180.8 10.2 %copy-start.16 = (bf16[512,512]{1,0:T(8,128)(2,1)S(1)}, bf16[512,512]{1,0:T(8,128)(2,1)}, u32[]{:S(2)}) copy-start(bf16[512,512]{1,0:T(8,128)(2,1)} %copy-done.15) | copy-start | bytes 1572868
  180.8 10.2 %copy-start.23 = (bf16[400,512]{1,0:T(8,128)(2,1)S(1)}, bf16[400,512]{1,0:T(8,128)(2,1)}, u32[]{:S(2)}) copy-start(bf16[400,512]{1,0:T(8,128)(2,1)} %copy-done.22) | copy-start | bytes 1228804
  180.8 29.1 %collective-permute-start.27 = (bf16[400,512]{1,0:T(8,128)(2,1)}, bf16[400,512]{1,0:T(8,128)(2,1)S(1)}, u32[]{:S(2)}, u32[]{:S(2)}) collective-permute-start(bf16[400,512]{1,0:T(8,128)(2,1)} %copy-done.20), channel_id=1, source_target_pairs={{0,16},{4,20},{8,24},{12,28},{16,0},{20,4},{24,8},{28,12},{1,17},{... | collective-permute-start | bytes 1228808 | tf_op jit(solution)/shard_map/ppermute | solution.py:383
  184.2 34.4 %collective-permute-start.28 = (bf16[400,512]{1,0:T(8,128)(2,1)}, bf16[400,512]{1,0:T(8,128)(2,1)S(1)}, u32[]{:S(2)}, u32[]{:S(2)}) collective-permute-start(bf16[400,512]{1,0:T(8,128)(2,1)} %copy-done.17), channel_id=1, source_target_pairs={{0,24},{4,28},{8,16},{12,20},{16,8},{20,12},{24,0},{28,4},{1,25},{... | collective-permute-start | bytes 1228808 | tf_op jit(solution)/shard_map/ppermute | solution.py:383
  187.4 34.3 %collective-permute-start.19 = (bf16[416,512]{1,0:T(8,128)(2,1)S(1)}, bf16[416,512]{1,0:T(8,128)(2,1)S(1)}, u32[]{:S(2)}, u32[]{:S(2)}) collective-permute-start(bf16[416,512]{1,0:T(8,128)(2,1)S(1)} %get-tuple-element.76), channel_id=1, source_target_pairs={{0,1},{1,0},{2,3},{3,2},{4,5},{5,4},{6,7},{7,6},{8,9},{9,8},{10,11... | collective-permute-start | bytes 1277960 | tf_op jit(solution)/shard_map/ppermute | solution.py:383
  188.3 35.1 %collective-permute-start.20 = (bf16[416,512]{1,0:T(8,128)(2,1)S(1)}, bf16[416,512]{1,0:T(8,128)(2,1)S(1)}, u32[]{:S(2)}, u32[]{:S(2)}) collective-permute-start(bf16[416,512]{1,0:T(8,128)(2,1)S(1)} %get-tuple-element.77), channel_id=1, source_target_pairs={{0,2},{1,3},{2,0},{3,1},{4,6},{5,7},{6,4},{7,5},{8,10},{9,11},{10,... | collective-permute-start | bytes 1277960 | tf_op jit(solution)/shard_map/ppermute | solution.py:383
  189.1 35.3 %collective-permute-start.21 = (bf16[416,512]{1,0:T(8,128)(2,1)S(1)}, bf16[416,512]{1,0:T(8,128)(2,1)S(1)}, u32[]{:S(2)}, u32[]{:S(2)}) collective-permute-start(bf16[416,512]{1,0:T(8,128)(2,1)S(1)} %get-tuple-element.78), channel_id=1, source_target_pairs={{0,3},{1,2},{2,1},{3,0},{4,7},{5,6},{6,5},{7,4},{8,11},{9,10},{10,... | collective-permute-start | bytes 1277960 | tf_op jit(solution)/shard_map/ppermute | solution.py:383
  209.8 15.5 %collective-permute-start.24 = (s16[416,256]{1,0:T(8,128)(2,1)S(1)}, s16[416,256]{1,0:T(8,128)(2,1)S(1)}, u32[]{:S(2)}, u32[]{:S(2)}) collective-permute-start(s16[416,256]{1,0:T(8,128)(2,1)S(1)} %get-tuple-element.85), channel_id=1, source_target_pairs={{0,1},{1,0},{2,3},{3,2},{4,5},{5,4},{6,7},{7,6},{8,9},{9,8},{10,11... | collective-permute-start | bytes 638984 | tf_op jit(solution)/shard_map/ppermute | solution.py:383
  218.6 14.9 %collective-permute-start.25 = (s16[416,256]{1,0:T(8,128)(2,1)S(1)}, s16[416,256]{1,0:T(8,128)(2,1)S(1)}, u32[]{:S(2)}, u32[]{:S(2)}) collective-permute-start(s16[416,256]{1,0:T(8,128)(2,1)S(1)} %get-tuple-element.86), channel_id=1, source_target_pairs={{0,2},{1,3},{2,0},{3,1},{4,6},{5,7},{6,4},{7,5},{8,10},{9,11},{10,... | collective-permute-start | bytes 638984 | tf_op jit(solution)/shard_map/ppermute | solution.py:383
  221.8 11.7 %collective-permute-start.26 = (s16[416,256]{1,0:T(8,128)(2,1)S(1)}, s16[416,256]{1,0:T(8,128)(2,1)S(1)}, u32[]{:S(2)}, u32[]{:S(2)}) collective-permute-start(s16[416,256]{1,0:T(8,128)(2,1)S(1)} %get-tuple-element.87), channel_id=1, source_target_pairs={{0,3},{1,2},{2,1},{3,0},{4,7},{5,6},{6,5},{7,4},{8,11},{9,10},{10,... | collective-permute-start | bytes 638984 | tf_op jit(solution)/shard_map/ppermute | solution.py:383
  223.4 11.6 %collective-permute-start.29 = (s16[416,256]{1,0:T(8,128)(2,1)S(1)}, s16[416,256]{1,0:T(8,128)(2,1)S(1)}, u32[]{:S(2)}, u32[]{:S(2)}) collective-permute-start(s16[416,256]{1,0:T(8,128)(2,1)S(1)} %get-tuple-element.93), channel_id=1, source_target_pairs={{0,1},{1,0},{2,3},{3,2},{4,5},{5,4},{6,7},{7,6},{8,9},{9,8},{10,11... | collective-permute-start | bytes 638984 | tf_op jit(solution)/shard_map/ppermute | solution.py:383
  224.4 15.1 %collective-permute-start.30 = (s16[416,256]{1,0:T(8,128)(2,1)S(1)}, s16[416,256]{1,0:T(8,128)(2,1)S(1)}, u32[]{:S(2)}, u32[]{:S(2)}) collective-permute-start(s16[416,256]{1,0:T(8,128)(2,1)S(1)} %get-tuple-element.94), channel_id=1, source_target_pairs={{0,2},{1,3},{2,0},{3,1},{4,6},{5,7},{6,4},{7,5},{8,10},{9,11},{10,... | collective-permute-start | bytes 638984 | tf_op jit(solution)/shard_map/ppermute | solution.py:383
  225.4 14.1 %collective-permute-start.31 = (s16[416,256]{1,0:T(8,128)(2,1)S(1)}, s16[416,256]{1,0:T(8,128)(2,1)S(1)}, u32[]{:S(2)}, u32[]{:S(2)}) collective-permute-start(s16[416,256]{1,0:T(8,128)(2,1)S(1)} %get-tuple-element.95), channel_id=1, source_target_pairs={{0,3},{1,2},{2,1},{3,0},{4,7},{5,6},{6,5},{7,4},{8,11},{9,10},{10,... | collective-permute-start | bytes 638984 | tf_op jit(solution)/shard_map/ppermute | solution.py:383
  239.4 6.7 %copy-start.1 = (s32[128,64]{0,1:T(8,128)S(1)}, s32[128,64]{0,1:T(8,128)}, u32[]{:S(2)}) copy-start(s32[128,64]{0,1:T(8,128)} %param.12) | copy-start | bytes 98308

commit v3 on v2

--- a/solution.py
+++ b/solution.py
@@ -298,10 +298,8 @@
         outs[j][...] = movers[(at[0] // 2) ^ j]
 
 
-def tail_kernel(plan, at, *refs):
-    ni, rows, w = plan.n_inc, plan.rows, plan.wide
-    mix_a, mix_b, *refs = refs
-    ins, outs, mixed = refs[: -1 - ni], refs[-1 - ni : -1], refs[-1]
+def code_blocks(plan, mix_a, mix_b, ins, mixed):
+    rows = plan.rows
     for i, part in enumerate(ins):
         x = part[...]
         new = dot_nt(x, mix_a[...]) + dot_nt(x, mix_b[...])
@@ -309,11 +307,16 @@
         power = jnp.ceil(jnp.log2(most))
         code = jnp.minimum(jnp.round(new * jnp.exp2(15.0 - power)), HALF - 1.0)
         mixed[:rows, :] = code.astype(jnp.int32)
-        mixed[rows:, :] = jnp.broadcast_to(power, (TILE, w)).astype(jnp.int32)
-        for k in range(ni):
-            outs[k][:, i * LANES : (i + 1) * LANES] = mixed[
-                :, lanes_at((at[1] ^ k) * LANES, LANES)
-            ].astype(jnp.int16)
+        mixed[rows:, :] = jnp.broadcast_to(power, (TILE, plan.wide)).astype(jnp.int32)
+        yield i
+
+
+def tail_kernel(plan, at, mix_a, mix_b, *refs):
+    ins, outs, mixed = refs[: -1 - plan.n_inc], refs[-1 - plan.n_inc : -1], refs[-1]
+    for i in code_blocks(plan, mix_a, mix_b, ins, mixed):
+        for k in range(plan.n_inc):
+            block = mixed[:, lanes_at((at[1] ^ k) * LANES, LANES)].astype(jnp.int16)
+            outs[k][:, i * LANES : (i + 1) * LANES] = block
 
 
 def next_mass_kernel(plan, at, *refs):
@@ -442,15 +445,8 @@
     mix_a, mix_b = call(
         bind(mix_kernel), [S((w, w), BF)] * 2, [trans_weight], specs=[VMEM]
     )
-    (own_near,) = call(
-        bind(window_kernel),
-        [S((rows, plan.window), BF)],
-        [at, move_cost],
-        [pltpu.VMEM((rows, ring), BF)],
-    )
     masses, codes = after(masses, codes)
     masses = exchange(masses, "inc", ni)
-    codes, _ = after(codes, pieces)
 
     live = (live_mask > 0).astype(F32)[:, None]
     weights = call(
@@ -460,13 +456,21 @@
         [pltpu.VMEM((rows, w), jnp.int32)],
         3 * pass_flops,
     )
-    weights = along_z(weights[0])
+    weights, _ = after(weights[0], pieces)
+    weights = along_z(weights)
     others = swap_core(weights)
 
     strip, _ = after(jnp.concatenate(pieces), masses)
     left, right = strip[:, : plan.cut], strip[:, plan.cut :]
     left = jnp.concatenate([left, swap(left, "inc", ni, 1)])
     right = jnp.concatenate([right, swap(right, "inc", ni, 2)])
+    later_cost, _ = after(move_cost, (left, right))
+    (own_near,) = call(
+        bind(window_kernel),
+        [S((rows, plan.window), BF)],
+        [at, later_cost],
+        [pltpu.VMEM((rows, ring), BF)],
+    )
     near = [own_near, left, swap(left, "inc", ni, 2), right, swap(right, "inc", ni, 1)]
     near = near + [swap_core(x) for x in near]
 
@@ -511,32 +515,33 @@
     close = [movers[0], swap(movers[1], "loc", nl, 2)]
     far = [swap(x, "loc", nl, 2 * (j + 2)) for j, x in enumerate(far)]
 
-    moved = []
-    for part in (close, far):
-        blocks = call(
-            bind(tail_kernel),
-            [S((packed, len(part) * LANES), jnp.int16)] * ni,
-            [at, mix_a, mix_b, *part],
-            [pltpu.VMEM((packed, w), jnp.int32)],
-            pass_flops,
-        )
-        moved += exchange(blocks, "inc", ni)
+    pack = lambda part, outs, kernel: call(
+        bind(kernel),
+        outs,
+        [at, mix_a, mix_b, *part],
+        [pltpu.VMEM((packed, w), jnp.int32)],
+        pass_flops,
+    )
+    close = pack(close, [S((packed, 2 * LANES), jnp.int16)] * ni, tail_kernel)
+    close = exchange(close, "inc", ni)
     sent = call(bind(collect_kernel), [S((packed, w), BF)] * ni, [at, sent])
     sent = exchange(sent, "inc", ni)
-
-    (new_mass,) = call(
-        bind(next_mass_kernel),
-        [S((rows, plan.columns), F32)],
-        [at, *moved, first, second],
-        [pltpu.VMEM((packed, w), jnp.int32)] + [pltpu.VMEM((ni, packed, w), BF)] * 2,
-        4 * pass_flops,
-    )
     (new_value,) = call(
         bind(value_kernel),
         [S((rows, plan.columns), F32)],
         [at, *sent, hit, second, flow_util],
         [pltpu.VMEM((ni, packed, w), BF)],
         2 * pass_flops,
+    )
+    far, _ = after(far, (close, new_value))
+    far = pack(far, [S((packed, 2 * LANES), jnp.int16)] * ni, tail_kernel)
+    far = exchange(far, "inc", ni)
+    (new_mass,) = call(
+        bind(next_mass_kernel),
+        [S((rows, plan.columns), F32)],
+        [at, *close, *far, first, second],
+        [pltpu.VMEM((packed, w), jnp.int32)] + [pltpu.VMEM((ni, packed, w), BF)] * 2,
+        4 * pass_flops,
     )
     return new_value, new_mass
 

time: 247 us -> 237 us (0.960)
  waiting for transfers between devices: 103 us -> 93.2 us
  local copies, waits for them, and re-layouts: 14.5 us -> 17.2 us
    ppermute x32, waiting for transfers between devices: 86.4 us -> 75.8 us  [swap(): return lax.ppermute(x, axis, [(s, s ^ k) for s in range(n)]) if k else x]
    unnamed x52 -> x70, local copies, waits for them, and re-layouts: 13.2 us -> 15.9 us
  transfers between devices with their start and end apart: 35 -> 35, of which waited for: 15 -> 17; matrix products, arithmetic and copies ran while one was open for 3% -> 3% of each run, Pallas kernels for 24% -> 25%
where the time goes in v3:
time: 237 us; the launch traced here: 236 us
  waiting for transfers between devices  93.2 us (39%)
  Pallas kernels  70.1 us (30%)
  starting transfers between devices  49.2 us (21%)
  local copies, waits for them, and re-layouts  17.2 us (7%)
  other arithmetic  5.3 us (2%)
    ppermute x32, waiting for transfers between devices, swap(): return lax.ppermute(x, axis, [(s, s ^ k) for s in range(n)]) if k else x  75.8 us
    pallas_call x15, Pallas kernels, call(): pl.pallas_call(kernel, out_shape=tuple(outs), in_specs=specs or [SMEM] +...  70.1 us
    ppermute x32, starting transfers between devices, swap(): return lax.ppermute(x, axis, [(s, s ^ k) for s in range(n)]) if k else x  32.3 us
    all_to_all x3, waiting for transfers between devices, state_split(): along_z = lambda x: lax.all_to_all(x, 'loc', 0, 0, axis_index_groups=lines)  17.4 us
    all_to_all x3, starting transfers between devices, state_split(): along_z = lambda x: lax.all_to_all(x, 'loc', 0, 0, axis_index_groups=lines)  16.9 us
    unnamed x70, local copies, waits for them, and re-layouts  15.9 us
  transfers between devices with their start and end apart: 35, of which 17 were waited for; matrix products, arithmetic and copies ran while one was open for 3% of the time, Pallas kernels for 25%

profile of v3, /device:TPU:8, one launch (start us, length us, event | category | flops | bytes accessed | tf_op | source)
XLA Modules:
  0.0 236.1 jit_solution(2956978934460490791)
XLA Ops:
  0.7 2.4 %copy-done.2 = f32[400,3200]{1,0:T(8,128)S(1)} copy-done((f32[400,3200]{1,0:T(8,128)S(1)}, f32[400,3200]{1,0:T(8,128)}, u32[]{:S(2)}) %copy-start.2) | copy-done | bytes 5120024
  3.2 1.1 shard_map.91
  4.2 1.6 collective-permute-start.8
  5.9 1.1 collective-permute-start.7
  7.0 1.2 fusion.12
  8.3 5.1 %shard_map.87 = (s16[400,512]{1,0:T(8,128)(2,1)S(1)}, s16[400,512]{1,0:T(8,128)(2,1)}, s16[400,512]{1,0:T(8,128)(2,1)}, s16[400,512]{1,0:T(8,128)(2,1)}) custom-call(s32[2]{0:T(128)S(1)} %pad_add_fusion.at, f32[400,2048]{1,0:T(8,128)S(1)} %copy-done.13, bf16[512,512]{1,0:T(8,128)(2,1)S(1)} %get-tuple-element.96.first.refs_8_, ...), custom_call_target="tpu_custom_call" | custom-call | flops 3355443200 | bytes 5963784 | tf_op jit(solution)/shard_map/pallas_call | solution.py:43
  13.4 1.6 collective-permute-start
  15.0 1.5 collective-permute-start.1
  17.3 0.9 copy.10.refs_6_
  19.2 6.8 %collective-permute-done.refs_1_ = s16[400,512]{1,0:T(8,128)(2,1)S(1)} collective-permute-done((s16[400,512]{1,0:T(8,128)(2,1)}, s16[400,512]{1,0:T(8,128)(2,1)S(1)}, u32[]{:S(2)}, u32[]{:S(2)}) %collective-permute-start) | collective-permute-done | bytes 409632 | tf_op jit(solution)/shard_map/ppermute | solution.py:386
  26.8 1.4 collective-permute-start.6
  28.2 4.8 %shard_map.86 = (bf16[400,512]{1,0:T(8,128)(2,1)S(1)}, bf16[400,512]{1,0:T(8,128)(2,1)S(1)}, bf16[400,512]{1,0:T(8,128)(2,1)S(1)}, bf16[400,512]{1,0:T(8,128)(2,1)S(1)}) custom-call(s32[2]{0:T(128)S(1)} %pad_add_fusion.at, f32[400,2048]{1,0:T(8,128)} %mass.1, bf16[4,512,512]{2,1,0:T(8,128)(2,1)S(1)} %fusion.hit.refs_4_, ...), custom_call_target="tpu_custom_call" | custom-call | flops 2516582400 | bytes 7536648 | tf_op jit(solution)/shard_map/pallas_call | solution.py:43
  33.8 0.8 copy-done.24
  35.4 5.3 %shard_map.90 = bf16[4,416,512]{2,1,0:T(8,128)(2,1)S(1)} custom-call(s32[2]{0:T(128)S(1)} %pad_add_fusion.at, s16[400,512]{1,0:T(8,128)(2,1)S(1)} %copy-done.29, s16[400,512]{1,0:T(8,128)(2,1)S(1)} %copy-done.22, s16[400,512]{1,0:T(8,128)(2,1)} %collective-permute-done.1.refs_2_, s16[400,512]{1,0:T(8,128)(2,1)} %collective-permute-done.2.refs_3_, ...), custom_call_target="tpu_custom_call" | custom-call | flops 2516582400 | bytes 4392520 | tf_op jit(solution)/shard_map/pallas_call | solution.py:43
  40.7 1.2 copy-done.5
  41.8 6.6 %all-to-all-start = ((bf16[4,416,512]{2,1,0:T(8,128)(2,1)}), bf16[4,416,512]{2,1,0:T(8,128)(2,1)}, u32[]{:S(2)}, u32[]{:S(2)}) async-start(bf16[4,416,512]{2,1,0:T(8,128)(2,1)} %copy-done.5), calls=%async_computation | async-start | bytes 3407872 | tf_op jit(solution)/shard_map/all_to_all | solution.py:409
  48.4 1.5 collective-permute-start.3
  49.9 1.5 collective-permute-start.4
  51.9 1.3 pad_maximum_fusion.1
  53.2 7.8 %collective-permute-done.3.refs_1_ = bf16[400,512]{1,0:T(8,128)(2,1)S(1)} collective-permute-done((bf16[400,512]{1,0:T(8,128)(2,1)}, bf16[400,512]{1,0:T(8,128)(2,1)S(1)}, u32[]{:S(2)}, u32[]{:S(2)}) %collective-permute-start.3) | collective-permute-done | bytes 409632 | tf_op jit(solution)/shard_map/ppermute | solution.py:386
  61.0 4.7 %collective-permute-done.4.refs_2_ = bf16[400,512]{1,0:T(8,128)(2,1)S(1)} collective-permute-done((bf16[400,512]{1,0:T(8,128)(2,1)}, bf16[400,512]{1,0:T(8,128)(2,1)S(1)}, u32[]{:S(2)}, u32[]{:S(2)}) %collective-permute-start.4) | collective-permute-done | bytes 409632 | tf_op jit(solution)/shard_map/ppermute | solution.py:386
  65.7 2.0 collective-permute-done.5.refs_3_
  67.8 1.6 collective-permute-start.10
  69.9 8.4 %collective-permute-done.10 = bf16[336,896]{1,0:T(8,128)(2,1)S(1)} collective-permute-done((bf16[336,896]{1,0:T(8,128)(2,1)S(1)}, bf16[336,896]{1,0:T(8,128)(2,1)S(1)}, u32[]{:S(2)}, u32[]{:S(2)}) %collective-permute-start.10) | collective-permute-done | bytes 602144 | tf_op jit(solution)/shard_map/ppermute | solution.py:386
  78.3 1.1 pad_maximum_fusion.refs_3_
  79.4 1.3 collective-permute-start.12
  80.7 1.0 pad_maximum_fusion.2.refs_5_
  81.8 1.5 collective-permute-start.13
  83.2 0.8 shard_map.88
  84.1 1.2 copy-done.4
  85.3 5.3 %all-to-all-start.2 = ((bf16[4,400,512]{2,1,0:T(8,128)(2,1)}), bf16[4,400,512]{2,1,0:T(8,128)(2,1)}, u32[]{:S(2)}, u32[]{:S(2)}) async-start(bf16[4,400,512]{2,1,0:T(8,128)(2,1)} %copy-done.4), calls=%async_computation.2 | async-start | bytes 3276800 | tf_op jit(solution)/shard_map/all_to_all | solution.py:409
  90.5 3.5 %shard_map.92.refs_2_ = bf16[400,1664]{1,0:T(8,128)(2,1)S(1)} custom-call(s32[2]{0:T(128)S(1)} %pad_add_fusion.at, f32[400,3200]{1,0:T(8,128)} %cost.2), custom_call_target="tpu_custom_call" | custom-call | bytes 6451208 | tf_op jit(solution)/shard_map/pallas_call | solution.py:43
  94.8 9.8 %collective-permute-done.12.refs_4_ = bf16[672,896]{1,0:T(8,128)(2,1)} collective-permute-done((bf16[672,896]{1,0:T(8,128)(2,1)}, bf16[672,896]{1,0:T(8,128)(2,1)}, u32[]{:S(2)}, u32[]{:S(2)}) %collective-permute-start.12) | collective-permute-done | bytes 1204256 | tf_op jit(solution)/shard_map/ppermute | solution.py:386
  104.5 2.8 %collective-permute-done.13.refs_6_ = bf16[672,768]{1,0:T(8,128)(2,1)} collective-permute-done((bf16[672,768]{1,0:T(8,128)(2,1)}, bf16[672,768]{1,0:T(8,128)(2,1)}, u32[]{:S(2)}, u32[]{:S(2)}) %collective-permute-start.13) | collective-permute-done | bytes 1032224 | tf_op jit(solution)/shard_map/ppermute | solution.py:386
  107.3 1.1 copy-done.31
  108.4 1.7 collective-permute-done.18.refs_11_
  110.2 1.0 copy-done.34
  111.2 1.1 copy-done.33
  112.3 16.8 %shard_map.93 = (bf16[4,416,512]{2,1,0:T(8,128)(2,1)}, bf16[4,400,512]{2,1,0:T(8,128)(2,1)}, bf16[1600,3200]{1,0:T(8,128)(2,1)}) custom-call(s32[2]{0:T(128)} %copy-done.11, bf16[4,416,512]{2,1,0:T(8,128)(2,1)} %all-to-all-done.refs_0_, bf16[4,416,512]{2,1,0:T(8,128)(2,1)} %collective-permute-done.9.refs_1_, bf16[400,1664]{1,0:T(8,128)(2,1)} %copy-done.6, ...), custom_call_target="tpu_custom_call" | custom-call | flops 5242880000 | bytes 28598280 | tf_op jit(solution)/shard_map/pallas_call | solution.py:43
  129.1 5.1 %all-to-all-start.1 = ((bf16[4,416,512]{2,1,0:T(8,128)(2,1)}), bf16[4,416,512]{2,1,0:T(8,128)(2,1)}, u32[]{:S(2)}, u32[]{:S(2)}) async-start(bf16[4,416,512]{2,1,0:T(8,128)(2,1)} %get-tuple-element.72.totals), calls=%async_computation.1 | async-start | bytes 3407872 | tf_op jit(solution)/shard_map/all_to_all | solution.py:409
  134.2 1.5 copy-done.3
  135.7 1.9 shard_map.96.own
  137.7 3.5 %collective-permute-done.22.other = bf16[4,400,512]{2,1,0:T(8,128)(2,1)S(1)} collective-permute-done((bf16[4,400,512]{2,1,0:T(8,128)(2,1)S(1)}, bf16[4,400,512]{2,1,0:T(8,128)(2,1)S(1)}, u32[]{:S(2)}, u32[]{:S(2)}) %collective-permute-start.22) | collective-permute-done | bytes 1638432 | tf_op jit(solution)/shard_map/ppermute | solution.py:386
  141.2 10.2 %shard_map.97 = (bf16[400,512]{1,0:T(8,128)(2,1)S(1)}, bf16[400,512]{1,0:T(8,128)(2,1)}, bf16[400,512]{1,0:T(8,128)(2,1)S(1)}, bf16[400,512]{1,0:T(8,128)(2,1)S(1)}) custom-call(s32[2]{0:T(128)S(1)} %copy-done.12, bf16[4,400,512]{2,1,0:T(8,128)(2,1)S(1)} %shard_map.96.own, bf16[4,400,512]{2,1,0:T(8,128)(2,1)S(1)} %collective-permute-done.22.other, ...), custom_call_target="tpu_custom_call" | custom-call | flops 5242880000 | bytes 16793608 | tf_op jit(solution)/shard_map/pallas_call | solution.py:43
  153.7 17.3 %all-to-all-done.1.refs_0_ = bf16[4,416,512]{2,1,0:T(8,128)(2,1)} async-done(((bf16[4,416,512]{2,1,0:T(8,128)(2,1)}), bf16[4,416,512]{2,1,0:T(8,128)(2,1)}, u32[]{:S(2)}, u32[]{:S(2)}) %all-to-all-start.1) | async-done | bytes 1703968 | tf_op jit(solution)/shard_map/all_to_all | solution.py:409
  171.0 1.8 shard_map.94
  172.9 1.6 collective-permute-start.19
  175.2 1.2 collective-permute-start.21
  176.4 3.4 %collective-permute-start.27 = (bf16[400,512]{1,0:T(8,128)(2,1)}, bf16[400,512]{1,0:T(8,128)(2,1)S(1)}, u32[]{:S(2)}, u32[]{:S(2)}) collective-permute-start(bf16[400,512]{1,0:T(8,128)(2,1)} %copy-done.20), channel_id=1, source_target_pairs={{0,16},{4,20},{8,24},{12,28},{16,0},{20,4},{24,8},{28,12},{1,17},{... | collective-permute-start | bytes 1228808 | tf_op jit(solution)/shard_map/ppermute | solution.py:386
  179.9 1.4 collective-permute-start.28
  181.2 1.0 copy-done.27
  182.2 2.7 %shard_map.98 = (s16[416,256]{1,0:T(8,128)(2,1)S(1)}, s16[416,256]{1,0:T(8,128)(2,1)S(1)}, s16[416,256]{1,0:T(8,128)(2,1)S(1)}, s16[416,256]{1,0:T(8,128)(2,1)S(1)}) custom-call(s32[2]{0:T(128)S(1)} %copy-done.12, bf16[512,512]{1,0:T(8,128)(2,1)S(1)} %copy-done.15, bf16[512,512]{1,0:T(8,128)(2,1)S(1)} %copy-done.17, bf16[400,512]{1,0:T(8,128)(2,1)S(1)} %copy-done.27, ...), custom_call_target="tpu_custom_call" | custom-call | flops 838860800 | bytes 2719752 | tf_op jit(solution)/shard_map/pallas_call | solution.py:43
  184.9 0.8 collective-permute-done.19.refs_1_
  185.7 1.5 collective-permute-start.24
  187.2 7.4 %collective-permute-done.20.refs_2_ = bf16[416,512]{1,0:T(8,128)(2,1)S(1)} collective-permute-done((bf16[416,512]{1,0:T(8,128)(2,1)S(1)}, bf16[416,512]{1,0:T(8,128)(2,1)S(1)}, u32[]{:S(2)}, u32[]{:S(2)}) %collective-permute-start.20) | collective-permute-done | bytes 426016 | tf_op jit(solution)/shard_map/ppermute | solution.py:386
  195.1 2.2 collective-permute-start.26
  197.3 6.6 %shard_map.95 = f32[400,2048]{1,0:T(8,128)} custom-call(s32[2]{0:T(128)S(1)} %copy-done.12, bf16[416,512]{1,0:T(8,128)(2,1)S(1)} %get-tuple-element.73.refs_0_, bf16[416,512]{1,0:T(8,128)(2,1)S(1)} %collective-permute-done.19.refs_1_, bf16[416,512]{1,0:T(8,128)(2,1)S(1)} %collective-permute-done.20.refs_2_, ...), custom_call_target="tpu_custom_call" | custom-call | flops 1677721600 | bytes 10878984 | tf_op jit(solution)/shard_map/pallas_call | solution.py:43
  204.6 9.5 %collective-permute-done.28.refs_1_ = bf16[400,512]{1,0:T(8,128)(2,1)S(1)} collective-permute-done((bf16[400,512]{1,0:T(8,128)(2,1)S(1)}, bf16[400,512]{1,0:T(8,128)(2,1)S(1)}, u32[]{:S(2)}, u32[]{:S(2)}) %collective-permute-start.28) | collective-permute-done | bytes 409632 | tf_op jit(solution)/shard_map/ppermute | solution.py:386
  214.1 2.2 shard_map.99
  216.3 1.6 collective-permute-start.29
  218.6 1.3 collective-permute-start.31
  219.9 4.6 %collective-permute-done.29.refs_5_ = s16[416,256]{1,0:T(8,128)(2,1)S(1)} collective-permute-done((s16[416,256]{1,0:T(8,128)(2,1)S(1)}, s16[416,256]{1,0:T(8,128)(2,1)S(1)}, u32[]{:S(2)}, u32[]{:S(2)}) %collective-permute-start.29) | collective-permute-done | bytes 213024 | tf_op jit(solution)/shard_map/ppermute | solution.py:386
  224.5 4.8 %collective-permute-done.30.refs_6_ = s16[416,256]{1,0:T(8,128)(2,1)S(1)} collective-permute-done((s16[416,256]{1,0:T(8,128)(2,1)S(1)}, s16[416,256]{1,0:T(8,128)(2,1)S(1)}, u32[]{:S(2)}, u32[]{:S(2)}) %collective-permute-start.30) | collective-permute-done | bytes 213024 | tf_op jit(solution)/shard_map/ppermute | solution.py:386
  229.4 6.8 %shard_map.100 = f32[400,2048]{1,0:T(8,128)} custom-call(s32[2]{0:T(128)S(1)} %copy-done.12, s16[416,256]{1,0:T(8,128)(2,1)S(1)} %get-tuple-element.82.refs_0_, s16[416,256]{1,0:T(8,128)(2,1)S(1)} %collective-permute-done.24.refs_1_, s16[416,256]{1,0:T(8,128)(2,1)S(1)} %collective-permute-done.25.refs_2_, ...), custom_call_target="tpu_custom_call" | custom-call | flops 3355443200 | bytes 6029320 | tf_op jit(solution)/shard_map/pallas_call | solution.py:43
  (114 shorter events, 10.9 us)
Async XLA Ops:
  0.6 16.4 %copy-start = (s32[128,64]{0,1:T(8,128)S(1)}, s32[128,64]{0,1:T(8,128)}, u32[]{:S(2)}) copy-start(s32[128,64]{0,1:T(8,128)} %param.12) | copy-start | bytes 98308
  0.7 2.5 %copy-start.2 = (f32[400,3200]{1,0:T(8,128)S(1)}, f32[400,3200]{1,0:T(8,128)}, u32[]{:S(2)}) copy-start(f32[400,3200]{1,0:T(8,128)} %cost.2) | copy-start | bytes 15360004
  3.2 87.4 %copy-start.11 = (s32[2]{0:T(128)}, s32[2]{0:T(128)S(1)}, u32[]{:S(2)}) copy-start(s32[2]{0:T(128)S(1)} %pad_add_fusion.at) | copy-start | bytes 28
  3.2 5.1 %copy-start.13 = (f32[400,2048]{1,0:T(8,128)S(1)}, f32[400,2048]{1,0:T(8,128)}, u32[]{:S(2)}) copy-start(f32[400,2048]{1,0:T(8,128)} %value.1) | copy-start | bytes 9830404
  4.2 37.6 %collective-permute-start.8 = (bf16[112,1664]{1,0:T(8,128)(2,1)S(1)}, bf16[112,1664]{1,0:T(8,128)(2,1)}, u32[]{:S(2)}, u32[]{:S(2)}) collective-permute-start(bf16[112,1664]{1,0:T(8,128)(2,1)S(1)} %shard_map.91), channel_id=1, source_target_pairs={{0,24},{4,28},{8,16},{12,20},{16,8},{20,12},{24,0},{28,4},{1,25},{... | collective-permute-start | bytes 1118216 | tf_op jit(solution)/shard_map/ppermute | solution.py:386
  5.9 36.0 %collective-permute-start.7 = (bf16[112,1664]{1,0:T(8,128)(2,1)S(1)}, bf16[112,1664]{1,0:T(8,128)(2,1)}, u32[]{:S(2)}, u32[]{:S(2)}) collective-permute-start(bf16[112,1664]{1,0:T(8,128)(2,1)S(1)} %shard_map.91), channel_id=1, source_target_pairs={{0,16},{4,20},{8,24},{12,28},{16,0},{20,4},{24,8},{28,12},{1,17},{... | collective-permute-start | bytes 1118216 | tf_op jit(solution)/shard_map/ppermute | solution.py:386
  8.2 5.2 %copy-start.7 = (bf16[512,512]{1,0:T(8,128)(2,1)}, bf16[512,512]{1,0:T(8,128)(2,1)S(1)}, u32[]{:S(2)}) copy-start(bf16[512,512]{1,0:T(8,128)(2,1)S(1)} %get-tuple-element.96.first.refs_8_) | copy-start | bytes 1572868
  8.3 8.6 %copy-start.30 = (s32[400]{0:T(512)S(1)}, s32[400]{0:T(512)}, u32[]{:S(2)}) copy-start(s32[400]{0:T(512)} %param.10) | copy-start | bytes 4804
  8.3 9.9 %copy-start.10 = (f32[128,128]{1,0:T(8,128)S(1)}, f32[128,128]{1,0:T(8,128)}, u32[]{:S(2)}) copy-start(f32[128,128]{1,0:T(8,128)} %trans.1) | copy-start | bytes 196612
  13.4 5.2 %copy-start.28 = (s16[400,512]{1,0:T(8,128)(2,1)}, s16[400,512]{1,0:T(8,128)(2,1)S(1)}, u32[]{:S(2)}) copy-start(s16[400,512]{1,0:T(8,128)(2,1)S(1)} %get-tuple-element.61.refs_0_) | copy-start | bytes 1228804
  13.4 12.6 %collective-permute-start = (s16[400,512]{1,0:T(8,128)(2,1)}, s16[400,512]{1,0:T(8,128)(2,1)S(1)}, u32[]{:S(2)}, u32[]{:S(2)}) collective-permute-start(s16[400,512]{1,0:T(8,128)(2,1)} %get-tuple-element.54), channel_id=1, source_target_pairs={{0,1},{1,0},{2,3},{3,2},{4,5},{5,4},{6,7},{7,6},{8,9},{9,8},{10,11... | collective-permute-start | bytes 1228808 | tf_op jit(solution)/shard_map/ppermute | solution.py:386
  15.0 20.3 %collective-permute-start.1 = (s16[400,512]{1,0:T(8,128)(2,1)}, s16[400,512]{1,0:T(8,128)(2,1)}, u32[]{:S(2)}, u32[]{:S(2)}) collective-permute-start(s16[400,512]{1,0:T(8,128)(2,1)} %get-tuple-element.55), channel_id=1, source_target_pairs={{0,2},{1,3},{2,0},{3,1},{4,6},{5,7},{6,4},{7,5},{8,10},{9,11},{10,... | collective-permute-start | bytes 1228808 | tf_op jit(solution)/shard_map/ppermute | solution.py:386
  16.6 18.8 %collective-permute-start.2 = (s16[400,512]{1,0:T(8,128)(2,1)}, s16[400,512]{1,0:T(8,128)(2,1)}, u32[]{:S(2)}, u32[]{:S(2)}) collective-permute-start(s16[400,512]{1,0:T(8,128)(2,1)} %get-tuple-element.56), channel_id=1, source_target_pairs={{0,3},{1,2},{2,1},{3,0},{4,7},{5,6},{6,5},{7,4},{8,11},{9,10},{10,... | collective-permute-start | bytes 1228808 | tf_op jit(solution)/shard_map/ppermute | solution.py:386
  18.6 16.7 %copy-start.14 = (bf16[512,512]{1,0:T(8,128)(2,1)}, bf16[512,512]{1,0:T(8,128)(2,1)S(1)}, u32[]{:S(2)}) copy-start(bf16[512,512]{1,0:T(8,128)(2,1)S(1)} %get-tuple-element.65.refs_4_.mix_a) | copy-start | bytes 1572868
  18.6 16.7 %copy-start.16 = (bf16[512,512]{1,0:T(8,128)(2,1)}, bf16[512,512]{1,0:T(8,128)(2,1)S(1)}, u32[]{:S(2)}) copy-start(bf16[512,512]{1,0:T(8,128)(2,1)S(1)} %get-tuple-element.66.refs_5_.mix_b) | copy-start | bytes 1572868
  19.2 16.1 %copy-start.9 = (f32[400,1]{1,0:T(8,128)S(1)}, f32[400,1]{1,0:T(8,128)}, u32[]{:S(2)}) copy-start(f32[400,1]{1,0:T(8,128)} %copy.10.refs_6_) | copy-start | bytes 4804
  19.2 16.1 %copy-start.29 = (s16[400,512]{1,0:T(8,128)(2,1)S(1)}, s16[400,512]{1,0:T(8,128)(2,1)}, u32[]{:S(2)}) copy-start(s16[400,512]{1,0:T(8,128)(2,1)} %copy-done.28) | copy-start | bytes 1228804
  26.8 15.1 %collective-permute-start.6 = (bf16[112,1664]{1,0:T(8,128)(2,1)S(1)}, bf16[112,1664]{1,0:T(8,128)(2,1)}, u32[]{:S(2)}, u32[]{:S(2)}) collective-permute-start(bf16[112,1664]{1,0:T(8,128)(2,1)S(1)} %shard_map.91), channel_id=1, source_target_pairs={{0,8},{4,12},{8,0},{12,4},{16,24},{20,28},{24,16},{28,20},{1,9},{5... | collective-permute-start | bytes 1118216 | tf_op jit(solution)/shard_map/ppermute | solution.py:386
  28.2 7.2 %copy-start.22 = (s16[400,512]{1,0:T(8,128)(2,1)S(1)}, s16[400,512]{1,0:T(8,128)(2,1)}, u32[]{:S(2)}) copy-start(s16[400,512]{1,0:T(8,128)(2,1)} %copy-done.21) | copy-start | bytes 1228804
  33.8 0.8 copy-start.24
  40.6 1.2 copy-start.5
  41.8 43.4 %all-to-all-start = ((bf16[4,416,512]{2,1,0:T(8,128)(2,1)}), bf16[4,416,512]{2,1,0:T(8,128)(2,1)}, u32[]{:S(2)}, u32[]{:S(2)}) async-start(bf16[4,416,512]{2,1,0:T(8,128)(2,1)} %copy-done.5), calls=%async_computation | async-start | bytes 3407872 | tf_op jit(solution)/shard_map/all_to_all | solution.py:409
  48.4 12.6 %collective-permute-start.3 = (bf16[400,512]{1,0:T(8,128)(2,1)}, bf16[400,512]{1,0:T(8,128)(2,1)S(1)}, u32[]{:S(2)}, u32[]{:S(2)}) collective-permute-start(bf16[400,512]{1,0:T(8,128)(2,1)} %copy-done.25), channel_id=1, source_target_pairs={{0,1},{1,0},{2,3},{3,2},{4,5},{5,4},{6,7},{7,6},{8,9},{9,8},{10,11... | collective-permute-start | bytes 1228808 | tf_op jit(solution)/shard_map/ppermute | solution.py:386
  49.9 15.8 %collective-permute-start.4 = (bf16[400,512]{1,0:T(8,128)(2,1)}, bf16[400,512]{1,0:T(8,128)(2,1)S(1)}, u32[]{:S(2)}, u32[]{:S(2)}) collective-permute-start(bf16[400,512]{1,0:T(8,128)(2,1)} %copy-done.24), channel_id=1, source_target_pairs={{0,2},{1,3},{2,0},{3,1},{4,6},{5,7},{6,4},{7,5},{8,10},{9,11},{10,... | collective-permute-start | bytes 1228808 | tf_op jit(solution)/shard_map/ppermute | solution.py:386
  51.5 16.3 %collective-permute-start.5 = (bf16[400,512]{1,0:T(8,128)(2,1)}, bf16[400,512]{1,0:T(8,128)(2,1)S(1)}, u32[]{:S(2)}, u32[]{:S(2)}) collective-permute-start(bf16[400,512]{1,0:T(8,128)(2,1)} %copy-done.23), channel_id=1, source_target_pairs={{0,3},{1,2},{2,1},{3,0},{4,7},{5,6},{6,5},{7,4},{8,11},{9,10},{10,... | collective-permute-start | bytes 1228808 | tf_op jit(solution)/shard_map/ppermute | solution.py:386
  67.8 10.5 %collective-permute-start.10 = (bf16[336,896]{1,0:T(8,128)(2,1)S(1)}, bf16[336,896]{1,0:T(8,128)(2,1)S(1)}, u32[]{:S(2)}, u32[]{:S(2)}) collective-permute-start(bf16[336,896]{1,0:T(8,128)(2,1)S(1)} %slice.6), channel_id=1, source_target_pairs={{0,1},{1,0},{2,3},{3,2},{4,5},{5,4},{6,7},{7,6},{8,9},{9,8},{10,11... | collective-permute-start | bytes 1806344 | tf_op jit(solution)/shard_map/ppermute | solution.py:386
  69.4 11.3 %collective-permute-start.11 = (bf16[336,768]{1,0:T(8,128)(2,1)S(1)}, bf16[336,768]{1,0:T(8,128)(2,1)S(1)}, u32[]{:S(2)}, u32[]{:S(2)}) collective-permute-start(bf16[336,768]{1,0:T(8,128)(2,1)S(1)} %slice.7), channel_id=1, source_target_pairs={{0,2},{1,3},{2,0},{3,1},{4,6},{5,7},{6,4},{7,5},{8,10},{9,11},{10,... | collective-permute-start | bytes 1548296 | tf_op jit(solution)/shard_map/ppermute | solution.py:386
  79.4 25.1 %collective-permute-start.12 = (bf16[672,896]{1,0:T(8,128)(2,1)}, bf16[672,896]{1,0:T(8,128)(2,1)}, u32[]{:S(2)}, u32[]{:S(2)}) collective-permute-start(bf16[672,896]{1,0:T(8,128)(2,1)} %pad_maximum_fusion.refs_3_), channel_id=1, source_target_pairs={{0,2},{1,3},{2,0},{3,1},{4,6},{5,7},{6,4},{7,5},{8,10},{9,11},{10,... | collective-permute-start | bytes 3612680 | tf_op jit(solution)/shard_map/ppermute | solution.py:386
  81.8 12.9 %collective-permute-start.17 = (bf16[672,768]{1,0:T(8,128)(2,1)}, bf16[672,768]{1,0:T(8,128)(2,1)}, u32[]{:S(2)}, u32[]{:S(2)}) collective-permute-start(bf16[672,768]{1,0:T(8,128)(2,1)} %pad_maximum_fusion.2.refs_5_), channel_id=1, source_target_pairs={{0,4},{4,0},{8,12},{12,8},{16,20},{20,16},{24,28},{28,24},{1,5},{5... | collective-permute-start | bytes 3096584 | tf_op jit(solution)/shard_map/ppermute | solution.py:386
  81.8 25.5 %collective-permute-start.13 = (bf16[672,768]{1,0:T(8,128)(2,1)}, bf16[672,768]{1,0:T(8,128)(2,1)}, u32[]{:S(2)}, u32[]{:S(2)}) collective-permute-start(bf16[672,768]{1,0:T(8,128)(2,1)} %pad_maximum_fusion.2.refs_5_), channel_id=1, source_target_pairs={{0,1},{1,0},{2,3},{3,2},{4,5},{5,4},{6,7},{7,6},{8,9},{9,8},{10,11... | collective-permute-start | bytes 3096584 | tf_op jit(solution)/shard_map/ppermute | solution.py:386
  84.1 1.2 copy-start.4
  85.3 43.8 %all-to-all-start.2 = ((bf16[4,400,512]{2,1,0:T(8,128)(2,1)}), bf16[4,400,512]{2,1,0:T(8,128)(2,1)}, u32[]{:S(2)}, u32[]{:S(2)}) async-start(bf16[4,400,512]{2,1,0:T(8,128)(2,1)} %copy-done.4), calls=%async_computation.2 | async-start | bytes 3276800 | tf_op jit(solution)/shard_map/all_to_all | solution.py:409
  90.5 21.8 %collective-permute-start.9 = (bf16[4,416,512]{2,1,0:T(8,128)(2,1)}, bf16[4,416,512]{2,1,0:T(8,128)(2,1)}, u32[]{:S(2)}, u32[]{:S(2)}) collective-permute-start(bf16[4,416,512]{2,1,0:T(8,128)(2,1)} %all-to-all-done.refs_0_), channel_id=1, source_target_pairs={{0,4},{4,0},{8,12},{12,8},{16,20},{20,16},{24,28},{28,24},{1,5},{5... | collective-permute-start | bytes 5111816 | tf_op jit(solution)/shard_map/ppermute | solution.py:386
  94.1 18.2 %copy-start.6 = (bf16[400,1664]{1,0:T(8,128)(2,1)}, bf16[400,1664]{1,0:T(8,128)(2,1)S(1)}, u32[]{:S(2)}) copy-start(bf16[400,1664]{1,0:T(8,128)(2,1)S(1)} %shard_map.92.refs_2_) | copy-start | bytes 3993604
  94.1 13.2 %collective-permute-start.14 = (bf16[400,1664]{1,0:T(8,128)(2,1)S(1)}, bf16[400,1664]{1,0:T(8,128)(2,1)S(1)}, u32[]{:S(2)}, u32[]{:S(2)}) collective-permute-start(bf16[400,1664]{1,0:T(8,128)(2,1)S(1)} %shard_map.92.refs_2_), channel_id=1, source_target_pairs={{0,4},{4,0},{8,12},{12,8},{16,20},{20,16},{24,28},{28,24},{1,5},{5... | collective-permute-start | bytes 3993608 | tf_op jit(solution)/shard_map/ppermute | solution.py:386
  94.7 12.6 %collective-permute-start.15 = (bf16[672,896]{1,0:T(8,128)(2,1)}, bf16[672,896]{1,0:T(8,128)(2,1)S(1)}, u32[]{:S(2)}, u32[]{:S(2)}) collective-permute-start(bf16[672,896]{1,0:T(8,128)(2,1)} %pad_maximum_fusion.refs_3_), channel_id=1, source_target_pairs={{0,4},{4,0},{8,12},{12,8},{16,20},{20,16},{24,28},{28,24},{1,5},{5... | collective-permute-start | bytes 3612680 | tf_op jit(solution)/shard_map/ppermute | solution.py:386
  104.5 5.6 %collective-permute-start.16 = (bf16[672,896]{1,0:T(8,128)(2,1)}, bf16[672,896]{1,0:T(8,128)(2,1)S(1)}, u32[]{:S(2)}, u32[]{:S(2)}) collective-permute-start(bf16[672,896]{1,0:T(8,128)(2,1)} %collective-permute-done.12.refs_4_), channel_id=1, source_target_pairs={{0,4},{4,0},{8,12},{12,8},{16,20},{20,16},{24,28},{28,24},{1,5},{5... | collective-permute-start | bytes 3612680 | tf_op jit(solution)/shard_map/ppermute | solution.py:386
  107.3 2.8 %collective-permute-start.18 = (bf16[672,768]{1,0:T(8,128)(2,1)}, bf16[672,768]{1,0:T(8,128)(2,1)S(1)}, u32[]{:S(2)}, u32[]{:S(2)}) collective-permute-start(bf16[672,768]{1,0:T(8,128)(2,1)} %collective-permute-done.13.refs_6_), channel_id=1, source_target_pairs={{0,4},{4,0},{8,12},{12,8},{16,20},{20,16},{24,28},{28,24},{1,5},{5... | collective-permute-start | bytes 3096584 | tf_op jit(solution)/shard_map/ppermute | solution.py:386
  107.3 2.8 %copy-start.32 = (bf16[672,896]{1,0:T(8,128)(2,1)}, bf16[672,896]{1,0:T(8,128)(2,1)S(1)}, u32[]{:S(2)}) copy-start(bf16[672,896]{1,0:T(8,128)(2,1)S(1)} %collective-permute-done.15.refs_8_) | copy-start | bytes 3612676
  107.3 1.1 copy-start.31
  110.1 1.0 copy-start.34
  111.2 1.1 copy-start.33
  129.1 41.9 %all-to-all-start.1 = ((bf16[4,416,512]{2,1,0:T(8,128)(2,1)}), bf16[4,416,512]{2,1,0:T(8,128)(2,1)}, u32[]{:S(2)}, u32[]{:S(2)}) async-start(bf16[4,416,512]{2,1,0:T(8,128)(2,1)} %get-tuple-element.72.totals), calls=%async_computation.1 | async-start | bytes 3407872 | tf_op jit(solution)/shard_map/all_to_all | solution.py:409
  134.2 1.5 copy-start.3
  135.7 5.5 %copy-start.12 = (s32[2]{0:T(128)S(1)}, s32[2]{0:T(128)}, u32[]{:S(2)}) copy-start(s32[2]{0:T(128)} %copy-done.11) | copy-start | bytes 28
  137.6 3.6 %collective-permute-start.22 = (bf16[4,400,512]{2,1,0:T(8,128)(2,1)S(1)}, bf16[4,400,512]{2,1,0:T(8,128)(2,1)S(1)}, u32[]{:S(2)}, u32[]{:S(2)}) collective-permute-start(bf16[4,400,512]{2,1,0:T(8,128)(2,1)S(1)} %shard_map.96.own), channel_id=1, source_target_pairs={{0,4},{4,0},{8,12},{12,8},{16,20},{20,16},{24,28},{28,24},{1,5},{5... | collective-permute-start | bytes 4915208 | tf_op jit(solution)/shard_map/ppermute | solution.py:386
  153.7 27.6 %copy-start.15 = (bf16[512,512]{1,0:T(8,128)(2,1)S(1)}, bf16[512,512]{1,0:T(8,128)(2,1)}, u32[]{:S(2)}) copy-start(bf16[512,512]{1,0:T(8,128)(2,1)} %copy-done.14) | copy-start | bytes 1572868
  153.7 26.2 %collective-permute-start.23 = (bf16[400,512]{1,0:T(8,128)(2,1)}, bf16[400,512]{1,0:T(8,128)(2,1)}, u32[]{:S(2)}, u32[]{:S(2)}) collective-permute-start(bf16[400,512]{1,0:T(8,128)(2,1)} %get-tuple-element.81), channel_id=1, source_target_pairs={{0,8},{4,12},{8,0},{12,4},{16,24},{20,28},{24,16},{28,20},{1,9},{5... | collective-permute-start | bytes 1228808 | tf_op jit(solution)/shard_map/ppermute | solution.py:386
  171.0 8.9 %copy-start.19 = (bf16[400,512]{1,0:T(8,128)(2,1)S(1)}, bf16[400,512]{1,0:T(8,128)(2,1)}, u32[]{:S(2)}) copy-start(bf16[400,512]{1,0:T(8,128)(2,1)} %copy-done.18) | copy-start | bytes 1228804
  171.0 10.2 %copy-start.17 = (bf16[512,512]{1,0:T(8,128)(2,1)S(1)}, bf16[512,512]{1,0:T(8,128)(2,1)}, u32[]{:S(2)}) copy-start(bf16[512,512]{1,0:T(8,128)(2,1)} %copy-done.16) | copy-start | bytes 1572868
  172.9 12.8 %collective-permute-start.19 = (bf16[416,512]{1,0:T(8,128)(2,1)S(1)}, bf16[416,512]{1,0:T(8,128)(2,1)S(1)}, u32[]{:S(2)}, u32[]{:S(2)}) collective-permute-start(bf16[416,512]{1,0:T(8,128)(2,1)S(1)} %get-tuple-element.74), channel_id=1, source_target_pairs={{0,1},{1,0},{2,3},{3,2},{4,5},{5,4},{6,7},{7,6},{8,9},{9,8},{10,11... | collective-permute-start | bytes 1277960 | tf_op jit(solution)/shard_map/ppermute | solution.py:386
  174.4 20.2 %collective-permute-start.20 = (bf16[416,512]{1,0:T(8,128)(2,1)S(1)}, bf16[416,512]{1,0:T(8,128)(2,1)S(1)}, u32[]{:S(2)}, u32[]{:S(2)}) collective-permute-start(bf16[416,512]{1,0:T(8,128)(2,1)S(1)} %get-tuple-element.75), channel_id=1, source_target_pairs={{0,2},{1,3},{2,0},{3,1},{4,6},{5,7},{6,4},{7,5},{8,10},{9,11},{10,... | collective-permute-start | bytes 1277960 | tf_op jit(solution)/shard_map/ppermute | solution.py:386
  175.2 19.9 %collective-permute-start.21 = (bf16[416,512]{1,0:T(8,128)(2,1)S(1)}, bf16[416,512]{1,0:T(8,128)(2,1)S(1)}, u32[]{:S(2)}, u32[]{:S(2)}) collective-permute-start(bf16[416,512]{1,0:T(8,128)(2,1)S(1)} %get-tuple-element.76), channel_id=1, source_target_pairs={{0,3},{1,2},{2,1},{3,0},{4,7},{5,6},{6,5},{7,4},{8,11},{9,10},{10,... | collective-permute-start | bytes 1277960 | tf_op jit(solution)/shard_map/ppermute | solution.py:386
  176.4 28.2 %collective-permute-start.27 = (bf16[400,512]{1,0:T(8,128)(2,1)}, bf16[400,512]{1,0:T(8,128)(2,1)S(1)}, u32[]{:S(2)}, u32[]{:S(2)}) collective-permute-start(bf16[400,512]{1,0:T(8,128)(2,1)} %copy-done.20), channel_id=1, source_target_pairs={{0,16},{4,20},{8,24},{12,28},{16,0},{20,4},{24,8},{28,12},{1,17},{... | collective-permute-start | bytes 1228808 | tf_op jit(solution)/shard_map/ppermute | solution.py:386
  179.9 34.2 %collective-permute-start.28 = (bf16[400,512]{1,0:T(8,128)(2,1)S(1)}, bf16[400,512]{1,0:T(8,128)(2,1)S(1)}, u32[]{:S(2)}, u32[]{:S(2)}) collective-permute-start(bf16[400,512]{1,0:T(8,128)(2,1)S(1)} %copy-done.19), channel_id=1, source_target_pairs={{0,24},{4,28},{8,16},{12,20},{16,8},{20,12},{24,0},{28,4},{1,25},{... | collective-permute-start | bytes 1228808 | tf_op jit(solution)/shard_map/ppermute | solution.py:386
  181.2 1.0 copy-start.27
  185.7 28.4 %collective-permute-start.24 = (s16[416,256]{1,0:T(8,128)(2,1)S(1)}, s16[416,256]{1,0:T(8,128)(2,1)S(1)}, u32[]{:S(2)}, u32[]{:S(2)}) collective-permute-start(s16[416,256]{1,0:T(8,128)(2,1)S(1)} %get-tuple-element.83), channel_id=1, source_target_pairs={{0,1},{1,0},{2,3},{3,2},{4,5},{5,4},{6,7},{7,6},{8,9},{9,8},{10,11... | collective-permute-start | bytes 638984 | tf_op jit(solution)/shard_map/ppermute | solution.py:386
  194.6 19.5 %collective-permute-start.25 = (s16[416,256]{1,0:T(8,128)(2,1)S(1)}, s16[416,256]{1,0:T(8,128)(2,1)S(1)}, u32[]{:S(2)}, u32[]{:S(2)}) collective-permute-start(s16[416,256]{1,0:T(8,128)(2,1)S(1)} %get-tuple-element.84), channel_id=1, source_target_pairs={{0,2},{1,3},{2,0},{3,1},{4,6},{5,7},{6,4},{7,5},{8,10},{9,11},{10,... | collective-permute-start | bytes 638984 | tf_op jit(solution)/shard_map/ppermute | solution.py:386
  195.1 19.0 %collective-permute-start.26 = (s16[416,256]{1,0:T(8,128)(2,1)S(1)}, s16[416,256]{1,0:T(8,128)(2,1)S(1)}, u32[]{:S(2)}, u32[]{:S(2)}) collective-permute-start(s16[416,256]{1,0:T(8,128)(2,1)S(1)} %get-tuple-element.85), channel_id=1, source_target_pairs={{0,3},{1,2},{2,1},{3,0},{4,7},{5,6},{6,5},{7,4},{8,11},{9,10},{10,... | collective-permute-start | bytes 638984 | tf_op jit(solution)/shard_map/ppermute | solution.py:386
  203.9 25.5 %copy-start.8 = (bf16[512,512]{1,0:T(8,128)(2,1)S(1)}, bf16[512,512]{1,0:T(8,128)(2,1)}, u32[]{:S(2)}) copy-start(bf16[512,512]{1,0:T(8,128)(2,1)} %copy-done.7) | copy-start | bytes 1572868
  216.3 8.2 %collective-permute-start.29 = (s16[416,256]{1,0:T(8,128)(2,1)S(1)}, s16[416,256]{1,0:T(8,128)(2,1)S(1)}, u32[]{:S(2)}, u32[]{:S(2)}) collective-permute-start(s16[416,256]{1,0:T(8,128)(2,1)S(1)} %get-tuple-element.93), channel_id=1, source_target_pairs={{0,1},{1,0},{2,3},{3,2},{4,5},{5,4},{6,7},{7,6},{8,9},{9,8},{10,11... | collective-permute-start | bytes 638984 | tf_op jit(solution)/shard_map/ppermute | solution.py:386
  217.9 11.5 %collective-permute-start.30 = (s16[416,256]{1,0:T(8,128)(2,1)S(1)}, s16[416,256]{1,0:T(8,128)(2,1)S(1)}, u32[]{:S(2)}, u32[]{:S(2)}) collective-permute-start(s16[416,256]{1,0:T(8,128)(2,1)S(1)} %get-tuple-element.94), channel_id=1, source_target_pairs={{0,2},{1,3},{2,0},{3,1},{4,6},{5,7},{6,4},{7,5},{8,10},{9,11},{10,... | collective-permute-start | bytes 638984 | tf_op jit(solution)/shard_map/ppermute | solution.py:386
  218.6 10.7 %collective-permute-start.31 = (s16[416,256]{1,0:T(8,128)(2,1)S(1)}, s16[416,256]{1,0:T(8,128)(2,1)S(1)}, u32[]{:S(2)}, u32[]{:S(2)}) collective-permute-start(s16[416,256]{1,0:T(8,128)(2,1)S(1)} %get-tuple-element.95), channel_id=1, source_target_pairs={{0,3},{1,2},{2,1},{3,0},{4,7},{5,6},{6,5},{7,4},{8,11},{9,10},{10,... | collective-permute-start | bytes 638984 | tf_op jit(solution)/shard_map/ppermute | solution.py:386
  229.3 6.8 %copy-start.1 = (s32[128,64]{0,1:T(8,128)S(1)}, s32[128,64]{0,1:T(8,128)}, u32[]{:S(2)}) copy-start(s32[128,64]{0,1:T(8,128)} %param.12) | copy-start | bytes 98308
  (6 other events, 4.5 us)

commit v4 on v3

--- a/solution.py
+++ b/solution.py
@@ -38,7 +38,7 @@
     return pl.ds(pl.multiple_of(start, LANES), size)
 
 
-def call(kernel, outs, ins, scratch=(), flops=0, specs=None, out_specs=None, vmem=48):
+def call(kernel, outs, ins, scratch=(), flops=0, specs=None, out_specs=None, vmem=24):
     moved = sum(math.prod(x.shape) * x.dtype.itemsize for x in list(ins) + list(outs))
     return pl.pallas_call(
         kernel,
@@ -210,14 +210,16 @@
 def total_kernel(plan, at, *refs):
     nz, rows, cut = plan.n_z, plan.rows, plan.cut
     own_weights, other_weights, refs = refs[0], refs[1], refs[2:]
-    both, (sent, scaled, near, weight, strip, full, sums, sem) = refs[:10], refs[10:]
+    both, (sent, scaled, near, given, weight, strip, full, sums, sems) = refs[:10], refs[10:]
     z, core, inc = at[0] // 2, at[0] % 2, at[1]
     left, right = pl.ds(0, cut), pl.ds(cut, plan.window - cut)
-    always, last = [], []
+    always = []
     for side in range(2):
         own, *parts = both[side * 5 : side * 5 + 5]
         first_row = lambda j: (2 * (z ^ j) + (core ^ side)) * rows
-        always.append((own, strip.at[pl.ds(pl.multiple_of(first_row(0), TILE), rows)]))
+        here = pl.ds(pl.multiple_of(first_row(0), TILE), rows)
+        for half, lanes in enumerate((left, right)):
+            always.append((half, None, own.at[:, lanes], strip.at[here, lanes]))
         places = ((0, 1), left), ((2, 3), left), ((0, 2), right), ((1, 3), right)
         for part, (steps, lanes) in zip(parts, places):
             for h, k in enumerate(steps):
@@ -227,41 +229,48 @@
                     start = first_row(j) + q * plan.stride
                     rest = plan.quarter - plan.stride
                     to = lambda r, size: strip.at[pl.ds(pl.multiple_of(r, TILE), size), lanes]
-                    always.append((part.at[pl.ds(base, plan.stride)], to(start, plan.stride)))
-                    extra = part.at[pl.ds(base + plan.stride, rest)]
-                    last.append((q == plan.n_inc - 1, extra, to(start + plan.stride, rest)))
-    copies = [pltpu.make_async_copy(a, b, sem) for a, b in always]
-    more = [(c, pltpu.make_async_copy(a, b, sem)) for c, a, b in last]
-    for c in copies:
+                    half = int(lanes is right)
+                    always.append((half, None, part.at[pl.ds(base, plan.stride)], to(start, plan.stride)))
+                    extra, when = part.at[pl.ds(base + plan.stride, rest)], q == plan.n_inc - 1
+                    always.append((half, when, extra, to(start + plan.stride, rest)))
+    loads = [pltpu.make_async_copy(own_weights, given.at[0], sems.at[0])]
+    loads.append(pltpu.make_async_copy(other_weights, given.at[1], sems.at[0]))
+    for c in loads:
         c.start()
-    for when, c in more:
-        pl.when(when)(c.start)
-
-    places = [(x, g) for x in (own_weights, other_weights) for g in range(nz)]
-    peaks = [x[g, rows : rows + 1, :].astype(F32) for x, g in places]
+    copies = [[], []]
+    for half, when, a, b in always:
+        copies[half].append((when, pltpu.make_async_copy(a, b, sems.at[1 + half])))
+    for when, c in copies[0] + copies[1]:
+        pl.when(when)(c.start) if when is not None else c.start()
+
+    for c in loads:
+        c.wait()
+    places = [(side, g) for side in range(2) for g in range(nz)]
+    peaks = [given[side, g, rows : rows + 1, :].astype(F32) for side, g in places]
     peak = functools.reduce(jnp.maximum, peaks)
-    for i, (x, g) in enumerate(places):
-        part = (x[g, :rows, :].astype(F32) * jnp.exp2(peaks[i] - peak)).astype(BF)
-        weight[county_rows(plan, at, g, i // nz), :] = part
-        if i < nz:
+    for (side, g), own_peak in zip(places, peaks):
+        part = (given[side, g, :rows, :].astype(F32) * jnp.exp2(own_peak - peak)).astype(BF)
+        weight[county_rows(plan, at, g, side), :] = part
+        if side == 0:
             scaled[g] = part
 
-    for c in copies:
-        c.wait()
-    for when, c in more:
-        pl.when(when)(c.wait)
-    blocks = plan.block_rows
-    for i in range(blocks):
-        for k in range(plan.window // LANES):
-            j = (i + k) % blocks
-            tile = strip[i * LANES : (i + 1) * LANES, k * LANES : (k + 1) * LANES]
-            full[i * LANES : (i + 1) * LANES, j * LANES : (j + 1) * LANES] = tile
-            if k:
-                full[j * LANES : (j + 1) * LANES, i * LANES : (i + 1) * LANES] = tile.T
+    blocks, cuts = plan.block_rows, (0, cut // LANES, plan.window // LANES)
+    for half in range(2):
+        for when, c in copies[half]:
+            pl.when(when)(c.wait) if when is not None else c.wait()
+        for i in range(blocks):
+            for k in range(cuts[half], cuts[half + 1]):
+                j = (i + k) % blocks
+                tile = strip[i * LANES : (i + 1) * LANES, k * LANES : (k + 1) * LANES]
+                full[i * LANES : (i + 1) * LANES, j * LANES : (j + 1) * LANES] = tile
+                if k:
+                    full[j * LANES : (j + 1) * LANES, i * LANES : (i + 1) * LANES] = tile.T
     copies = []
     for j in range(nz):
         out = near.at[pl.ds(j * rows, rows)]
-        copies.append(pltpu.make_async_copy(full.at[county_rows(plan, at, j, 0)], out, sem))
+        copies.append(
+            pltpu.make_async_copy(full.at[county_rows(plan, at, j, 0)], out, sems.at[0])
+        )
     for c in copies:
         c.start()
     def product(j, carry):
@@ -321,12 +330,11 @@
 
 def next_mass_kernel(plan, at, *refs):
     ni, w, rows = plan.n_inc, plan.wide, plan.rows
-    close, far, refs = refs[:ni], refs[ni : 2 * ni], refs[2 * ni :]
-    first, second, out, held, high, low = refs
+    ins, (first, second, out, held, high, low) = refs[:-6], refs[-6:]
     z, inc = at[0] // 2, at[1]
     for k in range(ni):
         j = 0
-        for part in (close[k], far[k]):
+        for part in ins[k::ni]:
             for i in range(part.shape[1] // LANES):
                 held[:, lanes_at((z ^ j) * LANES, LANES)] = part[
                     :, i * LANES : (i + 1) * LANES
@@ -483,16 +491,17 @@
         [S((nz, packed, w), BF), S((nz, rows, w), BF), S((half, n), BF)],
         [at, weights, others, *near],
         [
+            pltpu.VMEM((2, nz, packed, w), BF),
             pltpu.VMEM((n, w), BF),
             pltpu.VMEM((n, plan.window), BF),
             pltpu.VMEM((n, n), BF),
             pltpu.VMEM((nz, rows, w), F32),
-            pltpu.SemaphoreType.DMA,
+            pltpu.SemaphoreType.DMA((3,)),
         ],
         solve_flops,
-        specs=[SMEM, VMEM, VMEM] + [ANY] * len(near),
+        specs=[SMEM, ANY, ANY] + [ANY] * len(near),
         out_specs=[VMEM, VMEM, ANY],
-        vmem=60,
+        vmem=46,
     )
     sent = along_z(totals)
     (share,) = call(
@@ -511,9 +520,11 @@
         solve_flops,
         specs=[SMEM, VMEM, VMEM, ANY, VMEM],
     )
-    far, _ = after(movers[2:], sent)
     close = [movers[0], swap(movers[1], "loc", nl, 2)]
-    far = [swap(x, "loc", nl, 2 * (j + 2)) for j, x in enumerate(far)]
+    far = [swap(movers[2], "loc", nl, 4)]
+    for j in range(3, nz):
+        last, _ = after(movers[j], sent)
+        far.append(swap(last, "loc", nl, 2 * j))
 
     pack = lambda part, outs, kernel: call(
         bind(kernel),
@@ -533,13 +544,17 @@
         [pltpu.VMEM((ni, packed, w), BF)],
         2 * pass_flops,
     )
-    far, _ = after(far, (close, new_value))
-    far = pack(far, [S((packed, 2 * LANES), jnp.int16)] * ni, tail_kernel)
-    far = exchange(far, "inc", ni)
+    blocks, ready = close, (close, new_value)
+    for part in far:
+        part, _ = after(part, ready)
+        ready = pack([part], [S((packed, LANES), jnp.int16)] * ni, tail_kernel)
+        ready = exchange(ready, "inc", ni)
+        blocks = blocks + ready
+
     (new_mass,) = call(
         bind(next_mass_kernel),
         [S((rows, plan.columns), F32)],
-        [at, *close, *far, first, second],
+        [at, *blocks, first, second],
         [pltpu.VMEM((packed, w), jnp.int32)] + [pltpu.VMEM((ni, packed, w), BF)] * 2,
         4 * pass_flops,
     )

time: 237 us -> 232 us (0.979)
  waiting for transfers between devices: 93.2 us -> 78 us
  local copies, waits for them, and re-layouts: 17.2 us -> 25 us
  starting transfers between devices: 49.2 us -> 55.4 us
  Pallas kernels: 70.1 us -> 64.1 us
    ppermute x32 -> x35, waiting for transfers between devices: 75.8 us -> 64.9 us  [swap(): return lax.ppermute(x, axis, [(s, s ^ k) for s in range(n)]) if k else x]
    unnamed x70 -> x68, local copies, waits for them, and re-layouts: 15.9 us -> 23.7 us
    pallas_call x15 -> x16, Pallas kernels: 70.1 us -> 64.1 us  [call(): pl.pallas_call(kernel, out_shape=tuple(outs), in_specs=specs or [SMEM] +...]
    ppermute x32 -> x35, starting transfers between devices: 32.3 us -> 37.1 us  [swap(): return lax.ppermute(x, axis, [(s, s ^ k) for s in range(n)]) if k else x]
    all_to_all x3, waiting for transfers between devices: 17.4 us -> 13.1 us  [state_split(): along_z = lambda x: lax.all_to_all(x, 'loc', 0, 0, axis_index_groups=lines)]
  transfers between devices with their start and end apart: 35 -> 38, of which waited for: 17 -> 17; matrix products, arithmetic and copies ran while one was open for 3% -> 3% of each run, Pallas kernels for 25% -> 24%
where the time goes in v4:
time: 232 us; the launch traced here: 229 us
  waiting for transfers between devices  78 us (34%)
  Pallas kernels  64.1 us (28%)
  starting transfers between devices  55.4 us (24%)
  local copies, waits for them, and re-layouts  25 us (11%)
  other arithmetic  5.38 us (2%)
    ppermute x35, waiting for transfers between devices, swap(): return lax.ppermute(x, axis, [(s, s ^ k) for s in range(n)]) if k else x  64.9 us
    pallas_call x16, Pallas kernels, call(): pl.pallas_call(kernel, out_shape=tuple(outs), in_specs=specs or [SMEM] +...  64.1 us
    ppermute x35, starting transfers between devices, swap(): return lax.ppermute(x, axis, [(s, s ^ k) for s in range(n)]) if k else x  37.1 us
    unnamed x68, local copies, waits for them, and re-layouts  23.7 us
    all_to_all x3, starting transfers between devices, state_split(): along_z = lambda x: lax.all_to_all(x, 'loc', 0, 0, axis_index_groups=lines)  18.3 us
    all_to_all x3, waiting for transfers between devices, state_split(): along_z = lambda x: lax.all_to_all(x, 'loc', 0, 0, axis_index_groups=lines)  13.1 us
  transfers between devices with their start and end apart: 38, of which 17 were waited for; matrix products, arithmetic and copies ran while one was open for 3% of the time, Pallas kernels for 24%

profile of v4, /device:TPU:8, one launch (start us, length us, event | category | flops | bytes accessed | tf_op | source)
XLA Modules:
  0.0 229.1 jit_solution(17446048431222919147)
XLA Ops:
  0.7 2.4 %copy-done.2 = f32[400,3200]{1,0:T(8,128)S(1)} copy-done((f32[400,3200]{1,0:T(8,128)S(1)}, f32[400,3200]{1,0:T(8,128)}, u32[]{:S(2)}) %copy-start.2) | copy-done | bytes 5120024
  3.2 1.1 shard_map.91
  4.2 1.6 collective-permute-start.8
  5.9 1.1 collective-permute-start.7
  7.0 1.2 fusion.12
  8.3 5.2 %shard_map.87 = (s16[400,512]{1,0:T(8,128)(2,1)S(1)}, s16[400,512]{1,0:T(8,128)(2,1)}, s16[400,512]{1,0:T(8,128)(2,1)}, s16[400,512]{1,0:T(8,128)(2,1)}) custom-call(s32[2]{0:T(128)S(1)} %pad_add_fusion.at, f32[400,2048]{1,0:T(8,128)S(1)} %copy-done.13, bf16[512,512]{1,0:T(8,128)(2,1)S(1)} %get-tuple-element.102.first.refs_12_, ...), custom_call_target="tpu_custom_call" | custom-call | flops 3355443200 | bytes 5963784 | tf_op jit(solution)/shard_map/pallas_call | solution.py:43
  13.5 1.6 collective-permute-start
  15.1 1.5 collective-permute-start.1
  19.3 6.9 %collective-permute-done.refs_1_ = s16[400,512]{1,0:T(8,128)(2,1)} collective-permute-done((s16[400,512]{1,0:T(8,128)(2,1)}, s16[400,512]{1,0:T(8,128)(2,1)}, u32[]{:S(2)}, u32[]{:S(2)}) %collective-permute-start) | collective-permute-done | bytes 409632 | tf_op jit(solution)/shard_map/ppermute | solution.py:394
  26.2 1.4 collective-permute-start.6
  27.6 1.9 copy-done.14
  29.5 3.4 %shard_map.86 = (bf16[400,512]{1,0:T(8,128)(2,1)S(1)}, bf16[400,512]{1,0:T(8,128)(2,1)S(1)}, bf16[400,512]{1,0:T(8,128)(2,1)S(1)}, bf16[400,512]{1,0:T(8,128)(2,1)S(1)}) custom-call(s32[2]{0:T(128)S(1)} %pad_add_fusion.at, f32[400,2048]{1,0:T(8,128)S(1)} %copy-done.14, bf16[4,512,512]{2,1,0:T(8,128)(2,1)S(1)} %fusion.hit.refs_4_, ...), custom_call_target="tpu_custom_call" | custom-call | flops 2516582400 | bytes 7536648 | tf_op jit(solution)/shard_map/pallas_call | solution.py:43
  34.7 5.4 %shard_map.90 = bf16[4,416,512]{2,1,0:T(8,128)(2,1)S(1)} custom-call(s32[2]{0:T(128)S(1)} %pad_add_fusion.at, s16[400,512]{1,0:T(8,128)(2,1)S(1)} %copy-done.29, s16[400,512]{1,0:T(8,128)(2,1)} %collective-permute-done.refs_1_, s16[400,512]{1,0:T(8,128)(2,1)} %collective-permute-done.1.refs_2_, s16[400,512]{1,0:T(8,128)(2,1)} %collective-permute-done.2.refs_3_, ...), custom_call_target="tpu_custom_call" | custom-call | flops 2516582400 | bytes 4392520 | tf_op jit(solution)/shard_map/pallas_call | solution.py:43
  40.2 1.2 copy-done.7
  41.4 6.4 %all-to-all-start = ((bf16[4,416,512]{2,1,0:T(8,128)(2,1)}), bf16[4,416,512]{2,1,0:T(8,128)(2,1)}, u32[]{:S(2)}, u32[]{:S(2)}) async-start(bf16[4,416,512]{2,1,0:T(8,128)(2,1)} %copy-done.7), calls=%async_computation | async-start | bytes 3407872 | tf_op jit(solution)/shard_map/all_to_all | solution.py:417
  47.8 1.5 collective-permute-start.3
  49.2 1.5 collective-permute-start.4
  51.3 1.3 pad_maximum_fusion.1
  52.6 7.8 %collective-permute-done.3.refs_1_ = bf16[400,512]{1,0:T(8,128)(2,1)S(1)} collective-permute-done((bf16[400,512]{1,0:T(8,128)(2,1)}, bf16[400,512]{1,0:T(8,128)(2,1)S(1)}, u32[]{:S(2)}, u32[]{:S(2)}) %collective-permute-start.3) | collective-permute-done | bytes 409632 | tf_op jit(solution)/shard_map/ppermute | solution.py:394
  60.4 7.2 %collective-permute-done.4.refs_2_ = bf16[400,512]{1,0:T(8,128)(2,1)S(1)} collective-permute-done((bf16[400,512]{1,0:T(8,128)(2,1)}, bf16[400,512]{1,0:T(8,128)(2,1)S(1)}, u32[]{:S(2)}, u32[]{:S(2)}) %collective-permute-start.4) | collective-permute-done | bytes 409632 | tf_op jit(solution)/shard_map/ppermute | solution.py:394
  67.8 3.0 %collective-permute-start.11 = (bf16[336,768]{1,0:T(8,128)(2,1)S(1)}, bf16[336,768]{1,0:T(8,128)(2,1)S(1)}, u32[]{:S(2)}, u32[]{:S(2)}) collective-permute-start(bf16[336,768]{1,0:T(8,128)(2,1)S(1)} %slice.7), channel_id=1, source_target_pairs={{0,2},{1,3},{2,0},{3,1},{4,6},{5,7},{6,4},{7,5},{8,10},{9,11},{10,... | collective-permute-start | bytes 1548296 | tf_op jit(solution)/shard_map/ppermute | solution.py:394
  70.8 7.8 %collective-permute-done.10 = bf16[336,896]{1,0:T(8,128)(2,1)S(1)} collective-permute-done((bf16[336,896]{1,0:T(8,128)(2,1)S(1)}, bf16[336,896]{1,0:T(8,128)(2,1)S(1)}, u32[]{:S(2)}, u32[]{:S(2)}) %collective-permute-start.10) | collective-permute-done | bytes 602144 | tf_op jit(solution)/shard_map/ppermute | solution.py:394
  78.5 1.1 pad_maximum_fusion.refs_3_
  80.4 1.1 pad_maximum_fusion.2.refs_5_
  81.5 1.4 collective-permute-start.13
  83.8 1.2 copy-done.5
  85.0 5.4 %all-to-all-start.2 = ((bf16[4,400,512]{2,1,0:T(8,128)(2,1)}), bf16[4,400,512]{2,1,0:T(8,128)(2,1)}, u32[]{:S(2)}, u32[]{:S(2)}) async-start(bf16[4,400,512]{2,1,0:T(8,128)(2,1)} %copy-done.5), calls=%async_computation.2 | async-start | bytes 3276800 | tf_op jit(solution)/shard_map/all_to_all | solution.py:417
  90.4 2.4 %copy-done.3 = f32[400,3200]{1,0:T(8,128)S(1)} copy-done((f32[400,3200]{1,0:T(8,128)S(1)}, f32[400,3200]{1,0:T(8,128)}, u32[]{:S(2)}) %copy-start.3) | copy-done | bytes 5120024
  92.8 1.6 shard_map.92.refs_2_
  95.1 8.7 %collective-permute-done.12.refs_4_ = bf16[672,896]{1,0:T(8,128)(2,1)} collective-permute-done((bf16[672,896]{1,0:T(8,128)(2,1)}, bf16[672,896]{1,0:T(8,128)(2,1)}, u32[]{:S(2)}, u32[]{:S(2)}) %collective-permute-start.12) | collective-permute-done | bytes 1204256 | tf_op jit(solution)/shard_map/ppermute | solution.py:394
  103.8 3.3 %collective-permute-done.13.refs_6_ = bf16[672,768]{1,0:T(8,128)(2,1)} collective-permute-done((bf16[672,768]{1,0:T(8,128)(2,1)}, bf16[672,768]{1,0:T(8,128)(2,1)}, u32[]{:S(2)}, u32[]{:S(2)}) %collective-permute-start.13) | collective-permute-done | bytes 1032224 | tf_op jit(solution)/shard_map/ppermute | solution.py:394
  107.1 2.8 %collective-permute-done.18.refs_11_ = bf16[672,768]{1,0:T(8,128)(2,1)S(1)} collective-permute-done((bf16[672,768]{1,0:T(8,128)(2,1)}, bf16[672,768]{1,0:T(8,128)(2,1)S(1)}, u32[]{:S(2)}, u32[]{:S(2)}) %collective-permute-start.18) | collective-permute-done | bytes 1032224 | tf_op jit(solution)/shard_map/ppermute | solution.py:394
  110.9 1.2 copy-done.31
  112.1 15.0 %shard_map.93 = (bf16[4,416,512]{2,1,0:T(8,128)(2,1)}, bf16[4,400,512]{2,1,0:T(8,128)(2,1)}, bf16[1600,3200]{1,0:T(8,128)(2,1)}) custom-call(s32[2]{0:T(128)S(1)} %pad_add_fusion.at, bf16[4,416,512]{2,1,0:T(8,128)(2,1)} %all-to-all-done.refs_0_, bf16[4,416,512]{2,1,0:T(8,128)(2,1)} %copy-done.31, bf16[400,1664]{1,0:T(8,128)(2,1)} %copy-done.8, ...), custom_call_target="tpu_custom_call" | custom-call | flops 5242880000 | bytes 28598280 | tf_op jit(solution)/shard_map/pallas_call | solution.py:43
  127.1 6.6 %all-to-all-start.1 = ((bf16[4,416,512]{2,1,0:T(8,128)(2,1)}), bf16[4,416,512]{2,1,0:T(8,128)(2,1)}, u32[]{:S(2)}, u32[]{:S(2)}) async-start(bf16[4,416,512]{2,1,0:T(8,128)(2,1)} %get-tuple-element.75.totals), calls=%async_computation.1 | async-start | bytes 3407872 | tf_op jit(solution)/shard_map/all_to_all | solution.py:417
  133.6 1.5 copy-done.4
  135.1 2.0 shard_map.96.own
  137.2 3.5 %collective-permute-done.22.other = bf16[4,400,512]{2,1,0:T(8,128)(2,1)S(1)} collective-permute-done((bf16[4,400,512]{2,1,0:T(8,128)(2,1)S(1)}, bf16[4,400,512]{2,1,0:T(8,128)(2,1)S(1)}, u32[]{:S(2)}, u32[]{:S(2)}) %collective-permute-start.22) | collective-permute-done | bytes 1638432 | tf_op jit(solution)/shard_map/ppermute | solution.py:394
  140.7 3.9 %copy-done.24 = bf16[1600,3200]{1,0:T(8,128)(2,1)S(1)} copy-done((bf16[1600,3200]{1,0:T(8,128)(2,1)S(1)}, bf16[1600,3200]{1,0:T(8,128)(2,1)}, u32[]{:S(2)}) %copy-start.24) | copy-done | bytes 10240024
  144.7 9.7 %shard_map.97 = (bf16[400,512]{1,0:T(8,128)(2,1)S(1)}, bf16[400,512]{1,0:T(8,128)(2,1)}, bf16[400,512]{1,0:T(8,128)(2,1)S(1)}, bf16[400,512]{1,0:T(8,128)(2,1)S(1)}) custom-call(s32[2]{0:T(128)S(1)} %pad_add_fusion.at, bf16[4,400,512]{2,1,0:T(8,128)(2,1)S(1)} %shard_map.96.own, bf16[4,400,512]{2,1,0:T(8,128)(2,1)S(1)} %collective-permute-done.22.other, ...), custom_call_target="tpu_custom_call" | custom-call | flops 5242880000 | bytes 16793608 | tf_op jit(solution)/shard_map/pallas_call | solution.py:43
  156.7 13.1 %all-to-all-done.1.refs_0_ = bf16[4,416,512]{2,1,0:T(8,128)(2,1)} async-done(((bf16[4,416,512]{2,1,0:T(8,128)(2,1)}), bf16[4,416,512]{2,1,0:T(8,128)(2,1)}, u32[]{:S(2)}, u32[]{:S(2)}) %all-to-all-start.1) | async-done | bytes 1703968 | tf_op jit(solution)/shard_map/all_to_all | solution.py:417
  169.8 1.9 shard_map.94
  172.6 1.4 collective-permute-start.20
  174.0 1.3 collective-permute-start.21
  175.3 3.4 %collective-permute-start.27 = (bf16[400,512]{1,0:T(8,128)(2,1)}, bf16[400,512]{1,0:T(8,128)(2,1)S(1)}, u32[]{:S(2)}, u32[]{:S(2)}) collective-permute-start(bf16[400,512]{1,0:T(8,128)(2,1)} %copy-done.20), channel_id=1, source_target_pairs={{0,16},{4,20},{8,24},{12,28},{16,0},{20,4},{24,8},{28,12},{1,17},{... | collective-permute-start | bytes 1228808 | tf_op jit(solution)/shard_map/ppermute | solution.py:394
  178.8 1.5 collective-permute-start.31
  180.2 1.0 copy-done.16
  181.3 1.0 copy-done.18
  183.3 2.7 %shard_map.98 = (s16[416,256]{1,0:T(8,128)(2,1)S(1)}, s16[416,256]{1,0:T(8,128)(2,1)S(1)}, s16[416,256]{1,0:T(8,128)(2,1)S(1)}, s16[416,256]{1,0:T(8,128)(2,1)S(1)}) custom-call(s32[2]{0:T(128)S(1)} %pad_add_fusion.at, bf16[512,512]{1,0:T(8,128)(2,1)S(1)} %copy-done.16, bf16[512,512]{1,0:T(8,128)(2,1)S(1)} %copy-done.18, bf16[400,512]{1,0:T(8,128)(2,1)S(1)} %copy-done.26, ...), custom_call_target="tpu_custom_call" | custom-call | flops 838860800 | bytes 2719752 | tf_op jit(solution)/shard_map/pallas_call | solution.py:43
  186.9 2.9 %collective-permute-done.20.refs_2_ = bf16[416,512]{1,0:T(8,128)(2,1)S(1)} collective-permute-done((bf16[416,512]{1,0:T(8,128)(2,1)S(1)}, bf16[416,512]{1,0:T(8,128)(2,1)S(1)}, u32[]{:S(2)}, u32[]{:S(2)}) %collective-permute-start.20) | collective-permute-done | bytes 426016 | tf_op jit(solution)/shard_map/ppermute | solution.py:394
  189.8 2.3 collective-permute-start.25
  192.0 2.2 collective-permute-done.21.refs_3_
  194.2 1.3 collective-permute-start.26
  195.5 5.2 %shard_map.95 = f32[400,2048]{1,0:T(8,128)} custom-call(s32[2]{0:T(128)S(1)} %pad_add_fusion.at, bf16[416,512]{1,0:T(8,128)(2,1)S(1)} %get-tuple-element.76.refs_0_, bf16[416,512]{1,0:T(8,128)(2,1)S(1)} %collective-permute-done.19.refs_1_, bf16[416,512]{1,0:T(8,128)(2,1)S(1)} %collective-permute-done.20.refs_2_, ...), custom_call_target="tpu_custom_call" | custom-call | flops 1677721600 | bytes 10878984 | tf_op jit(solution)/shard_map/pallas_call | solution.py:43
  200.7 2.9 %collective-permute-done.27.refs_0_ = bf16[400,512]{1,0:T(8,128)(2,1)S(1)} collective-permute-done((bf16[400,512]{1,0:T(8,128)(2,1)}, bf16[400,512]{1,0:T(8,128)(2,1)S(1)}, u32[]{:S(2)}, u32[]{:S(2)}) %collective-permute-start.27) | collective-permute-done | bytes 409632 | tf_op jit(solution)/shard_map/ppermute | solution.py:394
  203.6 1.5 shard_map.99
  205.9 1.5 collective-permute-start.29
  207.3 1.3 collective-permute-start.30
  208.6 3.7 %collective-permute-done.31.refs_0_ = bf16[400,512]{1,0:T(8,128)(2,1)S(1)} collective-permute-done((bf16[400,512]{1,0:T(8,128)(2,1)}, bf16[400,512]{1,0:T(8,128)(2,1)S(1)}, u32[]{:S(2)}, u32[]{:S(2)}) %collective-permute-start.31) | collective-permute-done | bytes 409632 | tf_op jit(solution)/shard_map/ppermute | solution.py:394
  212.9 1.5 shard_map.100
  216.3 1.7 collective-permute-start.34
  218.0 2.0 collective-permute-done.32.refs_9_
  220.0 2.3 collective-permute-done.33.refs_10_
  222.3 6.8 %shard_map.101 = f32[400,2048]{1,0:T(8,128)} custom-call(s32[2]{0:T(128)S(1)} %pad_add_fusion.at, s16[416,256]{1,0:T(8,128)(2,1)S(1)} %get-tuple-element.85.refs_0_, s16[416,256]{1,0:T(8,128)(2,1)S(1)} %collective-permute-done.24.refs_1_, s16[416,256]{1,0:T(8,128)(2,1)S(1)} %collective-permute-done.25.refs_2_, ...), custom_call_target="tpu_custom_call" | custom-call | flops 3355443200 | bytes 6029320 | tf_op jit(solution)/shard_map/pallas_call | solution.py:43
  (119 shorter events, 16.9 us)
Async XLA Ops:
  0.6 16.5 %copy-start = (s32[128,64]{0,1:T(8,128)S(1)}, s32[128,64]{0,1:T(8,128)}, u32[]{:S(2)}) copy-start(s32[128,64]{0,1:T(8,128)} %param.12) | copy-start | bytes 98308
  0.7 2.5 %copy-start.2 = (f32[400,3200]{1,0:T(8,128)S(1)}, f32[400,3200]{1,0:T(8,128)}, u32[]{:S(2)}) copy-start(f32[400,3200]{1,0:T(8,128)} %cost.2) | copy-start | bytes 15360004
  3.2 5.1 %copy-start.13 = (f32[400,2048]{1,0:T(8,128)S(1)}, f32[400,2048]{1,0:T(8,128)}, u32[]{:S(2)}) copy-start(f32[400,2048]{1,0:T(8,128)} %value.1) | copy-start | bytes 9830404
  4.2 37.1 %collective-permute-start.8 = (bf16[112,1664]{1,0:T(8,128)(2,1)S(1)}, bf16[112,1664]{1,0:T(8,128)(2,1)}, u32[]{:S(2)}, u32[]{:S(2)}) collective-permute-start(bf16[112,1664]{1,0:T(8,128)(2,1)S(1)} %shard_map.91), channel_id=1, source_target_pairs={{0,24},{4,28},{8,16},{12,20},{16,8},{20,12},{24,0},{28,4},{1,25},{... | collective-permute-start | bytes 1118216 | tf_op jit(solution)/shard_map/ppermute | solution.py:394
  5.9 35.5 %collective-permute-start.7 = (bf16[112,1664]{1,0:T(8,128)(2,1)S(1)}, bf16[112,1664]{1,0:T(8,128)(2,1)}, u32[]{:S(2)}, u32[]{:S(2)}) collective-permute-start(bf16[112,1664]{1,0:T(8,128)(2,1)S(1)} %shard_map.91), channel_id=1, source_target_pairs={{0,16},{4,20},{8,24},{12,28},{16,0},{20,4},{24,8},{28,12},{1,17},{... | collective-permute-start | bytes 1118216 | tf_op jit(solution)/shard_map/ppermute | solution.py:394
  8.2 8.7 %copy-start.30 = (s32[400]{0:T(512)S(1)}, s32[400]{0:T(512)}, u32[]{:S(2)}) copy-start(s32[400]{0:T(512)} %param.10) | copy-start | bytes 4804
  8.3 10.0 %copy-start.12 = (f32[128,128]{1,0:T(8,128)S(1)}, f32[128,128]{1,0:T(8,128)}, u32[]{:S(2)}) copy-start(f32[128,128]{1,0:T(8,128)} %trans.1) | copy-start | bytes 196612
  13.5 5.2 %copy-start.28 = (s16[400,512]{1,0:T(8,128)(2,1)}, s16[400,512]{1,0:T(8,128)(2,1)S(1)}, u32[]{:S(2)}) copy-start(s16[400,512]{1,0:T(8,128)(2,1)S(1)} %get-tuple-element.64.refs_0_) | copy-start | bytes 1228804
  13.5 12.7 %collective-permute-start = (s16[400,512]{1,0:T(8,128)(2,1)}, s16[400,512]{1,0:T(8,128)(2,1)}, u32[]{:S(2)}, u32[]{:S(2)}) collective-permute-start(s16[400,512]{1,0:T(8,128)(2,1)} %get-tuple-element.57), channel_id=1, source_target_pairs={{0,1},{1,0},{2,3},{3,2},{4,5},{5,4},{6,7},{7,6},{8,9},{9,8},{10,11... | collective-permute-start | bytes 1228808 | tf_op jit(solution)/shard_map/ppermute | solution.py:394
  15.1 19.6 %collective-permute-start.1 = (s16[400,512]{1,0:T(8,128)(2,1)}, s16[400,512]{1,0:T(8,128)(2,1)}, u32[]{:S(2)}, u32[]{:S(2)}) collective-permute-start(s16[400,512]{1,0:T(8,128)(2,1)} %get-tuple-element.58), channel_id=1, source_target_pairs={{0,2},{1,3},{2,0},{3,1},{4,6},{5,7},{6,4},{7,5},{8,10},{9,11},{10,... | collective-permute-start | bytes 1228808 | tf_op jit(solution)/shard_map/ppermute | solution.py:394
  16.7 18.1 %collective-permute-start.2 = (s16[400,512]{1,0:T(8,128)(2,1)}, s16[400,512]{1,0:T(8,128)(2,1)}, u32[]{:S(2)}, u32[]{:S(2)}) collective-permute-start(s16[400,512]{1,0:T(8,128)(2,1)} %get-tuple-element.59), channel_id=1, source_target_pairs={{0,3},{1,2},{2,1},{3,0},{4,7},{5,6},{6,5},{7,4},{8,11},{9,10},{10,... | collective-permute-start | bytes 1228808 | tf_op jit(solution)/shard_map/ppermute | solution.py:394
  18.7 16.0 %copy-start.15 = (bf16[512,512]{1,0:T(8,128)(2,1)}, bf16[512,512]{1,0:T(8,128)(2,1)S(1)}, u32[]{:S(2)}) copy-start(bf16[512,512]{1,0:T(8,128)(2,1)S(1)} %get-tuple-element.68.refs_4_.mix_a) | copy-start | bytes 1572868
  18.7 16.0 %copy-start.17 = (bf16[512,512]{1,0:T(8,128)(2,1)}, bf16[512,512]{1,0:T(8,128)(2,1)S(1)}, u32[]{:S(2)}) copy-start(bf16[512,512]{1,0:T(8,128)(2,1)S(1)} %get-tuple-element.69.refs_5_.mix_b) | copy-start | bytes 1572868
  18.7 16.0 %copy-start.29 = (s16[400,512]{1,0:T(8,128)(2,1)S(1)}, s16[400,512]{1,0:T(8,128)(2,1)}, u32[]{:S(2)}) copy-start(s16[400,512]{1,0:T(8,128)(2,1)} %copy-done.28) | copy-start | bytes 1228804
  19.3 15.5 %copy-start.11 = (f32[400,1]{1,0:T(8,128)S(1)}, f32[400,1]{1,0:T(8,128)}, u32[]{:S(2)}) copy-start(f32[400,1]{1,0:T(8,128)} %copy.10.refs_6_) | copy-start | bytes 4804
  26.2 15.2 %collective-permute-start.6 = (bf16[112,1664]{1,0:T(8,128)(2,1)S(1)}, bf16[112,1664]{1,0:T(8,128)(2,1)}, u32[]{:S(2)}, u32[]{:S(2)}) collective-permute-start(bf16[112,1664]{1,0:T(8,128)(2,1)S(1)} %shard_map.91), channel_id=1, source_target_pairs={{0,8},{4,12},{8,0},{12,4},{16,24},{20,28},{24,16},{28,20},{1,9},{5... | collective-permute-start | bytes 1118216 | tf_op jit(solution)/shard_map/ppermute | solution.py:394
  27.6 1.9 copy-start.14
  34.5 5.7 %copy-start.21 = (bf16[400,512]{1,0:T(8,128)(2,1)}, bf16[400,512]{1,0:T(8,128)(2,1)S(1)}, u32[]{:S(2)}) copy-start(bf16[400,512]{1,0:T(8,128)(2,1)S(1)} %get-tuple-element.63) | copy-start | bytes 1228804
  34.5 5.7 %copy-start.22 = (bf16[400,512]{1,0:T(8,128)(2,1)}, bf16[400,512]{1,0:T(8,128)(2,1)S(1)}, u32[]{:S(2)}) copy-start(bf16[400,512]{1,0:T(8,128)(2,1)S(1)} %get-tuple-element.62) | copy-start | bytes 1228804
  40.2 1.2 copy-start.7
  41.4 43.6 %all-to-all-start = ((bf16[4,416,512]{2,1,0:T(8,128)(2,1)}), bf16[4,416,512]{2,1,0:T(8,128)(2,1)}, u32[]{:S(2)}, u32[]{:S(2)}) async-start(bf16[4,416,512]{2,1,0:T(8,128)(2,1)} %copy-done.7), calls=%async_computation | async-start | bytes 3407872 | tf_op jit(solution)/shard_map/all_to_all | solution.py:417
  47.8 12.6 %collective-permute-start.3 = (bf16[400,512]{1,0:T(8,128)(2,1)}, bf16[400,512]{1,0:T(8,128)(2,1)S(1)}, u32[]{:S(2)}, u32[]{:S(2)}) collective-permute-start(bf16[400,512]{1,0:T(8,128)(2,1)} %copy-done.23), channel_id=1, source_target_pairs={{0,1},{1,0},{2,3},{3,2},{4,5},{5,4},{6,7},{7,6},{8,9},{9,8},{10,11... | collective-permute-start | bytes 1228808 | tf_op jit(solution)/shard_map/ppermute | solution.py:394
  49.2 18.4 %collective-permute-start.4 = (bf16[400,512]{1,0:T(8,128)(2,1)}, bf16[400,512]{1,0:T(8,128)(2,1)S(1)}, u32[]{:S(2)}, u32[]{:S(2)}) collective-permute-start(bf16[400,512]{1,0:T(8,128)(2,1)} %copy-done.22), channel_id=1, source_target_pairs={{0,2},{1,3},{2,0},{3,1},{4,6},{5,7},{6,4},{7,5},{8,10},{9,11},{10,... | collective-permute-start | bytes 1228808 | tf_op jit(solution)/shard_map/ppermute | solution.py:394
  50.8 16.8 %collective-permute-start.5 = (bf16[400,512]{1,0:T(8,128)(2,1)}, bf16[400,512]{1,0:T(8,128)(2,1)S(1)}, u32[]{:S(2)}, u32[]{:S(2)}) collective-permute-start(bf16[400,512]{1,0:T(8,128)(2,1)} %copy-done.21), channel_id=1, source_target_pairs={{0,3},{1,2},{2,1},{3,0},{4,7},{5,6},{6,5},{7,4},{8,11},{9,10},{10,... | collective-permute-start | bytes 1228808 | tf_op jit(solution)/shard_map/ppermute | solution.py:394
  67.7 10.9 %collective-permute-start.10 = (bf16[336,896]{1,0:T(8,128)(2,1)S(1)}, bf16[336,896]{1,0:T(8,128)(2,1)S(1)}, u32[]{:S(2)}, u32[]{:S(2)}) collective-permute-start(bf16[336,896]{1,0:T(8,128)(2,1)S(1)} %slice.6), channel_id=1, source_target_pairs={{0,1},{1,0},{2,3},{3,2},{4,5},{5,4},{6,7},{7,6},{8,9},{9,8},{10,11... | collective-permute-start | bytes 1806344 | tf_op jit(solution)/shard_map/ppermute | solution.py:394
  67.8 15.2 %copy-start.10 = (bf16[400,512]{1,0:T(8,128)(2,1)S(1)}, bf16[400,512]{1,0:T(8,128)(2,1)}, u32[]{:S(2)}) copy-start(bf16[400,512]{1,0:T(8,128)(2,1)} %copy-done.9) | copy-start | bytes 1228804
  67.8 12.6 %collective-permute-start.11 = (bf16[336,768]{1,0:T(8,128)(2,1)S(1)}, bf16[336,768]{1,0:T(8,128)(2,1)S(1)}, u32[]{:S(2)}, u32[]{:S(2)}) collective-permute-start(bf16[336,768]{1,0:T(8,128)(2,1)S(1)} %slice.7), channel_id=1, source_target_pairs={{0,2},{1,3},{2,0},{3,1},{4,6},{5,7},{6,4},{7,5},{8,10},{9,11},{10,... | collective-permute-start | bytes 1548296 | tf_op jit(solution)/shard_map/ppermute | solution.py:394
  79.6 24.1 %collective-permute-start.12 = (bf16[672,896]{1,0:T(8,128)(2,1)}, bf16[672,896]{1,0:T(8,128)(2,1)}, u32[]{:S(2)}, u32[]{:S(2)}) collective-permute-start(bf16[672,896]{1,0:T(8,128)(2,1)} %pad_maximum_fusion.refs_3_), channel_id=1, source_target_pairs={{0,2},{1,3},{2,0},{3,1},{4,6},{5,7},{6,4},{7,5},{8,10},{9,11},{10,... | collective-permute-start | bytes 3612680 | tf_op jit(solution)/shard_map/ppermute | solution.py:394
  81.5 13.5 %collective-permute-start.17 = (bf16[672,768]{1,0:T(8,128)(2,1)}, bf16[672,768]{1,0:T(8,128)(2,1)}, u32[]{:S(2)}, u32[]{:S(2)}) collective-permute-start(bf16[672,768]{1,0:T(8,128)(2,1)} %pad_maximum_fusion.2.refs_5_), channel_id=1, source_target_pairs={{0,4},{4,0},{8,12},{12,8},{16,20},{20,16},{24,28},{28,24},{1,5},{5... | collective-permute-start | bytes 3096584 | tf_op jit(solution)/shard_map/ppermute | solution.py:394
  81.5 25.5 %collective-permute-start.13 = (bf16[672,768]{1,0:T(8,128)(2,1)}, bf16[672,768]{1,0:T(8,128)(2,1)}, u32[]{:S(2)}, u32[]{:S(2)}) collective-permute-start(bf16[672,768]{1,0:T(8,128)(2,1)} %pad_maximum_fusion.2.refs_5_), channel_id=1, source_target_pairs={{0,1},{1,0},{2,3},{3,2},{4,5},{5,4},{6,7},{7,6},{8,9},{9,8},{10,11... | collective-permute-start | bytes 3096584 | tf_op jit(solution)/shard_map/ppermute | solution.py:394
  83.8 1.2 copy-start.5
  85.0 42.1 %all-to-all-start.2 = ((bf16[4,400,512]{2,1,0:T(8,128)(2,1)}), bf16[4,400,512]{2,1,0:T(8,128)(2,1)}, u32[]{:S(2)}, u32[]{:S(2)}) async-start(bf16[4,400,512]{2,1,0:T(8,128)(2,1)} %copy-done.5), calls=%async_computation.2 | async-start | bytes 3276800 | tf_op jit(solution)/shard_map/all_to_all | solution.py:417
  90.4 19.5 %collective-permute-start.9 = (bf16[4,416,512]{2,1,0:T(8,128)(2,1)}, bf16[4,416,512]{2,1,0:T(8,128)(2,1)S(1)}, u32[]{:S(2)}, u32[]{:S(2)}) collective-permute-start(bf16[4,416,512]{2,1,0:T(8,128)(2,1)} %all-to-all-done.refs_0_), channel_id=1, source_target_pairs={{0,4},{4,0},{8,12},{12,8},{16,20},{20,16},{24,28},{28,24},{1,5},{5... | collective-permute-start | bytes 5111816 | tf_op jit(solution)/shard_map/ppermute | solution.py:394
  90.4 2.5 %copy-start.3 = (f32[400,3200]{1,0:T(8,128)S(1)}, f32[400,3200]{1,0:T(8,128)}, u32[]{:S(2)}) copy-start(f32[400,3200]{1,0:T(8,128)} %cost.2) | copy-start | bytes 15360004
  94.4 15.5 %copy-start.8 = (bf16[400,1664]{1,0:T(8,128)(2,1)}, bf16[400,1664]{1,0:T(8,128)(2,1)S(1)}, u32[]{:S(2)}) copy-start(bf16[400,1664]{1,0:T(8,128)(2,1)S(1)} %shard_map.92.refs_2_) | copy-start | bytes 3993604
  94.4 12.6 %collective-permute-start.14 = (bf16[400,1664]{1,0:T(8,128)(2,1)S(1)}, bf16[400,1664]{1,0:T(8,128)(2,1)S(1)}, u32[]{:S(2)}, u32[]{:S(2)}) collective-permute-start(bf16[400,1664]{1,0:T(8,128)(2,1)S(1)} %shard_map.92.refs_2_), channel_id=1, source_target_pairs={{0,4},{4,0},{8,12},{12,8},{16,20},{20,16},{24,28},{28,24},{1,5},{5... | collective-permute-start | bytes 3993608 | tf_op jit(solution)/shard_map/ppermute | solution.py:394
  95.0 12.0 %collective-permute-start.15 = (bf16[672,896]{1,0:T(8,128)(2,1)}, bf16[672,896]{1,0:T(8,128)(2,1)S(1)}, u32[]{:S(2)}, u32[]{:S(2)}) collective-permute-start(bf16[672,896]{1,0:T(8,128)(2,1)} %pad_maximum_fusion.refs_3_), channel_id=1, source_target_pairs={{0,4},{4,0},{8,12},{12,8},{16,20},{20,16},{24,28},{28,24},{1,5},{5... | collective-permute-start | bytes 3612680 | tf_op jit(solution)/shard_map/ppermute | solution.py:394
  103.8 6.1 %collective-permute-start.16 = (bf16[672,896]{1,0:T(8,128)(2,1)}, bf16[672,896]{1,0:T(8,128)(2,1)S(1)}, u32[]{:S(2)}, u32[]{:S(2)}) collective-permute-start(bf16[672,896]{1,0:T(8,128)(2,1)} %collective-permute-done.12.refs_4_), channel_id=1, source_target_pairs={{0,4},{4,0},{8,12},{12,8},{16,20},{20,16},{24,28},{28,24},{1,5},{5... | collective-permute-start | bytes 3612680 | tf_op jit(solution)/shard_map/ppermute | solution.py:394
  107.0 2.8 %collective-permute-start.18 = (bf16[672,768]{1,0:T(8,128)(2,1)}, bf16[672,768]{1,0:T(8,128)(2,1)S(1)}, u32[]{:S(2)}, u32[]{:S(2)}) collective-permute-start(bf16[672,768]{1,0:T(8,128)(2,1)} %collective-permute-done.13.refs_6_), channel_id=1, source_target_pairs={{0,4},{4,0},{8,12},{12,8},{16,20},{20,16},{24,28},{28,24},{1,5},{5... | collective-permute-start | bytes 3096584 | tf_op jit(solution)/shard_map/ppermute | solution.py:394
  107.0 2.9 %copy-start.32 = (bf16[400,1664]{1,0:T(8,128)(2,1)}, bf16[400,1664]{1,0:T(8,128)(2,1)S(1)}, u32[]{:S(2)}) copy-start(bf16[400,1664]{1,0:T(8,128)(2,1)S(1)} %collective-permute-done.14.refs_7_) | copy-start | bytes 3993604
  110.9 1.2 copy-start.31
  127.1 42.8 %all-to-all-start.1 = ((bf16[4,416,512]{2,1,0:T(8,128)(2,1)}), bf16[4,416,512]{2,1,0:T(8,128)(2,1)}, u32[]{:S(2)}, u32[]{:S(2)}) async-start(bf16[4,416,512]{2,1,0:T(8,128)(2,1)} %get-tuple-element.75.totals), calls=%async_computation.1 | async-start | bytes 3407872 | tf_op jit(solution)/shard_map/all_to_all | solution.py:417
  133.6 1.5 copy-start.4
  135.1 5.6 %copy-start.27 = (bf16[4,400,512]{2,1,0:T(8,128)(2,1)S(1)}, bf16[4,400,512]{2,1,0:T(8,128)(2,1)}, u32[]{:S(2)}) copy-start(bf16[4,400,512]{2,1,0:T(8,128)(2,1)} %get-tuple-element.82.scaled) | copy-start | bytes 4915204
  137.2 3.6 %collective-permute-start.22 = (bf16[4,400,512]{2,1,0:T(8,128)(2,1)S(1)}, bf16[4,400,512]{2,1,0:T(8,128)(2,1)S(1)}, u32[]{:S(2)}, u32[]{:S(2)}) collective-permute-start(bf16[4,400,512]{2,1,0:T(8,128)(2,1)S(1)} %shard_map.96.own), channel_id=1, source_target_pairs={{0,4},{4,0},{8,12},{12,8},{16,20},{20,16},{24,28},{28,24},{1,5},{5... | collective-permute-start | bytes 4915208 | tf_op jit(solution)/shard_map/ppermute | solution.py:394
  140.7 3.9 %copy-start.24 = (bf16[1600,3200]{1,0:T(8,128)(2,1)S(1)}, bf16[1600,3200]{1,0:T(8,128)(2,1)}, u32[]{:S(2)}) copy-start(bf16[1600,3200]{1,0:T(8,128)(2,1)} %get-tuple-element.81.near) | copy-start | bytes 30720004
  156.6 22.1 %collective-permute-start.23 = (bf16[400,512]{1,0:T(8,128)(2,1)}, bf16[400,512]{1,0:T(8,128)(2,1)}, u32[]{:S(2)}, u32[]{:S(2)}) collective-permute-start(bf16[400,512]{1,0:T(8,128)(2,1)} %get-tuple-element.84), channel_id=1, source_target_pairs={{0,8},{4,12},{8,0},{12,4},{16,24},{20,28},{24,16},{28,20},{1,9},{5... | collective-permute-start | bytes 1228808 | tf_op jit(solution)/shard_map/ppermute | solution.py:394
  169.8 25.7 %copy-start.6 = (f32[400,2048]{1,0:T(8,128)S(1)}, f32[400,2048]{1,0:T(8,128)}, u32[]{:S(2)}) copy-start(f32[400,2048]{1,0:T(8,128)} %refs_6_.1) | copy-start | bytes 9830404
  171.8 14.2 %collective-permute-start.19 = (bf16[416,512]{1,0:T(8,128)(2,1)S(1)}, bf16[416,512]{1,0:T(8,128)(2,1)S(1)}, u32[]{:S(2)}, u32[]{:S(2)}) collective-permute-start(bf16[416,512]{1,0:T(8,128)(2,1)S(1)} %get-tuple-element.77), channel_id=1, source_target_pairs={{0,1},{1,0},{2,3},{3,2},{4,5},{5,4},{6,7},{7,6},{8,9},{9,8},{10,11... | collective-permute-start | bytes 1277960 | tf_op jit(solution)/shard_map/ppermute | solution.py:394
  172.6 17.1 %collective-permute-start.20 = (bf16[416,512]{1,0:T(8,128)(2,1)S(1)}, bf16[416,512]{1,0:T(8,128)(2,1)S(1)}, u32[]{:S(2)}, u32[]{:S(2)}) collective-permute-start(bf16[416,512]{1,0:T(8,128)(2,1)S(1)} %get-tuple-element.78), channel_id=1, source_target_pairs={{0,2},{1,3},{2,0},{3,1},{4,6},{5,7},{6,4},{7,5},{8,10},{9,11},{10,... | collective-permute-start | bytes 1277960 | tf_op jit(solution)/shard_map/ppermute | solution.py:394
  174.0 20.2 %collective-permute-start.21 = (bf16[416,512]{1,0:T(8,128)(2,1)S(1)}, bf16[416,512]{1,0:T(8,128)(2,1)S(1)}, u32[]{:S(2)}, u32[]{:S(2)}) collective-permute-start(bf16[416,512]{1,0:T(8,128)(2,1)S(1)} %get-tuple-element.79), channel_id=1, source_target_pairs={{0,3},{1,2},{2,1},{3,0},{4,7},{5,6},{6,5},{7,4},{8,11},{9,10},{10,... | collective-permute-start | bytes 1277960 | tf_op jit(solution)/shard_map/ppermute | solution.py:394
  175.3 28.2 %collective-permute-start.27 = (bf16[400,512]{1,0:T(8,128)(2,1)}, bf16[400,512]{1,0:T(8,128)(2,1)S(1)}, u32[]{:S(2)}, u32[]{:S(2)}) collective-permute-start(bf16[400,512]{1,0:T(8,128)(2,1)} %copy-done.20), channel_id=1, source_target_pairs={{0,16},{4,20},{8,24},{12,28},{16,0},{20,4},{24,8},{28,12},{1,17},{... | collective-permute-start | bytes 1228808 | tf_op jit(solution)/shard_map/ppermute | solution.py:394
  178.8 33.5 %collective-permute-start.31 = (bf16[400,512]{1,0:T(8,128)(2,1)}, bf16[400,512]{1,0:T(8,128)(2,1)S(1)}, u32[]{:S(2)}, u32[]{:S(2)}) collective-permute-start(bf16[400,512]{1,0:T(8,128)(2,1)} %copy-done.19), channel_id=1, source_target_pairs={{0,24},{4,28},{8,16},{12,20},{16,8},{20,12},{24,0},{28,4},{1,25},{... | collective-permute-start | bytes 1228808 | tf_op jit(solution)/shard_map/ppermute | solution.py:394
  180.2 1.0 copy-start.16
  186.0 17.5 %collective-permute-start.24 = (s16[416,256]{1,0:T(8,128)(2,1)S(1)}, s16[416,256]{1,0:T(8,128)(2,1)S(1)}, u32[]{:S(2)}, u32[]{:S(2)}) collective-permute-start(s16[416,256]{1,0:T(8,128)(2,1)S(1)} %get-tuple-element.86), channel_id=1, source_target_pairs={{0,1},{1,0},{2,3},{3,2},{4,5},{5,4},{6,7},{7,6},{8,9},{9,8},{10,11... | collective-permute-start | bytes 638984 | tf_op jit(solution)/shard_map/ppermute | solution.py:394
  189.8 13.8 %collective-permute-start.25 = (s16[416,256]{1,0:T(8,128)(2,1)S(1)}, s16[416,256]{1,0:T(8,128)(2,1)S(1)}, u32[]{:S(2)}, u32[]{:S(2)}) collective-permute-start(s16[416,256]{1,0:T(8,128)(2,1)S(1)} %get-tuple-element.87), channel_id=1, source_target_pairs={{0,2},{1,3},{2,0},{3,1},{4,6},{5,7},{6,4},{7,5},{8,10},{9,11},{10,... | collective-permute-start | bytes 638984 | tf_op jit(solution)/shard_map/ppermute | solution.py:394
  194.2 9.3 %collective-permute-start.26 = (s16[416,256]{1,0:T(8,128)(2,1)S(1)}, s16[416,256]{1,0:T(8,128)(2,1)S(1)}, u32[]{:S(2)}, u32[]{:S(2)}) collective-permute-start(s16[416,256]{1,0:T(8,128)(2,1)S(1)} %get-tuple-element.88), channel_id=1, source_target_pairs={{0,3},{1,2},{2,1},{3,0},{4,7},{5,6},{6,5},{7,4},{8,11},{9,10},{10,... | collective-permute-start | bytes 638984 | tf_op jit(solution)/shard_map/ppermute | solution.py:394
  205.0 7.3 %collective-permute-start.28 = (s16[416,128]{1,0:T(8,128)(2,1)S(1)}, s16[416,128]{1,0:T(8,128)(2,1)S(1)}, u32[]{:S(2)}, u32[]{:S(2)}) collective-permute-start(s16[416,128]{1,0:T(8,128)(2,1)S(1)} %get-tuple-element.92), channel_id=1, source_target_pairs={{0,1},{1,0},{2,3},{3,2},{4,5},{5,4},{6,7},{7,6},{8,9},{9,8},{10,11... | collective-permute-start | bytes 319496 | tf_op jit(solution)/shard_map/ppermute | solution.py:394
  205.9 6.4 %collective-permute-start.29 = (s16[416,128]{1,0:T(8,128)(2,1)S(1)}, s16[416,128]{1,0:T(8,128)(2,1)S(1)}, u32[]{:S(2)}, u32[]{:S(2)}) collective-permute-start(s16[416,128]{1,0:T(8,128)(2,1)S(1)} %get-tuple-element.93), channel_id=1, source_target_pairs={{0,2},{1,3},{2,0},{3,1},{4,6},{5,7},{6,4},{7,5},{8,10},{9,11},{10,... | collective-permute-start | bytes 319496 | tf_op jit(solution)/shard_map/ppermute | solution.py:394
  207.3 5.6 %collective-permute-start.30 = (s16[416,128]{1,0:T(8,128)(2,1)S(1)}, s16[416,128]{1,0:T(8,128)(2,1)S(1)}, u32[]{:S(2)}, u32[]{:S(2)}) collective-permute-start(s16[416,128]{1,0:T(8,128)(2,1)S(1)} %get-tuple-element.94), channel_id=1, source_target_pairs={{0,3},{1,2},{2,1},{3,0},{4,7},{5,6},{6,5},{7,4},{8,11},{9,10},{10,... | collective-permute-start | bytes 319496 | tf_op jit(solution)/shard_map/ppermute | solution.py:394
  214.4 5.6 %collective-permute-start.32 = (s16[416,128]{1,0:T(8,128)(2,1)S(1)}, s16[416,128]{1,0:T(8,128)(2,1)S(1)}, u32[]{:S(2)}, u32[]{:S(2)}) collective-permute-start(s16[416,128]{1,0:T(8,128)(2,1)S(1)} %get-tuple-element.99), channel_id=1, source_target_pairs={{0,1},{1,0},{2,3},{3,2},{4,5},{5,4},{6,7},{7,6},{8,9},{9,8},{10,11... | collective-permute-start | bytes 319496 | tf_op jit(solution)/shard_map/ppermute | solution.py:394
  215.3 7.0 %collective-permute-start.33 = (s16[416,128]{1,0:T(8,128)(2,1)S(1)}, s16[416,128]{1,0:T(8,128)(2,1)S(1)}, u32[]{:S(2)}, u32[]{:S(2)}) collective-permute-start(s16[416,128]{1,0:T(8,128)(2,1)S(1)} %get-tuple-element.100), channel_id=1, source_target_pairs={{0,2},{1,3},{2,0},{3,1},{4,6},{5,7},{6,4},{7,5},{8,10},{9,11},{10,... | collective-permute-start | bytes 319496 | tf_op jit(solution)/shard_map/ppermute | solution.py:394
  216.3 6.0 %collective-permute-start.34 = (s16[416,128]{1,0:T(8,128)(2,1)S(1)}, s16[416,128]{1,0:T(8,128)(2,1)S(1)}, u32[]{:S(2)}, u32[]{:S(2)}) collective-permute-start(s16[416,128]{1,0:T(8,128)(2,1)S(1)} %get-tuple-element.101), channel_id=1, source_target_pairs={{0,3},{1,2},{2,1},{3,0},{4,7},{5,6},{6,5},{7,4},{8,11},{9,10},{10,... | collective-permute-start | bytes 319496 | tf_op jit(solution)/shard_map/ppermute | solution.py:394
  222.3 6.8 %copy-start.1 = (s32[128,64]{0,1:T(8,128)S(1)}, s32[128,64]{0,1:T(8,128)}, u32[]{:S(2)}) copy-start(s32[128,64]{0,1:T(8,128)} %param.12) | copy-start | bytes 98308
  (8 other events, 6.9 us)

commit v5 on v4

--- a/solution.py
+++ b/solution.py
@@ -330,7 +330,8 @@
 
 def next_mass_kernel(plan, at, *refs):
     ni, w, rows = plan.n_inc, plan.wide, plan.rows
-    ins, (first, second, out, held, high, low) = refs[:-6], refs[-6:]
+    ins, (first, second, out, held, high, low, done, sem) = refs[:-8], refs[-8:]
+    copies = []
     z, inc = at[0] // 2, at[1]
     for k in range(ni):
         j = 0
@@ -347,7 +348,11 @@
                 into[t, :, lanes_at((inc ^ k) * LANES, LANES)] = back[:, t * LANES : (t + 1) * LANES]
     for t in range(ni):
         code = dot_nt(high[t], first[...]) * 256.0 + dot_nt(low[t], first[...])
-        out[:, t * w : (t + 1) * w] = code[:rows, :] * jnp.exp2(code[rows : rows + 1, :] - 15.0)
+        done[t] = code[:rows, :] * jnp.exp2(code[rows : rows + 1, :] - 15.0)
+        copies.append(pltpu.make_async_copy(done.at[t], out.at[:, pl.ds(t * w, w)], sem))
+        copies[t].start()
+    for c in copies:
+        c.wait()
 
 
 def value_kernel(plan, at, *refs):
@@ -519,6 +524,7 @@
         ],
         solve_flops,
         specs=[SMEM, VMEM, VMEM, ANY, VMEM],
+        vmem=56,
     )
     close = [movers[0], swap(movers[1], "loc", nl, 2)]
     far = [swap(movers[2], "loc", nl, 4)]
@@ -555,8 +561,11 @@
         bind(next_mass_kernel),
         [S((rows, plan.columns), F32)],
         [at, *blocks, first, second],
-        [pltpu.VMEM((packed, w), jnp.int32)] + [pltpu.VMEM((ni, packed, w), BF)] * 2,
+        [pltpu.VMEM((packed, w), jnp.int32)]
+        + [pltpu.VMEM((ni, packed, w), BF)] * 2
+        + [pltpu.VMEM((ni, rows, w), F32), pltpu.SemaphoreType.DMA],
         4 * pass_flops,
+        out_specs=[ANY],
     )
     return new_value, new_mass
 

time: 232 us -> 232 us (level)
  local copies, waits for them, and re-layouts: 25 us -> 20 us
  waiting for transfers between devices: 78 us -> 82.3 us
    unnamed x68 -> x66, local copies, waits for them, and re-layouts: 23.7 us -> 18.7 us
    all_to_all x3, waiting for transfers between devices: 13.1 us -> 16.3 us  [state_split(): along_z = lambda x: lax.all_to_all(x, 'loc', 0, 0, axis_index_groups=lines)]
  transfers between devices with their start and end apart: 38 -> 38, of which waited for: 17 -> 17; matrix products, arithmetic and copies ran while one was open for 3% -> 3% of each run, Pallas kernels for 24% -> 25%
where the time goes in v5:
time: 232 us; the launch traced here: 228 us
  waiting for transfers between devices  82.3 us (35%)
  Pallas kernels  64.9 us (28%)
  starting transfers between devices  54.4 us (23%)
  local copies, waits for them, and re-layouts  20 us (9%)
  other arithmetic  5.4 us (2%)
    ppermute x35, waiting for transfers between devices, swap(): return lax.ppermute(x, axis, [(s, s ^ k) for s in range(n)]) if k else x  66 us
    pallas_call x16, Pallas kernels, call(): pl.pallas_call(kernel, out_shape=tuple(outs), in_specs=specs or [SMEM] +...  64.9 us
    ppermute x35, starting transfers between devices, swap(): return lax.ppermute(x, axis, [(s, s ^ k) for s in range(n)]) if k else x  36.1 us
    unnamed x66, local copies, waits for them, and re-layouts  18.7 us
    all_to_all x3, starting transfers between devices, state_split(): along_z = lambda x: lax.all_to_all(x, 'loc', 0, 0, axis_index_groups=lines)  18.3 us
    all_to_all x3, waiting for transfers between devices, state_split(): along_z = lambda x: lax.all_to_all(x, 'loc', 0, 0, axis_index_groups=lines)  16.3 us
  transfers between devices with their start and end apart: 38, of which 17 were waited for; matrix products, arithmetic and copies ran while one was open for 3% of the time, Pallas kernels for 25%

profile of v5, /device:TPU:8, one launch (start us, length us, event | category | flops | bytes accessed | tf_op | source)
XLA Modules:
  0.0 228.3 jit_solution(12297915801397805364)
XLA Ops:
  0.7 2.4 %copy-done.2 = f32[400,3200]{1,0:T(8,128)S(1)} copy-done((f32[400,3200]{1,0:T(8,128)S(1)}, f32[400,3200]{1,0:T(8,128)}, u32[]{:S(2)}) %copy-start.2) | copy-done | bytes 5120024
  3.2 1.1 shard_map.91
  4.2 1.6 collective-permute-start.8
  5.9 1.1 collective-permute-start.7
  7.0 1.2 fusion.12
  8.3 5.2 %shard_map.87 = (s16[400,512]{1,0:T(8,128)(2,1)S(1)}, s16[400,512]{1,0:T(8,128)(2,1)}, s16[400,512]{1,0:T(8,128)(2,1)}, s16[400,512]{1,0:T(8,128)(2,1)}) custom-call(s32[2]{0:T(128)S(1)} %pad_add_fusion.at, f32[400,2048]{1,0:T(8,128)S(1)} %copy-done.16, bf16[512,512]{1,0:T(8,128)(2,1)S(1)} %get-tuple-element.102.first.refs_12_, ...), custom_call_target="tpu_custom_call" | custom-call | flops 3355443200 | bytes 5963784 | tf_op jit(solution)/shard_map/pallas_call | solution.py:43
  13.4 1.6 collective-permute-start
  15.1 1.5 collective-permute-start.1
  19.2 6.9 %collective-permute-done.refs_1_ = s16[400,512]{1,0:T(8,128)(2,1)} collective-permute-done((s16[400,512]{1,0:T(8,128)(2,1)}, s16[400,512]{1,0:T(8,128)(2,1)}, u32[]{:S(2)}, u32[]{:S(2)}) %collective-permute-start) | collective-permute-done | bytes 409632 | tf_op jit(solution)/shard_map/ppermute | solution.py:399
  26.1 1.4 collective-permute-start.6
  27.5 1.9 copy-done.17
  29.5 3.4 %shard_map.86 = (bf16[400,512]{1,0:T(8,128)(2,1)S(1)}, bf16[400,512]{1,0:T(8,128)(2,1)S(1)}, bf16[400,512]{1,0:T(8,128)(2,1)S(1)}, bf16[400,512]{1,0:T(8,128)(2,1)S(1)}) custom-call(s32[2]{0:T(128)S(1)} %pad_add_fusion.at, f32[400,2048]{1,0:T(8,128)S(1)} %copy-done.17, bf16[4,512,512]{2,1,0:T(8,128)(2,1)S(1)} %fusion.hit.refs_4_, ...), custom_call_target="tpu_custom_call" | custom-call | flops 2516582400 | bytes 7536648 | tf_op jit(solution)/shard_map/pallas_call | solution.py:43
  34.7 5.4 %shard_map.90 = bf16[4,416,512]{2,1,0:T(8,128)(2,1)S(1)} custom-call(s32[2]{0:T(128)S(1)} %pad_add_fusion.at, s16[400,512]{1,0:T(8,128)(2,1)S(1)} %copy-done.27, s16[400,512]{1,0:T(8,128)(2,1)} %collective-permute-done.refs_1_, s16[400,512]{1,0:T(8,128)(2,1)} %collective-permute-done.1.refs_2_, s16[400,512]{1,0:T(8,128)(2,1)} %collective-permute-done.2.refs_3_, ...), custom_call_target="tpu_custom_call" | custom-call | flops 2516582400 | bytes 4392520 | tf_op jit(solution)/shard_map/pallas_call | solution.py:43
  40.1 1.2 copy-done.7
  41.3 6.4 %all-to-all-start = ((bf16[4,416,512]{2,1,0:T(8,128)(2,1)}), bf16[4,416,512]{2,1,0:T(8,128)(2,1)}, u32[]{:S(2)}, u32[]{:S(2)}) async-start(bf16[4,416,512]{2,1,0:T(8,128)(2,1)} %copy-done.7), calls=%async_computation | async-start | bytes 3407872 | tf_op jit(solution)/shard_map/all_to_all | solution.py:422
  47.7 1.5 collective-permute-start.3
  49.2 1.5 collective-permute-start.4
  51.2 1.3 pad_maximum_fusion.1
  52.5 7.8 %collective-permute-done.3.refs_1_ = bf16[400,512]{1,0:T(8,128)(2,1)S(1)} collective-permute-done((bf16[400,512]{1,0:T(8,128)(2,1)}, bf16[400,512]{1,0:T(8,128)(2,1)S(1)}, u32[]{:S(2)}, u32[]{:S(2)}) %collective-permute-start.3) | collective-permute-done | bytes 409632 | tf_op jit(solution)/shard_map/ppermute | solution.py:399
  60.3 7.3 %collective-permute-done.4.refs_2_ = bf16[400,512]{1,0:T(8,128)(2,1)S(1)} collective-permute-done((bf16[400,512]{1,0:T(8,128)(2,1)}, bf16[400,512]{1,0:T(8,128)(2,1)S(1)}, u32[]{:S(2)}, u32[]{:S(2)}) %collective-permute-start.4) | collective-permute-done | bytes 409632 | tf_op jit(solution)/shard_map/ppermute | solution.py:399
  67.8 2.9 %collective-permute-start.11 = (bf16[336,768]{1,0:T(8,128)(2,1)S(1)}, bf16[336,768]{1,0:T(8,128)(2,1)S(1)}, u32[]{:S(2)}, u32[]{:S(2)}) collective-permute-start(bf16[336,768]{1,0:T(8,128)(2,1)S(1)} %slice.7), channel_id=1, source_target_pairs={{0,2},{1,3},{2,0},{3,1},{4,6},{5,7},{6,4},{7,5},{8,10},{9,11},{10,... | collective-permute-start | bytes 1548296 | tf_op jit(solution)/shard_map/ppermute | solution.py:399
  70.7 7.8 %collective-permute-done.10 = bf16[336,896]{1,0:T(8,128)(2,1)S(1)} collective-permute-done((bf16[336,896]{1,0:T(8,128)(2,1)S(1)}, bf16[336,896]{1,0:T(8,128)(2,1)S(1)}, u32[]{:S(2)}, u32[]{:S(2)}) %collective-permute-start.10) | collective-permute-done | bytes 602144 | tf_op jit(solution)/shard_map/ppermute | solution.py:399
  78.5 1.1 pad_maximum_fusion.refs_3_
  80.4 1.1 pad_maximum_fusion.2.refs_5_
  81.5 1.4 collective-permute-start.13
  83.7 1.2 copy-done.5
  84.9 5.4 %all-to-all-start.2 = ((bf16[4,400,512]{2,1,0:T(8,128)(2,1)}), bf16[4,400,512]{2,1,0:T(8,128)(2,1)}, u32[]{:S(2)}, u32[]{:S(2)}) async-start(bf16[4,400,512]{2,1,0:T(8,128)(2,1)} %copy-done.5), calls=%async_computation.2 | async-start | bytes 3276800 | tf_op jit(solution)/shard_map/all_to_all | solution.py:422
  90.3 2.4 %copy-done.3 = f32[400,3200]{1,0:T(8,128)S(1)} copy-done((f32[400,3200]{1,0:T(8,128)S(1)}, f32[400,3200]{1,0:T(8,128)}, u32[]{:S(2)}) %copy-start.3) | copy-done | bytes 5120024
  92.8 1.6 shard_map.92.refs_2_
  95.0 8.7 %collective-permute-done.12.refs_4_ = bf16[672,896]{1,0:T(8,128)(2,1)} collective-permute-done((bf16[672,896]{1,0:T(8,128)(2,1)}, bf16[672,896]{1,0:T(8,128)(2,1)}, u32[]{:S(2)}, u32[]{:S(2)}) %collective-permute-start.12) | collective-permute-done | bytes 1204256 | tf_op jit(solution)/shard_map/ppermute | solution.py:399
  103.7 3.3 %collective-permute-done.13.refs_6_ = bf16[672,768]{1,0:T(8,128)(2,1)} collective-permute-done((bf16[672,768]{1,0:T(8,128)(2,1)}, bf16[672,768]{1,0:T(8,128)(2,1)}, u32[]{:S(2)}, u32[]{:S(2)}) %collective-permute-start.13) | collective-permute-done | bytes 1032224 | tf_op jit(solution)/shard_map/ppermute | solution.py:399
  107.1 2.8 %collective-permute-done.18.refs_11_ = bf16[672,768]{1,0:T(8,128)(2,1)S(1)} collective-permute-done((bf16[672,768]{1,0:T(8,128)(2,1)}, bf16[672,768]{1,0:T(8,128)(2,1)S(1)}, u32[]{:S(2)}, u32[]{:S(2)}) %collective-permute-start.18) | collective-permute-done | bytes 1032224 | tf_op jit(solution)/shard_map/ppermute | solution.py:399
  110.9 1.2 copy-done.29
  112.1 14.9 %shard_map.93 = (bf16[4,416,512]{2,1,0:T(8,128)(2,1)}, bf16[4,400,512]{2,1,0:T(8,128)(2,1)}, bf16[1600,3200]{1,0:T(8,128)(2,1)}) custom-call(s32[2]{0:T(128)S(1)} %pad_add_fusion.at, bf16[4,416,512]{2,1,0:T(8,128)(2,1)} %all-to-all-done.refs_0_, bf16[4,416,512]{2,1,0:T(8,128)(2,1)} %copy-done.29, bf16[400,1664]{1,0:T(8,128)(2,1)} %copy-done.9, ...), custom_call_target="tpu_custom_call" | custom-call | flops 5242880000 | bytes 28598280 | tf_op jit(solution)/shard_map/pallas_call | solution.py:43
  127.1 6.5 %all-to-all-start.1 = ((bf16[4,416,512]{2,1,0:T(8,128)(2,1)}), bf16[4,416,512]{2,1,0:T(8,128)(2,1)}, u32[]{:S(2)}, u32[]{:S(2)}) async-start(bf16[4,416,512]{2,1,0:T(8,128)(2,1)} %get-tuple-element.75.totals), calls=%async_computation.1 | async-start | bytes 3407872 | tf_op jit(solution)/shard_map/all_to_all | solution.py:422
  133.6 1.5 copy-done.4
  135.1 1.9 shard_map.96.own
  137.1 3.5 %collective-permute-done.22.other = bf16[4,400,512]{2,1,0:T(8,128)(2,1)S(1)} collective-permute-done((bf16[4,400,512]{2,1,0:T(8,128)(2,1)S(1)}, bf16[4,400,512]{2,1,0:T(8,128)(2,1)S(1)}, u32[]{:S(2)}, u32[]{:S(2)}) %collective-permute-start.22) | collective-permute-done | bytes 1638432 | tf_op jit(solution)/shard_map/ppermute | solution.py:399
  140.6 1.2 copy-done.30
  141.8 11.5 %shard_map.97 = (bf16[400,512]{1,0:T(8,128)(2,1)}, bf16[400,512]{1,0:T(8,128)(2,1)}, bf16[400,512]{1,0:T(8,128)(2,1)}, bf16[400,512]{1,0:T(8,128)(2,1)}) custom-call(s32[2]{0:T(128)} %copy-done.14, bf16[4,400,512]{2,1,0:T(8,128)(2,1)} %copy-done.8, bf16[4,400,512]{2,1,0:T(8,128)(2,1)} %copy-done.30, bf16[1600,3200]{1,0:T(8,128)(2,1)} %get-tuple-element.81.near, ...), custom_call_target="tpu_custom_call" | custom-call | flops 5242880000 | bytes 16793608 | tf_op jit(solution)/shard_map/pallas_call | solution.py:43
  153.4 16.3 %all-to-all-done.1.refs_0_ = bf16[4,416,512]{2,1,0:T(8,128)(2,1)} async-done(((bf16[4,416,512]{2,1,0:T(8,128)(2,1)}), bf16[4,416,512]{2,1,0:T(8,128)(2,1)}, u32[]{:S(2)}, u32[]{:S(2)}) %all-to-all-start.1) | async-done | bytes 1703968 | tf_op jit(solution)/shard_map/all_to_all | solution.py:422
  169.8 1.9 shard_map.94
  172.6 1.2 collective-permute-start.20
  173.8 1.5 collective-permute-start.21
  175.2 3.4 %collective-permute-start.27 = (bf16[400,512]{1,0:T(8,128)(2,1)}, bf16[400,512]{1,0:T(8,128)(2,1)S(1)}, u32[]{:S(2)}, u32[]{:S(2)}) collective-permute-start(bf16[400,512]{1,0:T(8,128)(2,1)} %get-tuple-element.89), channel_id=1, source_target_pairs={{0,16},{4,20},{8,24},{12,28},{16,0},{20,4},{24,8},{28,12},{1,17},{... | collective-permute-start | bytes 1228808 | tf_op jit(solution)/shard_map/ppermute | solution.py:399
  178.7 1.5 collective-permute-start.31
  180.2 1.0 copy-done.19
  183.2 2.7 %shard_map.98 = (s16[416,256]{1,0:T(8,128)(2,1)S(1)}, s16[416,256]{1,0:T(8,128)(2,1)S(1)}, s16[416,256]{1,0:T(8,128)(2,1)S(1)}, s16[416,256]{1,0:T(8,128)(2,1)S(1)}) custom-call(s32[2]{0:T(128)S(1)} %copy-done.15, bf16[512,512]{1,0:T(8,128)(2,1)S(1)} %copy-done.19, bf16[512,512]{1,0:T(8,128)(2,1)S(1)} %copy-done.21, bf16[400,512]{1,0:T(8,128)(2,1)S(1)} %copy-done.25, ...), custom_call_target="tpu_custom_call" | custom-call | flops 838860800 | bytes 2719752 | tf_op jit(solution)/shard_map/pallas_call | solution.py:43
  186.8 2.6 %collective-permute-done.20.refs_2_ = bf16[416,512]{1,0:T(8,128)(2,1)S(1)} collective-permute-done((bf16[416,512]{1,0:T(8,128)(2,1)S(1)}, bf16[416,512]{1,0:T(8,128)(2,1)S(1)}, u32[]{:S(2)}, u32[]{:S(2)}) %collective-permute-start.20) | collective-permute-done | bytes 426016 | tf_op jit(solution)/shard_map/ppermute | solution.py:399
  189.4 1.4 collective-permute-start.25
  190.8 3.4 %collective-permute-done.21.refs_3_ = bf16[416,512]{1,0:T(8,128)(2,1)S(1)} collective-permute-done((bf16[416,512]{1,0:T(8,128)(2,1)S(1)}, bf16[416,512]{1,0:T(8,128)(2,1)S(1)}, u32[]{:S(2)}, u32[]{:S(2)}) %collective-permute-start.21) | collective-permute-done | bytes 426016 | tf_op jit(solution)/shard_map/ppermute | solution.py:399
  194.2 1.2 collective-permute-start.26
  195.5 5.2 %shard_map.95 = f32[400,2048]{1,0:T(8,128)} custom-call(s32[2]{0:T(128)S(1)} %copy-done.15, bf16[416,512]{1,0:T(8,128)(2,1)S(1)} %get-tuple-element.76.refs_0_, bf16[416,512]{1,0:T(8,128)(2,1)S(1)} %collective-permute-done.19.refs_1_, bf16[416,512]{1,0:T(8,128)(2,1)S(1)} %collective-permute-done.20.refs_2_, ...), custom_call_target="tpu_custom_call" | custom-call | flops 1677721600 | bytes 10878984 | tf_op jit(solution)/shard_map/pallas_call | solution.py:43
  200.6 2.8 %collective-permute-done.27.refs_0_ = bf16[400,512]{1,0:T(8,128)(2,1)S(1)} collective-permute-done((bf16[400,512]{1,0:T(8,128)(2,1)}, bf16[400,512]{1,0:T(8,128)(2,1)S(1)}, u32[]{:S(2)}, u32[]{:S(2)}) %collective-permute-start.27) | collective-permute-done | bytes 409632 | tf_op jit(solution)/shard_map/ppermute | solution.py:399
  203.5 1.5 shard_map.99
  205.9 1.2 collective-permute-start.29
  207.1 1.5 collective-permute-start.30
  208.5 3.7 %collective-permute-done.31.refs_0_ = bf16[400,512]{1,0:T(8,128)(2,1)S(1)} collective-permute-done((bf16[400,512]{1,0:T(8,128)(2,1)}, bf16[400,512]{1,0:T(8,128)(2,1)S(1)}, u32[]{:S(2)}, u32[]{:S(2)}) %collective-permute-start.31) | collective-permute-done | bytes 409632 | tf_op jit(solution)/shard_map/ppermute | solution.py:399
  212.7 1.5 shard_map.100
  214.2 1.1 collective-permute-start.32
  216.3 1.5 collective-permute-start.34
  217.7 1.9 collective-permute-done.32.refs_9_
  219.6 2.6 %collective-permute-done.33.refs_10_ = s16[416,128]{1,0:T(8,128)(2,1)S(1)} collective-permute-done((s16[416,128]{1,0:T(8,128)(2,1)S(1)}, s16[416,128]{1,0:T(8,128)(2,1)S(1)}, u32[]{:S(2)}, u32[]{:S(2)}) %collective-permute-start.33) | collective-permute-done | bytes 106528 | tf_op jit(solution)/shard_map/ppermute | solution.py:399
  222.3 5.9 %shard_map.101 = f32[400,2048]{1,0:T(8,128)} custom-call(s32[2]{0:T(128)S(1)} %copy-done.15, s16[416,256]{1,0:T(8,128)(2,1)S(1)} %get-tuple-element.85.refs_0_, s16[416,256]{1,0:T(8,128)(2,1)S(1)} %collective-permute-done.24.refs_1_, s16[416,256]{1,0:T(8,128)(2,1)S(1)} %collective-permute-done.25.refs_2_, ...), custom_call_target="tpu_custom_call" | custom-call | flops 3355443200 | bytes 6029320 | tf_op jit(solution)/shard_map/pallas_call | solution.py:43
  (117 shorter events, 14.8 us)
Async XLA Ops:
  0.6 16.5 %copy-start = (s32[128,64]{0,1:T(8,128)S(1)}, s32[128,64]{0,1:T(8,128)}, u32[]{:S(2)}) copy-start(s32[128,64]{0,1:T(8,128)} %param.12) | copy-start | bytes 98308
  0.7 2.5 %copy-start.2 = (f32[400,3200]{1,0:T(8,128)S(1)}, f32[400,3200]{1,0:T(8,128)}, u32[]{:S(2)}) copy-start(f32[400,3200]{1,0:T(8,128)} %cost.2) | copy-start | bytes 15360004
  3.2 106.7 %copy-start.14 = (s32[2]{0:T(128)}, s32[2]{0:T(128)S(1)}, u32[]{:S(2)}) copy-start(s32[2]{0:T(128)S(1)} %pad_add_fusion.at) | copy-start | bytes 28
  3.2 5.1 %copy-start.16 = (f32[400,2048]{1,0:T(8,128)S(1)}, f32[400,2048]{1,0:T(8,128)}, u32[]{:S(2)}) copy-start(f32[400,2048]{1,0:T(8,128)} %value.1) | copy-start | bytes 9830404
  4.2 37.1 %collective-permute-start.8 = (bf16[112,1664]{1,0:T(8,128)(2,1)S(1)}, bf16[112,1664]{1,0:T(8,128)(2,1)}, u32[]{:S(2)}, u32[]{:S(2)}) collective-permute-start(bf16[112,1664]{1,0:T(8,128)(2,1)S(1)} %shard_map.91), channel_id=1, source_target_pairs={{0,24},{4,28},{8,16},{12,20},{16,8},{20,12},{24,0},{28,4},{1,25},{... | collective-permute-start | bytes 1118216 | tf_op jit(solution)/shard_map/ppermute | solution.py:399
  5.9 35.4 %collective-permute-start.7 = (bf16[112,1664]{1,0:T(8,128)(2,1)S(1)}, bf16[112,1664]{1,0:T(8,128)(2,1)}, u32[]{:S(2)}, u32[]{:S(2)}) collective-permute-start(bf16[112,1664]{1,0:T(8,128)(2,1)S(1)} %shard_map.91), channel_id=1, source_target_pairs={{0,16},{4,20},{8,24},{12,28},{16,0},{20,4},{24,8},{28,12},{1,17},{... | collective-permute-start | bytes 1118216 | tf_op jit(solution)/shard_map/ppermute | solution.py:399
  8.3 8.7 %copy-start.28 = (s32[400]{0:T(512)S(1)}, s32[400]{0:T(512)}, u32[]{:S(2)}) copy-start(s32[400]{0:T(512)} %param.10) | copy-start | bytes 4804
  8.3 9.9 %copy-start.13 = (f32[128,128]{1,0:T(8,128)S(1)}, f32[128,128]{1,0:T(8,128)}, u32[]{:S(2)}) copy-start(f32[128,128]{1,0:T(8,128)} %trans.1) | copy-start | bytes 196612
  13.4 5.2 %copy-start.26 = (s16[400,512]{1,0:T(8,128)(2,1)}, s16[400,512]{1,0:T(8,128)(2,1)S(1)}, u32[]{:S(2)}) copy-start(s16[400,512]{1,0:T(8,128)(2,1)S(1)} %get-tuple-element.64.refs_0_) | copy-start | bytes 1228804
  13.4 12.7 %collective-permute-start = (s16[400,512]{1,0:T(8,128)(2,1)}, s16[400,512]{1,0:T(8,128)(2,1)}, u32[]{:S(2)}, u32[]{:S(2)}) collective-permute-start(s16[400,512]{1,0:T(8,128)(2,1)} %get-tuple-element.57), channel_id=1, source_target_pairs={{0,1},{1,0},{2,3},{3,2},{4,5},{5,4},{6,7},{7,6},{8,9},{9,8},{10,11... | collective-permute-start | bytes 1228808 | tf_op jit(solution)/shard_map/ppermute | solution.py:399
  15.1 19.6 %collective-permute-start.1 = (s16[400,512]{1,0:T(8,128)(2,1)}, s16[400,512]{1,0:T(8,128)(2,1)}, u32[]{:S(2)}, u32[]{:S(2)}) collective-permute-start(s16[400,512]{1,0:T(8,128)(2,1)} %get-tuple-element.58), channel_id=1, source_target_pairs={{0,2},{1,3},{2,0},{3,1},{4,6},{5,7},{6,4},{7,5},{8,10},{9,11},{10,... | collective-permute-start | bytes 1228808 | tf_op jit(solution)/shard_map/ppermute | solution.py:399
  16.6 18.1 %collective-permute-start.2 = (s16[400,512]{1,0:T(8,128)(2,1)}, s16[400,512]{1,0:T(8,128)(2,1)}, u32[]{:S(2)}, u32[]{:S(2)}) collective-permute-start(s16[400,512]{1,0:T(8,128)(2,1)} %get-tuple-element.59), channel_id=1, source_target_pairs={{0,3},{1,2},{2,1},{3,0},{4,7},{5,6},{6,5},{7,4},{8,11},{9,10},{10,... | collective-permute-start | bytes 1228808 | tf_op jit(solution)/shard_map/ppermute | solution.py:399
  18.6 16.0 %copy-start.18 = (bf16[512,512]{1,0:T(8,128)(2,1)}, bf16[512,512]{1,0:T(8,128)(2,1)S(1)}, u32[]{:S(2)}) copy-start(bf16[512,512]{1,0:T(8,128)(2,1)S(1)} %get-tuple-element.68.refs_4_.mix_a) | copy-start | bytes 1572868
  18.6 16.0 %copy-start.20 = (bf16[512,512]{1,0:T(8,128)(2,1)}, bf16[512,512]{1,0:T(8,128)(2,1)S(1)}, u32[]{:S(2)}) copy-start(bf16[512,512]{1,0:T(8,128)(2,1)S(1)} %get-tuple-element.69.refs_5_.mix_b) | copy-start | bytes 1572868
  18.7 16.0 %copy-start.27 = (s16[400,512]{1,0:T(8,128)(2,1)S(1)}, s16[400,512]{1,0:T(8,128)(2,1)}, u32[]{:S(2)}) copy-start(s16[400,512]{1,0:T(8,128)(2,1)} %copy-done.26) | copy-start | bytes 1228804
  19.2 15.5 %copy-start.12 = (f32[400,1]{1,0:T(8,128)S(1)}, f32[400,1]{1,0:T(8,128)}, u32[]{:S(2)}) copy-start(f32[400,1]{1,0:T(8,128)} %copy.10.refs_6_) | copy-start | bytes 4804
  26.1 15.2 %collective-permute-start.6 = (bf16[112,1664]{1,0:T(8,128)(2,1)S(1)}, bf16[112,1664]{1,0:T(8,128)(2,1)}, u32[]{:S(2)}, u32[]{:S(2)}) collective-permute-start(bf16[112,1664]{1,0:T(8,128)(2,1)S(1)} %shard_map.91), channel_id=1, source_target_pairs={{0,8},{4,12},{8,0},{12,4},{16,24},{20,28},{24,16},{28,20},{1,9},{5... | collective-permute-start | bytes 1118216 | tf_op jit(solution)/shard_map/ppermute | solution.py:399
  27.5 1.9 copy-start.17
  34.4 5.7 %copy-start.22 = (bf16[400,512]{1,0:T(8,128)(2,1)}, bf16[400,512]{1,0:T(8,128)(2,1)S(1)}, u32[]{:S(2)}) copy-start(bf16[400,512]{1,0:T(8,128)(2,1)S(1)} %get-tuple-element.63) | copy-start | bytes 1228804
  34.4 5.7 %copy-start.23 = (bf16[400,512]{1,0:T(8,128)(2,1)}, bf16[400,512]{1,0:T(8,128)(2,1)S(1)}, u32[]{:S(2)}) copy-start(bf16[400,512]{1,0:T(8,128)(2,1)S(1)} %get-tuple-element.62) | copy-start | bytes 1228804
  40.1 1.2 copy-start.7
  41.3 43.6 %all-to-all-start = ((bf16[4,416,512]{2,1,0:T(8,128)(2,1)}), bf16[4,416,512]{2,1,0:T(8,128)(2,1)}, u32[]{:S(2)}, u32[]{:S(2)}) async-start(bf16[4,416,512]{2,1,0:T(8,128)(2,1)} %copy-done.7), calls=%async_computation | async-start | bytes 3407872 | tf_op jit(solution)/shard_map/all_to_all | solution.py:422
  47.7 12.6 %collective-permute-start.3 = (bf16[400,512]{1,0:T(8,128)(2,1)}, bf16[400,512]{1,0:T(8,128)(2,1)S(1)}, u32[]{:S(2)}, u32[]{:S(2)}) collective-permute-start(bf16[400,512]{1,0:T(8,128)(2,1)} %copy-done.24), channel_id=1, source_target_pairs={{0,1},{1,0},{2,3},{3,2},{4,5},{5,4},{6,7},{7,6},{8,9},{9,8},{10,11... | collective-permute-start | bytes 1228808 | tf_op jit(solution)/shard_map/ppermute | solution.py:399
  49.2 18.4 %collective-permute-start.4 = (bf16[400,512]{1,0:T(8,128)(2,1)}, bf16[400,512]{1,0:T(8,128)(2,1)S(1)}, u32[]{:S(2)}, u32[]{:S(2)}) collective-permute-start(bf16[400,512]{1,0:T(8,128)(2,1)} %copy-done.23), channel_id=1, source_target_pairs={{0,2},{1,3},{2,0},{3,1},{4,6},{5,7},{6,4},{7,5},{8,10},{9,11},{10,... | collective-permute-start | bytes 1228808 | tf_op jit(solution)/shard_map/ppermute | solution.py:399
  50.7 16.9 %collective-permute-start.5 = (bf16[400,512]{1,0:T(8,128)(2,1)}, bf16[400,512]{1,0:T(8,128)(2,1)S(1)}, u32[]{:S(2)}, u32[]{:S(2)}) collective-permute-start(bf16[400,512]{1,0:T(8,128)(2,1)} %copy-done.22), channel_id=1, source_target_pairs={{0,3},{1,2},{2,1},{3,0},{4,7},{5,6},{6,5},{7,4},{8,11},{9,10},{10,... | collective-permute-start | bytes 1228808 | tf_op jit(solution)/shard_map/ppermute | solution.py:399
  67.6 10.9 %collective-permute-start.10 = (bf16[336,896]{1,0:T(8,128)(2,1)S(1)}, bf16[336,896]{1,0:T(8,128)(2,1)S(1)}, u32[]{:S(2)}, u32[]{:S(2)}) collective-permute-start(bf16[336,896]{1,0:T(8,128)(2,1)S(1)} %slice.6), channel_id=1, source_target_pairs={{0,1},{1,0},{2,3},{3,2},{4,5},{5,4},{6,7},{7,6},{8,9},{9,8},{10,11... | collective-permute-start | bytes 1806344 | tf_op jit(solution)/shard_map/ppermute | solution.py:399
  67.8 15.1 %copy-start.11 = (bf16[400,512]{1,0:T(8,128)(2,1)S(1)}, bf16[400,512]{1,0:T(8,128)(2,1)}, u32[]{:S(2)}) copy-start(bf16[400,512]{1,0:T(8,128)(2,1)} %copy-done.10) | copy-start | bytes 1228804
  67.8 12.6 %collective-permute-start.11 = (bf16[336,768]{1,0:T(8,128)(2,1)S(1)}, bf16[336,768]{1,0:T(8,128)(2,1)S(1)}, u32[]{:S(2)}, u32[]{:S(2)}) collective-permute-start(bf16[336,768]{1,0:T(8,128)(2,1)S(1)} %slice.7), channel_id=1, source_target_pairs={{0,2},{1,3},{2,0},{3,1},{4,6},{5,7},{6,4},{7,5},{8,10},{9,11},{10,... | collective-permute-start | bytes 1548296 | tf_op jit(solution)/shard_map/ppermute | solution.py:399
  79.6 24.1 %collective-permute-start.12 = (bf16[672,896]{1,0:T(8,128)(2,1)}, bf16[672,896]{1,0:T(8,128)(2,1)}, u32[]{:S(2)}, u32[]{:S(2)}) collective-permute-start(bf16[672,896]{1,0:T(8,128)(2,1)} %pad_maximum_fusion.refs_3_), channel_id=1, source_target_pairs={{0,2},{1,3},{2,0},{3,1},{4,6},{5,7},{6,4},{7,5},{8,10},{9,11},{10,... | collective-permute-start | bytes 3612680 | tf_op jit(solution)/shard_map/ppermute | solution.py:399
  81.5 13.5 %collective-permute-start.17 = (bf16[672,768]{1,0:T(8,128)(2,1)}, bf16[672,768]{1,0:T(8,128)(2,1)}, u32[]{:S(2)}, u32[]{:S(2)}) collective-permute-start(bf16[672,768]{1,0:T(8,128)(2,1)} %pad_maximum_fusion.2.refs_5_), channel_id=1, source_target_pairs={{0,4},{4,0},{8,12},{12,8},{16,20},{20,16},{24,28},{28,24},{1,5},{5... | collective-permute-start | bytes 3096584 | tf_op jit(solution)/shard_map/ppermute | solution.py:399
  81.5 25.5 %collective-permute-start.13 = (bf16[672,768]{1,0:T(8,128)(2,1)}, bf16[672,768]{1,0:T(8,128)(2,1)}, u32[]{:S(2)}, u32[]{:S(2)}) collective-permute-start(bf16[672,768]{1,0:T(8,128)(2,1)} %pad_maximum_fusion.2.refs_5_), channel_id=1, source_target_pairs={{0,1},{1,0},{2,3},{3,2},{4,5},{5,4},{6,7},{7,6},{8,9},{9,8},{10,11... | collective-permute-start | bytes 3096584 | tf_op jit(solution)/shard_map/ppermute | solution.py:399
  83.7 1.2 copy-start.5
  84.9 42.1 %all-to-all-start.2 = ((bf16[4,400,512]{2,1,0:T(8,128)(2,1)}), bf16[4,400,512]{2,1,0:T(8,128)(2,1)}, u32[]{:S(2)}, u32[]{:S(2)}) async-start(bf16[4,400,512]{2,1,0:T(8,128)(2,1)} %copy-done.5), calls=%async_computation.2 | async-start | bytes 3276800 | tf_op jit(solution)/shard_map/all_to_all | solution.py:422
  90.3 19.6 %collective-permute-start.9 = (bf16[4,416,512]{2,1,0:T(8,128)(2,1)}, bf16[4,416,512]{2,1,0:T(8,128)(2,1)S(1)}, u32[]{:S(2)}, u32[]{:S(2)}) collective-permute-start(bf16[4,416,512]{2,1,0:T(8,128)(2,1)} %all-to-all-done.refs_0_), channel_id=1, source_target_pairs={{0,4},{4,0},{8,12},{12,8},{16,20},{20,16},{24,28},{28,24},{1,5},{5... | collective-permute-start | bytes 5111816 | tf_op jit(solution)/shard_map/ppermute | solution.py:399
  90.3 2.5 %copy-start.3 = (f32[400,3200]{1,0:T(8,128)S(1)}, f32[400,3200]{1,0:T(8,128)}, u32[]{:S(2)}) copy-start(f32[400,3200]{1,0:T(8,128)} %cost.2) | copy-start | bytes 15360004
  94.4 15.5 %copy-start.9 = (bf16[400,1664]{1,0:T(8,128)(2,1)}, bf16[400,1664]{1,0:T(8,128)(2,1)S(1)}, u32[]{:S(2)}) copy-start(bf16[400,1664]{1,0:T(8,128)(2,1)S(1)} %shard_map.92.refs_2_) | copy-start | bytes 3993604
  94.4 12.7 %collective-permute-start.14 = (bf16[400,1664]{1,0:T(8,128)(2,1)S(1)}, bf16[400,1664]{1,0:T(8,128)(2,1)S(1)}, u32[]{:S(2)}, u32[]{:S(2)}) collective-permute-start(bf16[400,1664]{1,0:T(8,128)(2,1)S(1)} %shard_map.92.refs_2_), channel_id=1, source_target_pairs={{0,4},{4,0},{8,12},{12,8},{16,20},{20,16},{24,28},{28,24},{1,5},{5... | collective-permute-start | bytes 3993608 | tf_op jit(solution)/shard_map/ppermute | solution.py:399
  95.0 12.1 %collective-permute-start.15 = (bf16[672,896]{1,0:T(8,128)(2,1)}, bf16[672,896]{1,0:T(8,128)(2,1)S(1)}, u32[]{:S(2)}, u32[]{:S(2)}) collective-permute-start(bf16[672,896]{1,0:T(8,128)(2,1)} %pad_maximum_fusion.refs_3_), channel_id=1, source_target_pairs={{0,4},{4,0},{8,12},{12,8},{16,20},{20,16},{24,28},{28,24},{1,5},{5... | collective-permute-start | bytes 3612680 | tf_op jit(solution)/shard_map/ppermute | solution.py:399
  103.7 6.2 %collective-permute-start.16 = (bf16[672,896]{1,0:T(8,128)(2,1)}, bf16[672,896]{1,0:T(8,128)(2,1)S(1)}, u32[]{:S(2)}, u32[]{:S(2)}) collective-permute-start(bf16[672,896]{1,0:T(8,128)(2,1)} %collective-permute-done.12.refs_4_), channel_id=1, source_target_pairs={{0,4},{4,0},{8,12},{12,8},{16,20},{20,16},{24,28},{28,24},{1,5},{5... | collective-permute-start | bytes 3612680 | tf_op jit(solution)/shard_map/ppermute | solution.py:399
  107.0 2.8 %collective-permute-start.18 = (bf16[672,768]{1,0:T(8,128)(2,1)}, bf16[672,768]{1,0:T(8,128)(2,1)S(1)}, u32[]{:S(2)}, u32[]{:S(2)}) collective-permute-start(bf16[672,768]{1,0:T(8,128)(2,1)} %collective-permute-done.13.refs_6_), channel_id=1, source_target_pairs={{0,4},{4,0},{8,12},{12,8},{16,20},{20,16},{24,28},{28,24},{1,5},{5... | collective-permute-start | bytes 3096584 | tf_op jit(solution)/shard_map/ppermute | solution.py:399
  107.1 2.9 %copy-start.31 = (bf16[400,1664]{1,0:T(8,128)(2,1)}, bf16[400,1664]{1,0:T(8,128)(2,1)S(1)}, u32[]{:S(2)}) copy-start(bf16[400,1664]{1,0:T(8,128)(2,1)S(1)} %collective-permute-done.14.refs_7_) | copy-start | bytes 3993604
  127.1 42.7 %all-to-all-start.1 = ((bf16[4,416,512]{2,1,0:T(8,128)(2,1)}), bf16[4,416,512]{2,1,0:T(8,128)(2,1)}, u32[]{:S(2)}, u32[]{:S(2)}) async-start(bf16[4,416,512]{2,1,0:T(8,128)(2,1)} %get-tuple-element.75.totals), calls=%async_computation.1 | async-start | bytes 3407872 | tf_op jit(solution)/shard_map/all_to_all | solution.py:422
  133.6 1.5 copy-start.4
  137.0 3.6 %copy-start.8 = (bf16[4,400,512]{2,1,0:T(8,128)(2,1)}, bf16[4,400,512]{2,1,0:T(8,128)(2,1)S(1)}, u32[]{:S(2)}) copy-start(bf16[4,400,512]{2,1,0:T(8,128)(2,1)S(1)} %shard_map.96.own) | copy-start | bytes 4915204
  137.0 3.6 %collective-permute-start.22 = (bf16[4,400,512]{2,1,0:T(8,128)(2,1)S(1)}, bf16[4,400,512]{2,1,0:T(8,128)(2,1)S(1)}, u32[]{:S(2)}, u32[]{:S(2)}) collective-permute-start(bf16[4,400,512]{2,1,0:T(8,128)(2,1)S(1)} %shard_map.96.own), channel_id=1, source_target_pairs={{0,4},{4,0},{8,12},{12,8},{16,20},{20,16},{24,28},{28,24},{1,5},{5... | collective-permute-start | bytes 4915208 | tf_op jit(solution)/shard_map/ppermute | solution.py:399
  140.6 1.2 copy-start.30
  141.8 28.0 %copy-start.15 = (s32[2]{0:T(128)S(1)}, s32[2]{0:T(128)}, u32[]{:S(2)}) copy-start(s32[2]{0:T(128)} %copy-done.14) | copy-start | bytes 28
  153.3 25.4 %collective-permute-start.23 = (bf16[400,512]{1,0:T(8,128)(2,1)}, bf16[400,512]{1,0:T(8,128)(2,1)}, u32[]{:S(2)}, u32[]{:S(2)}) collective-permute-start(bf16[400,512]{1,0:T(8,128)(2,1)} %get-tuple-element.84), channel_id=1, source_target_pairs={{0,8},{4,12},{8,0},{12,4},{16,24},{20,28},{24,16},{28,20},{1,9},{5... | collective-permute-start | bytes 1228808 | tf_op jit(solution)/shard_map/ppermute | solution.py:399
  169.8 25.7 %copy-start.6 = (f32[400,2048]{1,0:T(8,128)S(1)}, f32[400,2048]{1,0:T(8,128)}, u32[]{:S(2)}) copy-start(f32[400,2048]{1,0:T(8,128)} %refs_6_.1) | copy-start | bytes 9830404
  171.7 14.2 %collective-permute-start.19 = (bf16[416,512]{1,0:T(8,128)(2,1)S(1)}, bf16[416,512]{1,0:T(8,128)(2,1)S(1)}, u32[]{:S(2)}, u32[]{:S(2)}) collective-permute-start(bf16[416,512]{1,0:T(8,128)(2,1)S(1)} %get-tuple-element.77), channel_id=1, source_target_pairs={{0,1},{1,0},{2,3},{3,2},{4,5},{5,4},{6,7},{7,6},{8,9},{9,8},{10,11... | collective-permute-start | bytes 1277960 | tf_op jit(solution)/shard_map/ppermute | solution.py:399
  172.6 16.8 %collective-permute-start.20 = (bf16[416,512]{1,0:T(8,128)(2,1)S(1)}, bf16[416,512]{1,0:T(8,128)(2,1)S(1)}, u32[]{:S(2)}, u32[]{:S(2)}) collective-permute-start(bf16[416,512]{1,0:T(8,128)(2,1)S(1)} %get-tuple-element.78), channel_id=1, source_target_pairs={{0,2},{1,3},{2,0},{3,1},{4,6},{5,7},{6,4},{7,5},{8,10},{9,11},{10,... | collective-permute-start | bytes 1277960 | tf_op jit(solution)/shard_map/ppermute | solution.py:399
  173.8 20.4 %collective-permute-start.21 = (bf16[416,512]{1,0:T(8,128)(2,1)S(1)}, bf16[416,512]{1,0:T(8,128)(2,1)S(1)}, u32[]{:S(2)}, u32[]{:S(2)}) collective-permute-start(bf16[416,512]{1,0:T(8,128)(2,1)S(1)} %get-tuple-element.79), channel_id=1, source_target_pairs={{0,3},{1,2},{2,1},{3,0},{4,7},{5,6},{6,5},{7,4},{8,11},{9,10},{10,... | collective-permute-start | bytes 1277960 | tf_op jit(solution)/shard_map/ppermute | solution.py:399
  175.2 28.2 %collective-permute-start.27 = (bf16[400,512]{1,0:T(8,128)(2,1)}, bf16[400,512]{1,0:T(8,128)(2,1)S(1)}, u32[]{:S(2)}, u32[]{:S(2)}) collective-permute-start(bf16[400,512]{1,0:T(8,128)(2,1)} %get-tuple-element.89), channel_id=1, source_target_pairs={{0,16},{4,20},{8,24},{12,28},{16,0},{20,4},{24,8},{28,12},{1,17},{... | collective-permute-start | bytes 1228808 | tf_op jit(solution)/shard_map/ppermute | solution.py:399
  178.7 33.5 %collective-permute-start.31 = (bf16[400,512]{1,0:T(8,128)(2,1)}, bf16[400,512]{1,0:T(8,128)(2,1)S(1)}, u32[]{:S(2)}, u32[]{:S(2)}) collective-permute-start(bf16[400,512]{1,0:T(8,128)(2,1)} %get-tuple-element.96), channel_id=1, source_target_pairs={{0,24},{4,28},{8,16},{12,20},{16,8},{20,12},{24,0},{28,4},{1,25},{... | collective-permute-start | bytes 1228808 | tf_op jit(solution)/shard_map/ppermute | solution.py:399
  185.9 17.5 %collective-permute-start.24 = (s16[416,256]{1,0:T(8,128)(2,1)S(1)}, s16[416,256]{1,0:T(8,128)(2,1)S(1)}, u32[]{:S(2)}, u32[]{:S(2)}) collective-permute-start(s16[416,256]{1,0:T(8,128)(2,1)S(1)} %get-tuple-element.86), channel_id=1, source_target_pairs={{0,1},{1,0},{2,3},{3,2},{4,5},{5,4},{6,7},{7,6},{8,9},{9,8},{10,11... | collective-permute-start | bytes 638984 | tf_op jit(solution)/shard_map/ppermute | solution.py:399
  189.4 14.0 %collective-permute-start.25 = (s16[416,256]{1,0:T(8,128)(2,1)S(1)}, s16[416,256]{1,0:T(8,128)(2,1)S(1)}, u32[]{:S(2)}, u32[]{:S(2)}) collective-permute-start(s16[416,256]{1,0:T(8,128)(2,1)S(1)} %get-tuple-element.87), channel_id=1, source_target_pairs={{0,2},{1,3},{2,0},{3,1},{4,6},{5,7},{6,4},{7,5},{8,10},{9,11},{10,... | collective-permute-start | bytes 638984 | tf_op jit(solution)/shard_map/ppermute | solution.py:399
  194.2 9.3 %collective-permute-start.26 = (s16[416,256]{1,0:T(8,128)(2,1)S(1)}, s16[416,256]{1,0:T(8,128)(2,1)S(1)}, u32[]{:S(2)}, u32[]{:S(2)}) collective-permute-start(s16[416,256]{1,0:T(8,128)(2,1)S(1)} %get-tuple-element.88), channel_id=1, source_target_pairs={{0,3},{1,2},{2,1},{3,0},{4,7},{5,6},{6,5},{7,4},{8,11},{9,10},{10,... | collective-permute-start | bytes 638984 | tf_op jit(solution)/shard_map/ppermute | solution.py:399
  205.0 7.2 %collective-permute-start.28 = (s16[416,128]{1,0:T(8,128)(2,1)S(1)}, s16[416,128]{1,0:T(8,128)(2,1)S(1)}, u32[]{:S(2)}, u32[]{:S(2)}) collective-permute-start(s16[416,128]{1,0:T(8,128)(2,1)S(1)} %get-tuple-element.92), channel_id=1, source_target_pairs={{0,1},{1,0},{2,3},{3,2},{4,5},{5,4},{6,7},{7,6},{8,9},{9,8},{10,11... | collective-permute-start | bytes 319496 | tf_op jit(solution)/shard_map/ppermute | solution.py:399
  205.9 6.3 %collective-permute-start.29 = (s16[416,128]{1,0:T(8,128)(2,1)S(1)}, s16[416,128]{1,0:T(8,128)(2,1)S(1)}, u32[]{:S(2)}, u32[]{:S(2)}) collective-permute-start(s16[416,128]{1,0:T(8,128)(2,1)S(1)} %get-tuple-element.93), channel_id=1, source_target_pairs={{0,2},{1,3},{2,0},{3,1},{4,6},{5,7},{6,4},{7,5},{8,10},{9,11},{10,... | collective-permute-start | bytes 319496 | tf_op jit(solution)/shard_map/ppermute | solution.py:399
  207.1 5.6 %collective-permute-start.30 = (s16[416,128]{1,0:T(8,128)(2,1)S(1)}, s16[416,128]{1,0:T(8,128)(2,1)S(1)}, u32[]{:S(2)}, u32[]{:S(2)}) collective-permute-start(s16[416,128]{1,0:T(8,128)(2,1)S(1)} %get-tuple-element.94), channel_id=1, source_target_pairs={{0,3},{1,2},{2,1},{3,0},{4,7},{5,6},{6,5},{7,4},{8,11},{9,10},{10,... | collective-permute-start | bytes 319496 | tf_op jit(solution)/shard_map/ppermute | solution.py:399
  214.2 5.4 %collective-permute-start.32 = (s16[416,128]{1,0:T(8,128)(2,1)S(1)}, s16[416,128]{1,0:T(8,128)(2,1)S(1)}, u32[]{:S(2)}, u32[]{:S(2)}) collective-permute-start(s16[416,128]{1,0:T(8,128)(2,1)S(1)} %get-tuple-element.99), channel_id=1, source_target_pairs={{0,1},{1,0},{2,3},{3,2},{4,5},{5,4},{6,7},{7,6},{8,9},{9,8},{10,11... | collective-permute-start | bytes 319496 | tf_op jit(solution)/shard_map/ppermute | solution.py:399
  215.3 7.0 %collective-permute-start.33 = (s16[416,128]{1,0:T(8,128)(2,1)S(1)}, s16[416,128]{1,0:T(8,128)(2,1)S(1)}, u32[]{:S(2)}, u32[]{:S(2)}) collective-permute-start(s16[416,128]{1,0:T(8,128)(2,1)S(1)} %get-tuple-element.100), channel_id=1, source_target_pairs={{0,2},{1,3},{2,0},{3,1},{4,6},{5,7},{6,4},{7,5},{8,10},{9,11},{10,... | collective-permute-start | bytes 319496 | tf_op jit(solution)/shard_map/ppermute | solution.py:399
  216.3 6.0 %collective-permute-start.34 = (s16[416,128]{1,0:T(8,128)(2,1)S(1)}, s16[416,128]{1,0:T(8,128)(2,1)S(1)}, u32[]{:S(2)}, u32[]{:S(2)}) collective-permute-start(s16[416,128]{1,0:T(8,128)(2,1)S(1)} %get-tuple-element.101), channel_id=1, source_target_pairs={{0,3},{1,2},{2,1},{3,0},{4,7},{5,6},{6,5},{7,4},{8,11},{9,10},{10,... | collective-permute-start | bytes 319496 | tf_op jit(solution)/shard_map/ppermute | solution.py:399
  222.3 5.9 %copy-start.1 = (s32[128,64]{0,1:T(8,128)S(1)}, s32[128,64]{0,1:T(8,128)}, u32[]{:S(2)}) copy-start(s32[128,64]{0,1:T(8,128)} %param.12) | copy-start | bytes 98308
  (7 other events, 6.8 us)

commit v6 on v5

--- a/solution.py
+++ b/solution.py
@@ -210,7 +210,7 @@
 def total_kernel(plan, at, *refs):
     nz, rows, cut = plan.n_z, plan.rows, plan.cut
     own_weights, other_weights, refs = refs[0], refs[1], refs[2:]
-    both, (sent, scaled, near, given, weight, strip, full, sums, sems) = refs[:10], refs[10:]
+    both, (sent, scaled_out, near, given, scaled, weight, strip, full, sums, sems) = refs[:10], refs[10:]
     z, core, inc = at[0] // 2, at[0] % 2, at[1]
     left, right = pl.ds(0, cut), pl.ds(cut, plan.window - cut)
     always = []
@@ -254,6 +254,8 @@
         if side == 0:
             scaled[g] = part
 
+    scaled_copy = pltpu.make_async_copy(scaled, scaled_out, sems.at[0])
+    scaled_copy.start()
     blocks, cuts = plan.block_rows, (0, cut // LANES, plan.window // LANES)
     for half in range(2):
         for when, c in copies[half]:
@@ -265,13 +267,13 @@
                 full[i * LANES : (i + 1) * LANES, j * LANES : (j + 1) * LANES] = tile
                 if k:
                     full[j * LANES : (j + 1) * LANES, i * LANES : (i + 1) * LANES] = tile.T
-    copies = []
+    copies = [scaled_copy]
     for j in range(nz):
         out = near.at[pl.ds(j * rows, rows)]
         copies.append(
             pltpu.make_async_copy(full.at[county_rows(plan, at, j, 0)], out, sems.at[0])
         )
-    for c in copies:
+    for c in copies[1:]:
         c.start()
     def product(j, carry):
         sums[j] = dot(full[county_rows(plan, at, j, 0), :], weight[...])
@@ -497,6 +499,7 @@
         [at, weights, others, *near],
         [
             pltpu.VMEM((2, nz, packed, w), BF),
+            pltpu.VMEM((nz, rows, w), BF),
             pltpu.VMEM((n, w), BF),
             pltpu.VMEM((n, plan.window), BF),
             pltpu.VMEM((n, n), BF),
@@ -505,7 +508,7 @@
         ],
         solve_flops,
         specs=[SMEM, ANY, ANY] + [ANY] * len(near),
-        out_specs=[VMEM, VMEM, ANY],
+        out_specs=[VMEM, ANY, ANY],
         vmem=46,
     )
     sent = along_z(totals)

time: 232 us -> 232 us (level)
  no operation moved by 1% of the time
where the time goes in v6:
time: 232 us; the launch traced here: 228 us
  waiting for transfers between devices  81.4 us (35%)
  Pallas kernels  64.5 us (28%)
  starting transfers between devices  55.7 us (24%)
  local copies, waits for them, and re-layouts  20 us (9%)
  other arithmetic  5.4 us (2%)
    ppermute x35, waiting for transfers between devices, swap(): return lax.ppermute(x, axis, [(s, s ^ k) for s in range(n)]) if k else x  65.1 us
    pallas_call x16, Pallas kernels, call(): pl.pallas_call(kernel, out_shape=tuple(outs), in_specs=specs or [SMEM] +...  64.5 us
    ppermute x35, starting transfers between devices, swap(): return lax.ppermute(x, axis, [(s, s ^ k) for s in range(n)]) if k else x  37 us
    unnamed x66, local copies, waits for them, and re-layouts  18.7 us
    all_to_all x3, starting transfers between devices, state_split(): along_z = lambda x: lax.all_to_all(x, 'loc', 0, 0, axis_index_groups=lines)  18.7 us
    all_to_all x3, waiting for transfers between devices, state_split(): along_z = lambda x: lax.all_to_all(x, 'loc', 0, 0, axis_index_groups=lines)  16.3 us
  transfers between devices with their start and end apart: 38, of which 17 were waited for; matrix products, arithmetic and copies ran while one was open for 3% of the time, Pallas kernels for 25%

profile of v6, /device:TPU:8, one launch (start us, length us, event | category | flops | bytes accessed | tf_op | source)
XLA Modules:
  0.0 228.3 jit_solution(13952640019606020054)
XLA Ops:
  0.7 2.4 %copy-done.2 = f32[400,3200]{1,0:T(8,128)S(1)} copy-done((f32[400,3200]{1,0:T(8,128)S(1)}, f32[400,3200]{1,0:T(8,128)}, u32[]{:S(2)}) %copy-start.2) | copy-done | bytes 5120024
  3.2 1.1 shard_map.91
  4.2 1.6 collective-permute-start.8
  5.9 1.1 collective-permute-start.7
  7.0 1.2 fusion.12
  8.3 5.2 %shard_map.87 = (s16[400,512]{1,0:T(8,128)(2,1)S(1)}, s16[400,512]{1,0:T(8,128)(2,1)}, s16[400,512]{1,0:T(8,128)(2,1)}, s16[400,512]{1,0:T(8,128)(2,1)}) custom-call(s32[2]{0:T(128)S(1)} %pad_add_fusion.at, f32[400,2048]{1,0:T(8,128)S(1)} %copy-done.16, bf16[512,512]{1,0:T(8,128)(2,1)S(1)} %get-tuple-element.102.first.refs_12_, ...), custom_call_target="tpu_custom_call" | custom-call | flops 3355443200 | bytes 5963784 | tf_op jit(solution)/shard_map/pallas_call | solution.py:43
  13.4 1.6 collective-permute-start
  15.1 1.5 collective-permute-start.1
  19.2 6.9 %collective-permute-done.refs_1_ = s16[400,512]{1,0:T(8,128)(2,1)} collective-permute-done((s16[400,512]{1,0:T(8,128)(2,1)}, s16[400,512]{1,0:T(8,128)(2,1)}, u32[]{:S(2)}, u32[]{:S(2)}) %collective-permute-start) | collective-permute-done | bytes 409632 | tf_op jit(solution)/shard_map/ppermute | solution.py:401
  26.1 1.4 collective-permute-start.6
  27.5 1.9 copy-done.17
  29.5 3.4 %shard_map.86 = (bf16[400,512]{1,0:T(8,128)(2,1)S(1)}, bf16[400,512]{1,0:T(8,128)(2,1)S(1)}, bf16[400,512]{1,0:T(8,128)(2,1)S(1)}, bf16[400,512]{1,0:T(8,128)(2,1)S(1)}) custom-call(s32[2]{0:T(128)S(1)} %pad_add_fusion.at, f32[400,2048]{1,0:T(8,128)S(1)} %copy-done.17, bf16[4,512,512]{2,1,0:T(8,128)(2,1)S(1)} %fusion.hit.refs_4_, ...), custom_call_target="tpu_custom_call" | custom-call | flops 2516582400 | bytes 7536648 | tf_op jit(solution)/shard_map/pallas_call | solution.py:43
  34.7 5.4 %shard_map.90 = bf16[4,416,512]{2,1,0:T(8,128)(2,1)S(1)} custom-call(s32[2]{0:T(128)S(1)} %pad_add_fusion.at, s16[400,512]{1,0:T(8,128)(2,1)S(1)} %copy-done.27, s16[400,512]{1,0:T(8,128)(2,1)} %collective-permute-done.refs_1_, s16[400,512]{1,0:T(8,128)(2,1)} %collective-permute-done.1.refs_2_, s16[400,512]{1,0:T(8,128)(2,1)} %collective-permute-done.2.refs_3_, ...), custom_call_target="tpu_custom_call" | custom-call | flops 2516582400 | bytes 4392520 | tf_op jit(solution)/shard_map/pallas_call | solution.py:43
  40.1 1.2 copy-done.7
  41.3 6.4 %all-to-all-start = ((bf16[4,416,512]{2,1,0:T(8,128)(2,1)}), bf16[4,416,512]{2,1,0:T(8,128)(2,1)}, u32[]{:S(2)}, u32[]{:S(2)}) async-start(bf16[4,416,512]{2,1,0:T(8,128)(2,1)} %copy-done.7), calls=%async_computation | async-start | bytes 3407872 | tf_op jit(solution)/shard_map/all_to_all | solution.py:424
  47.7 1.5 collective-permute-start.3
  49.2 1.5 collective-permute-start.4
  51.2 1.3 pad_maximum_fusion.1
  52.5 7.8 %collective-permute-done.3.refs_1_ = bf16[400,512]{1,0:T(8,128)(2,1)S(1)} collective-permute-done((bf16[400,512]{1,0:T(8,128)(2,1)}, bf16[400,512]{1,0:T(8,128)(2,1)S(1)}, u32[]{:S(2)}, u32[]{:S(2)}) %collective-permute-start.3) | collective-permute-done | bytes 409632 | tf_op jit(solution)/shard_map/ppermute | solution.py:401
  60.3 7.3 %collective-permute-done.4.refs_2_ = bf16[400,512]{1,0:T(8,128)(2,1)S(1)} collective-permute-done((bf16[400,512]{1,0:T(8,128)(2,1)}, bf16[400,512]{1,0:T(8,128)(2,1)S(1)}, u32[]{:S(2)}, u32[]{:S(2)}) %collective-permute-start.4) | collective-permute-done | bytes 409632 | tf_op jit(solution)/shard_map/ppermute | solution.py:401
  67.8 2.9 %collective-permute-start.11 = (bf16[336,768]{1,0:T(8,128)(2,1)S(1)}, bf16[336,768]{1,0:T(8,128)(2,1)S(1)}, u32[]{:S(2)}, u32[]{:S(2)}) collective-permute-start(bf16[336,768]{1,0:T(8,128)(2,1)S(1)} %slice.7), channel_id=1, source_target_pairs={{0,2},{1,3},{2,0},{3,1},{4,6},{5,7},{6,4},{7,5},{8,10},{9,11},{10,... | collective-permute-start | bytes 1548296 | tf_op jit(solution)/shard_map/ppermute | solution.py:401
  70.7 7.8 %collective-permute-done.10 = bf16[336,896]{1,0:T(8,128)(2,1)S(1)} collective-permute-done((bf16[336,896]{1,0:T(8,128)(2,1)S(1)}, bf16[336,896]{1,0:T(8,128)(2,1)S(1)}, u32[]{:S(2)}, u32[]{:S(2)}) %collective-permute-start.10) | collective-permute-done | bytes 602144 | tf_op jit(solution)/shard_map/ppermute | solution.py:401
  78.5 1.1 pad_maximum_fusion.refs_3_
  80.4 1.1 pad_maximum_fusion.2.refs_5_
  81.5 1.4 collective-permute-start.13
  83.7 1.2 copy-done.5
  84.9 5.4 %all-to-all-start.2 = ((bf16[4,400,512]{2,1,0:T(8,128)(2,1)}), bf16[4,400,512]{2,1,0:T(8,128)(2,1)}, u32[]{:S(2)}, u32[]{:S(2)}) async-start(bf16[4,400,512]{2,1,0:T(8,128)(2,1)} %copy-done.5), calls=%async_computation.2 | async-start | bytes 3276800 | tf_op jit(solution)/shard_map/all_to_all | solution.py:424
  90.3 2.4 %copy-done.3 = f32[400,3200]{1,0:T(8,128)S(1)} copy-done((f32[400,3200]{1,0:T(8,128)S(1)}, f32[400,3200]{1,0:T(8,128)}, u32[]{:S(2)}) %copy-start.3) | copy-done | bytes 5120024
  92.8 1.6 shard_map.92.refs_2_
  95.0 8.7 %collective-permute-done.12.refs_4_ = bf16[672,896]{1,0:T(8,128)(2,1)} collective-permute-done((bf16[672,896]{1,0:T(8,128)(2,1)}, bf16[672,896]{1,0:T(8,128)(2,1)}, u32[]{:S(2)}, u32[]{:S(2)}) %collective-permute-start.12) | collective-permute-done | bytes 1204256 | tf_op jit(solution)/shard_map/ppermute | solution.py:401
  103.7 3.3 %collective-permute-done.13.refs_6_ = bf16[672,768]{1,0:T(8,128)(2,1)} collective-permute-done((bf16[672,768]{1,0:T(8,128)(2,1)}, bf16[672,768]{1,0:T(8,128)(2,1)}, u32[]{:S(2)}, u32[]{:S(2)}) %collective-permute-start.13) | collective-permute-done | bytes 1032224 | tf_op jit(solution)/shard_map/ppermute | solution.py:401
  107.1 2.8 %collective-permute-done.18.refs_11_ = bf16[672,768]{1,0:T(8,128)(2,1)S(1)} collective-permute-done((bf16[672,768]{1,0:T(8,128)(2,1)}, bf16[672,768]{1,0:T(8,128)(2,1)S(1)}, u32[]{:S(2)}, u32[]{:S(2)}) %collective-permute-start.18) | collective-permute-done | bytes 1032224 | tf_op jit(solution)/shard_map/ppermute | solution.py:401
  110.9 1.2 copy-done.29
  112.1 14.5 %shard_map.93 = (bf16[4,416,512]{2,1,0:T(8,128)(2,1)}, bf16[4,400,512]{2,1,0:T(8,128)(2,1)}, bf16[1600,3200]{1,0:T(8,128)(2,1)}) custom-call(s32[2]{0:T(128)S(1)} %pad_add_fusion.at, bf16[4,416,512]{2,1,0:T(8,128)(2,1)} %all-to-all-done.refs_0_, bf16[4,416,512]{2,1,0:T(8,128)(2,1)} %copy-done.29, bf16[400,1664]{1,0:T(8,128)(2,1)} %copy-done.9, ...), custom_call_target="tpu_custom_call" | custom-call | flops 5242880000 | bytes 28598280 | tf_op jit(solution)/shard_map/pallas_call | solution.py:43
  126.7 6.9 %all-to-all-start.1 = ((bf16[4,416,512]{2,1,0:T(8,128)(2,1)}), bf16[4,416,512]{2,1,0:T(8,128)(2,1)}, u32[]{:S(2)}, u32[]{:S(2)}) async-start(bf16[4,416,512]{2,1,0:T(8,128)(2,1)} %get-tuple-element.75.totals), calls=%async_computation.1 | async-start | bytes 3407872 | tf_op jit(solution)/shard_map/all_to_all | solution.py:424
  133.6 1.5 copy-done.4
  135.1 1.9 shard_map.96.own
  137.1 3.5 %collective-permute-done.22.other = bf16[4,400,512]{2,1,0:T(8,128)(2,1)S(1)} collective-permute-done((bf16[4,400,512]{2,1,0:T(8,128)(2,1)S(1)}, bf16[4,400,512]{2,1,0:T(8,128)(2,1)S(1)}, u32[]{:S(2)}, u32[]{:S(2)}) %collective-permute-start.22) | collective-permute-done | bytes 1638432 | tf_op jit(solution)/shard_map/ppermute | solution.py:401
  140.6 1.2 copy-done.30
  141.8 11.5 %shard_map.97 = (bf16[400,512]{1,0:T(8,128)(2,1)}, bf16[400,512]{1,0:T(8,128)(2,1)}, bf16[400,512]{1,0:T(8,128)(2,1)}, bf16[400,512]{1,0:T(8,128)(2,1)}) custom-call(s32[2]{0:T(128)} %copy-done.14, bf16[4,400,512]{2,1,0:T(8,128)(2,1)} %copy-done.8, bf16[4,400,512]{2,1,0:T(8,128)(2,1)} %copy-done.30, bf16[1600,3200]{1,0:T(8,128)(2,1)} %get-tuple-element.81.near, ...), custom_call_target="tpu_custom_call" | custom-call | flops 5242880000 | bytes 16793608 | tf_op jit(solution)/shard_map/pallas_call | solution.py:43
  153.4 16.3 %all-to-all-done.1.refs_0_ = bf16[4,416,512]{2,1,0:T(8,128)(2,1)} async-done(((bf16[4,416,512]{2,1,0:T(8,128)(2,1)}), bf16[4,416,512]{2,1,0:T(8,128)(2,1)}, u32[]{:S(2)}, u32[]{:S(2)}) %all-to-all-start.1) | async-done | bytes 1703968 | tf_op jit(solution)/shard_map/all_to_all | solution.py:424
  169.8 1.9 shard_map.94
  172.2 1.6 collective-permute-start.20
  173.8 1.5 collective-permute-start.21
  175.2 3.4 %collective-permute-start.27 = (bf16[400,512]{1,0:T(8,128)(2,1)}, bf16[400,512]{1,0:T(8,128)(2,1)S(1)}, u32[]{:S(2)}, u32[]{:S(2)}) collective-permute-start(bf16[400,512]{1,0:T(8,128)(2,1)} %get-tuple-element.89), channel_id=1, source_target_pairs={{0,16},{4,20},{8,24},{12,28},{16,0},{20,4},{24,8},{28,12},{1,17},{... | collective-permute-start | bytes 1228808 | tf_op jit(solution)/shard_map/ppermute | solution.py:401
  178.7 1.5 collective-permute-start.31
  180.2 1.0 copy-done.19
  181.2 1.0 copy-done.21
  183.2 2.7 %shard_map.98 = (s16[416,256]{1,0:T(8,128)(2,1)S(1)}, s16[416,256]{1,0:T(8,128)(2,1)S(1)}, s16[416,256]{1,0:T(8,128)(2,1)S(1)}, s16[416,256]{1,0:T(8,128)(2,1)S(1)}) custom-call(s32[2]{0:T(128)S(1)} %copy-done.15, bf16[512,512]{1,0:T(8,128)(2,1)S(1)} %copy-done.19, bf16[512,512]{1,0:T(8,128)(2,1)S(1)} %copy-done.21, bf16[400,512]{1,0:T(8,128)(2,1)S(1)} %copy-done.25, ...), custom_call_target="tpu_custom_call" | custom-call | flops 838860800 | bytes 2719752 | tf_op jit(solution)/shard_map/pallas_call | solution.py:43
  186.5 1.4 collective-permute-done.20.refs_2_
  187.8 3.0 %collective-permute-start.25 = (s16[416,256]{1,0:T(8,128)(2,1)S(1)}, s16[416,256]{1,0:T(8,128)(2,1)S(1)}, u32[]{:S(2)}, u32[]{:S(2)}) collective-permute-start(s16[416,256]{1,0:T(8,128)(2,1)S(1)} %get-tuple-element.87), channel_id=1, source_target_pairs={{0,2},{1,3},{2,0},{3,1},{4,6},{5,7},{6,4},{7,5},{8,10},{9,11},{10,... | collective-permute-start | bytes 638984 | tf_op jit(solution)/shard_map/ppermute | solution.py:401
  190.8 3.4 %collective-permute-done.21.refs_3_ = bf16[416,512]{1,0:T(8,128)(2,1)S(1)} collective-permute-done((bf16[416,512]{1,0:T(8,128)(2,1)S(1)}, bf16[416,512]{1,0:T(8,128)(2,1)S(1)}, u32[]{:S(2)}, u32[]{:S(2)}) %collective-permute-start.21) | collective-permute-done | bytes 426016 | tf_op jit(solution)/shard_map/ppermute | solution.py:401
  195.1 5.2 %shard_map.95 = f32[400,2048]{1,0:T(8,128)} custom-call(s32[2]{0:T(128)S(1)} %copy-done.15, bf16[416,512]{1,0:T(8,128)(2,1)S(1)} %get-tuple-element.76.refs_0_, bf16[416,512]{1,0:T(8,128)(2,1)S(1)} %collective-permute-done.19.refs_1_, bf16[416,512]{1,0:T(8,128)(2,1)S(1)} %collective-permute-done.20.refs_2_, ...), custom_call_target="tpu_custom_call" | custom-call | flops 1677721600 | bytes 10878984 | tf_op jit(solution)/shard_map/pallas_call | solution.py:43
  200.3 3.2 %collective-permute-done.27.refs_0_ = bf16[400,512]{1,0:T(8,128)(2,1)S(1)} collective-permute-done((bf16[400,512]{1,0:T(8,128)(2,1)}, bf16[400,512]{1,0:T(8,128)(2,1)S(1)}, u32[]{:S(2)}, u32[]{:S(2)}) %collective-permute-start.27) | collective-permute-done | bytes 409632 | tf_op jit(solution)/shard_map/ppermute | solution.py:401
  203.5 1.5 shard_map.99
  205.5 1.5 collective-permute-start.29
  207.1 1.5 collective-permute-start.30
  208.5 3.7 %collective-permute-done.31.refs_0_ = bf16[400,512]{1,0:T(8,128)(2,1)S(1)} collective-permute-done((bf16[400,512]{1,0:T(8,128)(2,1)}, bf16[400,512]{1,0:T(8,128)(2,1)S(1)}, u32[]{:S(2)}, u32[]{:S(2)}) %collective-permute-start.31) | collective-permute-done | bytes 409632 | tf_op jit(solution)/shard_map/ppermute | solution.py:401
  212.7 1.5 shard_map.100
  214.2 1.1 collective-permute-start.32
  216.3 1.5 collective-permute-start.34
  217.7 2.3 collective-permute-done.32.refs_9_
  220.0 2.3 collective-permute-done.33.refs_10_
  222.3 5.9 %shard_map.101 = f32[400,2048]{1,0:T(8,128)} custom-call(s32[2]{0:T(128)S(1)} %copy-done.15, s16[416,256]{1,0:T(8,128)(2,1)S(1)} %get-tuple-element.85.refs_0_, s16[416,256]{1,0:T(8,128)(2,1)S(1)} %collective-permute-done.24.refs_1_, s16[416,256]{1,0:T(8,128)(2,1)S(1)} %collective-permute-done.25.refs_2_, ...), custom_call_target="tpu_custom_call" | custom-call | flops 3355443200 | bytes 6029320 | tf_op jit(solution)/shard_map/pallas_call | solution.py:43
  (117 shorter events, 13.6 us)
Async XLA Ops:
  0.6 16.5 %copy-start = (s32[128,64]{0,1:T(8,128)S(1)}, s32[128,64]{0,1:T(8,128)}, u32[]{:S(2)}) copy-start(s32[128,64]{0,1:T(8,128)} %param.12) | copy-start | bytes 98308
  0.7 2.5 %copy-start.2 = (f32[400,3200]{1,0:T(8,128)S(1)}, f32[400,3200]{1,0:T(8,128)}, u32[]{:S(2)}) copy-start(f32[400,3200]{1,0:T(8,128)} %cost.2) | copy-start | bytes 15360004
  3.2 106.7 %copy-start.14 = (s32[2]{0:T(128)}, s32[2]{0:T(128)S(1)}, u32[]{:S(2)}) copy-start(s32[2]{0:T(128)S(1)} %pad_add_fusion.at) | copy-start | bytes 28
  3.2 5.1 %copy-start.16 = (f32[400,2048]{1,0:T(8,128)S(1)}, f32[400,2048]{1,0:T(8,128)}, u32[]{:S(2)}) copy-start(f32[400,2048]{1,0:T(8,128)} %value.1) | copy-start | bytes 9830404
  4.2 37.1 %collective-permute-start.8 = (bf16[112,1664]{1,0:T(8,128)(2,1)S(1)}, bf16[112,1664]{1,0:T(8,128)(2,1)}, u32[]{:S(2)}, u32[]{:S(2)}) collective-permute-start(bf16[112,1664]{1,0:T(8,128)(2,1)S(1)} %shard_map.91), channel_id=1, source_target_pairs={{0,24},{4,28},{8,16},{12,20},{16,8},{20,12},{24,0},{28,4},{1,25},{... | collective-permute-start | bytes 1118216 | tf_op jit(solution)/shard_map/ppermute | solution.py:401
  5.9 35.4 %collective-permute-start.7 = (bf16[112,1664]{1,0:T(8,128)(2,1)S(1)}, bf16[112,1664]{1,0:T(8,128)(2,1)}, u32[]{:S(2)}, u32[]{:S(2)}) collective-permute-start(bf16[112,1664]{1,0:T(8,128)(2,1)S(1)} %shard_map.91), channel_id=1, source_target_pairs={{0,16},{4,20},{8,24},{12,28},{16,0},{20,4},{24,8},{28,12},{1,17},{... | collective-permute-start | bytes 1118216 | tf_op jit(solution)/shard_map/ppermute | solution.py:401
  8.3 8.7 %copy-start.28 = (s32[400]{0:T(512)S(1)}, s32[400]{0:T(512)}, u32[]{:S(2)}) copy-start(s32[400]{0:T(512)} %param.10) | copy-start | bytes 4804
  8.3 9.9 %copy-start.13 = (f32[128,128]{1,0:T(8,128)S(1)}, f32[128,128]{1,0:T(8,128)}, u32[]{:S(2)}) copy-start(f32[128,128]{1,0:T(8,128)} %trans.1) | copy-start | bytes 196612
  13.4 5.2 %copy-start.26 = (s16[400,512]{1,0:T(8,128)(2,1)}, s16[400,512]{1,0:T(8,128)(2,1)S(1)}, u32[]{:S(2)}) copy-start(s16[400,512]{1,0:T(8,128)(2,1)S(1)} %get-tuple-element.64.refs_0_) | copy-start | bytes 1228804
  13.4 12.7 %collective-permute-start = (s16[400,512]{1,0:T(8,128)(2,1)}, s16[400,512]{1,0:T(8,128)(2,1)}, u32[]{:S(2)}, u32[]{:S(2)}) collective-permute-start(s16[400,512]{1,0:T(8,128)(2,1)} %get-tuple-element.57), channel_id=1, source_target_pairs={{0,1},{1,0},{2,3},{3,2},{4,5},{5,4},{6,7},{7,6},{8,9},{9,8},{10,11... | collective-permute-start | bytes 1228808 | tf_op jit(solution)/shard_map/ppermute | solution.py:401
  15.1 19.6 %collective-permute-start.1 = (s16[400,512]{1,0:T(8,128)(2,1)}, s16[400,512]{1,0:T(8,128)(2,1)}, u32[]{:S(2)}, u32[]{:S(2)}) collective-permute-start(s16[400,512]{1,0:T(8,128)(2,1)} %get-tuple-element.58), channel_id=1, source_target_pairs={{0,2},{1,3},{2,0},{3,1},{4,6},{5,7},{6,4},{7,5},{8,10},{9,11},{10,... | collective-permute-start | bytes 1228808 | tf_op jit(solution)/shard_map/ppermute | solution.py:401
  16.6 18.1 %collective-permute-start.2 = (s16[400,512]{1,0:T(8,128)(2,1)}, s16[400,512]{1,0:T(8,128)(2,1)}, u32[]{:S(2)}, u32[]{:S(2)}) collective-permute-start(s16[400,512]{1,0:T(8,128)(2,1)} %get-tuple-element.59), channel_id=1, source_target_pairs={{0,3},{1,2},{2,1},{3,0},{4,7},{5,6},{6,5},{7,4},{8,11},{9,10},{10,... | collective-permute-start | bytes 1228808 | tf_op jit(solution)/shard_map/ppermute | solution.py:401
  18.6 16.0 %copy-start.18 = (bf16[512,512]{1,0:T(8,128)(2,1)}, bf16[512,512]{1,0:T(8,128)(2,1)S(1)}, u32[]{:S(2)}) copy-start(bf16[512,512]{1,0:T(8,128)(2,1)S(1)} %get-tuple-element.68.refs_4_.mix_a) | copy-start | bytes 1572868
  18.6 16.0 %copy-start.20 = (bf16[512,512]{1,0:T(8,128)(2,1)}, bf16[512,512]{1,0:T(8,128)(2,1)S(1)}, u32[]{:S(2)}) copy-start(bf16[512,512]{1,0:T(8,128)(2,1)S(1)} %get-tuple-element.69.refs_5_.mix_b) | copy-start | bytes 1572868
  18.7 16.0 %copy-start.27 = (s16[400,512]{1,0:T(8,128)(2,1)S(1)}, s16[400,512]{1,0:T(8,128)(2,1)}, u32[]{:S(2)}) copy-start(s16[400,512]{1,0:T(8,128)(2,1)} %copy-done.26) | copy-start | bytes 1228804
  19.2 15.5 %copy-start.12 = (f32[400,1]{1,0:T(8,128)S(1)}, f32[400,1]{1,0:T(8,128)}, u32[]{:S(2)}) copy-start(f32[400,1]{1,0:T(8,128)} %copy.10.refs_6_) | copy-start | bytes 4804
  26.1 15.2 %collective-permute-start.6 = (bf16[112,1664]{1,0:T(8,128)(2,1)S(1)}, bf16[112,1664]{1,0:T(8,128)(2,1)}, u32[]{:S(2)}, u32[]{:S(2)}) collective-permute-start(bf16[112,1664]{1,0:T(8,128)(2,1)S(1)} %shard_map.91), channel_id=1, source_target_pairs={{0,8},{4,12},{8,0},{12,4},{16,24},{20,28},{24,16},{28,20},{1,9},{5... | collective-permute-start | bytes 1118216 | tf_op jit(solution)/shard_map/ppermute | solution.py:401
  27.5 1.9 copy-start.17
  34.4 5.7 %copy-start.22 = (bf16[400,512]{1,0:T(8,128)(2,1)}, bf16[400,512]{1,0:T(8,128)(2,1)S(1)}, u32[]{:S(2)}) copy-start(bf16[400,512]{1,0:T(8,128)(2,1)S(1)} %get-tuple-element.63) | copy-start | bytes 1228804
  34.4 5.7 %copy-start.23 = (bf16[400,512]{1,0:T(8,128)(2,1)}, bf16[400,512]{1,0:T(8,128)(2,1)S(1)}, u32[]{:S(2)}) copy-start(bf16[400,512]{1,0:T(8,128)(2,1)S(1)} %get-tuple-element.62) | copy-start | bytes 1228804
  40.1 1.2 copy-start.7
  41.3 43.6 %all-to-all-start = ((bf16[4,416,512]{2,1,0:T(8,128)(2,1)}), bf16[4,416,512]{2,1,0:T(8,128)(2,1)}, u32[]{:S(2)}, u32[]{:S(2)}) async-start(bf16[4,416,512]{2,1,0:T(8,128)(2,1)} %copy-done.7), calls=%async_computation | async-start | bytes 3407872 | tf_op jit(solution)/shard_map/all_to_all | solution.py:424
  47.7 12.6 %collective-permute-start.3 = (bf16[400,512]{1,0:T(8,128)(2,1)}, bf16[400,512]{1,0:T(8,128)(2,1)S(1)}, u32[]{:S(2)}, u32[]{:S(2)}) collective-permute-start(bf16[400,512]{1,0:T(8,128)(2,1)} %copy-done.24), channel_id=1, source_target_pairs={{0,1},{1,0},{2,3},{3,2},{4,5},{5,4},{6,7},{7,6},{8,9},{9,8},{10,11... | collective-permute-start | bytes 1228808 | tf_op jit(solution)/shard_map/ppermute | solution.py:401
  49.2 18.4 %collective-permute-start.4 = (bf16[400,512]{1,0:T(8,128)(2,1)}, bf16[400,512]{1,0:T(8,128)(2,1)S(1)}, u32[]{:S(2)}, u32[]{:S(2)}) collective-permute-start(bf16[400,512]{1,0:T(8,128)(2,1)} %copy-done.23), channel_id=1, source_target_pairs={{0,2},{1,3},{2,0},{3,1},{4,6},{5,7},{6,4},{7,5},{8,10},{9,11},{10,... | collective-permute-start | bytes 1228808 | tf_op jit(solution)/shard_map/ppermute | solution.py:401
  50.7 16.9 %collective-permute-start.5 = (bf16[400,512]{1,0:T(8,128)(2,1)}, bf16[400,512]{1,0:T(8,128)(2,1)S(1)}, u32[]{:S(2)}, u32[]{:S(2)}) collective-permute-start(bf16[400,512]{1,0:T(8,128)(2,1)} %copy-done.22), channel_id=1, source_target_pairs={{0,3},{1,2},{2,1},{3,0},{4,7},{5,6},{6,5},{7,4},{8,11},{9,10},{10,... | collective-permute-start | bytes 1228808 | tf_op jit(solution)/shard_map/ppermute | solution.py:401
  67.6 10.9 %collective-permute-start.10 = (bf16[336,896]{1,0:T(8,128)(2,1)S(1)}, bf16[336,896]{1,0:T(8,128)(2,1)S(1)}, u32[]{:S(2)}, u32[]{:S(2)}) collective-permute-start(bf16[336,896]{1,0:T(8,128)(2,1)S(1)} %slice.6), channel_id=1, source_target_pairs={{0,1},{1,0},{2,3},{3,2},{4,5},{5,4},{6,7},{7,6},{8,9},{9,8},{10,11... | collective-permute-start | bytes 1806344 | tf_op jit(solution)/shard_map/ppermute | solution.py:401
  67.8 15.1 %copy-start.11 = (bf16[400,512]{1,0:T(8,128)(2,1)S(1)}, bf16[400,512]{1,0:T(8,128)(2,1)}, u32[]{:S(2)}) copy-start(bf16[400,512]{1,0:T(8,128)(2,1)} %copy-done.10) | copy-start | bytes 1228804
  67.8 12.6 %collective-permute-start.11 = (bf16[336,768]{1,0:T(8,128)(2,1)S(1)}, bf16[336,768]{1,0:T(8,128)(2,1)S(1)}, u32[]{:S(2)}, u32[]{:S(2)}) collective-permute-start(bf16[336,768]{1,0:T(8,128)(2,1)S(1)} %slice.7), channel_id=1, source_target_pairs={{0,2},{1,3},{2,0},{3,1},{4,6},{5,7},{6,4},{7,5},{8,10},{9,11},{10,... | collective-permute-start | bytes 1548296 | tf_op jit(solution)/shard_map/ppermute | solution.py:401
  79.6 24.1 %collective-permute-start.12 = (bf16[672,896]{1,0:T(8,128)(2,1)}, bf16[672,896]{1,0:T(8,128)(2,1)}, u32[]{:S(2)}, u32[]{:S(2)}) collective-permute-start(bf16[672,896]{1,0:T(8,128)(2,1)} %pad_maximum_fusion.refs_3_), channel_id=1, source_target_pairs={{0,2},{1,3},{2,0},{3,1},{4,6},{5,7},{6,4},{7,5},{8,10},{9,11},{10,... | collective-permute-start | bytes 3612680 | tf_op jit(solution)/shard_map/ppermute | solution.py:401
  81.5 13.5 %collective-permute-start.17 = (bf16[672,768]{1,0:T(8,128)(2,1)}, bf16[672,768]{1,0:T(8,128)(2,1)}, u32[]{:S(2)}, u32[]{:S(2)}) collective-permute-start(bf16[672,768]{1,0:T(8,128)(2,1)} %pad_maximum_fusion.2.refs_5_), channel_id=1, source_target_pairs={{0,4},{4,0},{8,12},{12,8},{16,20},{20,16},{24,28},{28,24},{1,5},{5... | collective-permute-start | bytes 3096584 | tf_op jit(solution)/shard_map/ppermute | solution.py:401
  81.5 25.5 %collective-permute-start.13 = (bf16[672,768]{1,0:T(8,128)(2,1)}, bf16[672,768]{1,0:T(8,128)(2,1)}, u32[]{:S(2)}, u32[]{:S(2)}) collective-permute-start(bf16[672,768]{1,0:T(8,128)(2,1)} %pad_maximum_fusion.2.refs_5_), channel_id=1, source_target_pairs={{0,1},{1,0},{2,3},{3,2},{4,5},{5,4},{6,7},{7,6},{8,9},{9,8},{10,11... | collective-permute-start | bytes 3096584 | tf_op jit(solution)/shard_map/ppermute | solution.py:401
  83.7 1.2 copy-start.5
  84.9 41.7 %all-to-all-start.2 = ((bf16[4,400,512]{2,1,0:T(8,128)(2,1)}), bf16[4,400,512]{2,1,0:T(8,128)(2,1)}, u32[]{:S(2)}, u32[]{:S(2)}) async-start(bf16[4,400,512]{2,1,0:T(8,128)(2,1)} %copy-done.5), calls=%async_computation.2 | async-start | bytes 3276800 | tf_op jit(solution)/shard_map/all_to_all | solution.py:424
  90.3 19.6 %collective-permute-start.9 = (bf16[4,416,512]{2,1,0:T(8,128)(2,1)}, bf16[4,416,512]{2,1,0:T(8,128)(2,1)S(1)}, u32[]{:S(2)}, u32[]{:S(2)}) collective-permute-start(bf16[4,416,512]{2,1,0:T(8,128)(2,1)} %all-to-all-done.refs_0_), channel_id=1, source_target_pairs={{0,4},{4,0},{8,12},{12,8},{16,20},{20,16},{24,28},{28,24},{1,5},{5... | collective-permute-start | bytes 5111816 | tf_op jit(solution)/shard_map/ppermute | solution.py:401
  90.3 2.5 %copy-start.3 = (f32[400,3200]{1,0:T(8,128)S(1)}, f32[400,3200]{1,0:T(8,128)}, u32[]{:S(2)}) copy-start(f32[400,3200]{1,0:T(8,128)} %cost.2) | copy-start | bytes 15360004
  94.4 15.5 %copy-start.9 = (bf16[400,1664]{1,0:T(8,128)(2,1)}, bf16[400,1664]{1,0:T(8,128)(2,1)S(1)}, u32[]{:S(2)}) copy-start(bf16[400,1664]{1,0:T(8,128)(2,1)S(1)} %shard_map.92.refs_2_) | copy-start | bytes 3993604
  94.4 12.7 %collective-permute-start.14 = (bf16[400,1664]{1,0:T(8,128)(2,1)S(1)}, bf16[400,1664]{1,0:T(8,128)(2,1)S(1)}, u32[]{:S(2)}, u32[]{:S(2)}) collective-permute-start(bf16[400,1664]{1,0:T(8,128)(2,1)S(1)} %shard_map.92.refs_2_), channel_id=1, source_target_pairs={{0,4},{4,0},{8,12},{12,8},{16,20},{20,16},{24,28},{28,24},{1,5},{5... | collective-permute-start | bytes 3993608 | tf_op jit(solution)/shard_map/ppermute | solution.py:401
  95.0 12.1 %collective-permute-start.15 = (bf16[672,896]{1,0:T(8,128)(2,1)}, bf16[672,896]{1,0:T(8,128)(2,1)S(1)}, u32[]{:S(2)}, u32[]{:S(2)}) collective-permute-start(bf16[672,896]{1,0:T(8,128)(2,1)} %pad_maximum_fusion.refs_3_), channel_id=1, source_target_pairs={{0,4},{4,0},{8,12},{12,8},{16,20},{20,16},{24,28},{28,24},{1,5},{5... | collective-permute-start | bytes 3612680 | tf_op jit(solution)/shard_map/ppermute | solution.py:401
  103.7 6.2 %collective-permute-start.16 = (bf16[672,896]{1,0:T(8,128)(2,1)}, bf16[672,896]{1,0:T(8,128)(2,1)S(1)}, u32[]{:S(2)}, u32[]{:S(2)}) collective-permute-start(bf16[672,896]{1,0:T(8,128)(2,1)} %collective-permute-done.12.refs_4_), channel_id=1, source_target_pairs={{0,4},{4,0},{8,12},{12,8},{16,20},{20,16},{24,28},{28,24},{1,5},{5... | collective-permute-start | bytes 3612680 | tf_op jit(solution)/shard_map/ppermute | solution.py:401
  107.0 2.8 %collective-permute-start.18 = (bf16[672,768]{1,0:T(8,128)(2,1)}, bf16[672,768]{1,0:T(8,128)(2,1)S(1)}, u32[]{:S(2)}, u32[]{:S(2)}) collective-permute-start(bf16[672,768]{1,0:T(8,128)(2,1)} %collective-permute-done.13.refs_6_), channel_id=1, source_target_pairs={{0,4},{4,0},{8,12},{12,8},{16,20},{20,16},{24,28},{28,24},{1,5},{5... | collective-permute-start | bytes 3096584 | tf_op jit(solution)/shard_map/ppermute | solution.py:401
  107.1 2.9 %copy-start.31 = (bf16[400,1664]{1,0:T(8,128)(2,1)}, bf16[400,1664]{1,0:T(8,128)(2,1)S(1)}, u32[]{:S(2)}) copy-start(bf16[400,1664]{1,0:T(8,128)(2,1)S(1)} %collective-permute-done.14.refs_7_) | copy-start | bytes 3993604
  126.7 43.1 %all-to-all-start.1 = ((bf16[4,416,512]{2,1,0:T(8,128)(2,1)}), bf16[4,416,512]{2,1,0:T(8,128)(2,1)}, u32[]{:S(2)}, u32[]{:S(2)}) async-start(bf16[4,416,512]{2,1,0:T(8,128)(2,1)} %get-tuple-element.75.totals), calls=%async_computation.1 | async-start | bytes 3407872 | tf_op jit(solution)/shard_map/all_to_all | solution.py:424
  133.6 1.5 copy-start.4
  137.0 3.6 %copy-start.8 = (bf16[4,400,512]{2,1,0:T(8,128)(2,1)}, bf16[4,400,512]{2,1,0:T(8,128)(2,1)S(1)}, u32[]{:S(2)}) copy-start(bf16[4,400,512]{2,1,0:T(8,128)(2,1)S(1)} %shard_map.96.own) | copy-start | bytes 4915204
  137.0 3.6 %collective-permute-start.22 = (bf16[4,400,512]{2,1,0:T(8,128)(2,1)S(1)}, bf16[4,400,512]{2,1,0:T(8,128)(2,1)S(1)}, u32[]{:S(2)}, u32[]{:S(2)}) collective-permute-start(bf16[4,400,512]{2,1,0:T(8,128)(2,1)S(1)} %shard_map.96.own), channel_id=1, source_target_pairs={{0,4},{4,0},{8,12},{12,8},{16,20},{20,16},{24,28},{28,24},{1,5},{5... | collective-permute-start | bytes 4915208 | tf_op jit(solution)/shard_map/ppermute | solution.py:401
  140.6 1.2 copy-start.30
  141.8 28.0 %copy-start.15 = (s32[2]{0:T(128)S(1)}, s32[2]{0:T(128)}, u32[]{:S(2)}) copy-start(s32[2]{0:T(128)} %copy-done.14) | copy-start | bytes 28
  153.3 25.4 %collective-permute-start.23 = (bf16[400,512]{1,0:T(8,128)(2,1)}, bf16[400,512]{1,0:T(8,128)(2,1)}, u32[]{:S(2)}, u32[]{:S(2)}) collective-permute-start(bf16[400,512]{1,0:T(8,128)(2,1)} %get-tuple-element.84), channel_id=1, source_target_pairs={{0,8},{4,12},{8,0},{12,4},{16,24},{20,28},{24,16},{28,20},{1,9},{5... | collective-permute-start | bytes 1228808 | tf_op jit(solution)/shard_map/ppermute | solution.py:401
  169.8 25.4 %copy-start.6 = (f32[400,2048]{1,0:T(8,128)S(1)}, f32[400,2048]{1,0:T(8,128)}, u32[]{:S(2)}) copy-start(f32[400,2048]{1,0:T(8,128)} %refs_6_.1) | copy-start | bytes 9830404
  171.7 14.2 %collective-permute-start.19 = (bf16[416,512]{1,0:T(8,128)(2,1)S(1)}, bf16[416,512]{1,0:T(8,128)(2,1)S(1)}, u32[]{:S(2)}, u32[]{:S(2)}) collective-permute-start(bf16[416,512]{1,0:T(8,128)(2,1)S(1)} %get-tuple-element.77), channel_id=1, source_target_pairs={{0,1},{1,0},{2,3},{3,2},{4,5},{5,4},{6,7},{7,6},{8,9},{9,8},{10,11... | collective-permute-start | bytes 1277960 | tf_op jit(solution)/shard_map/ppermute | solution.py:401
  172.2 15.6 %collective-permute-start.20 = (bf16[416,512]{1,0:T(8,128)(2,1)S(1)}, bf16[416,512]{1,0:T(8,128)(2,1)S(1)}, u32[]{:S(2)}, u32[]{:S(2)}) collective-permute-start(bf16[416,512]{1,0:T(8,128)(2,1)S(1)} %get-tuple-element.78), channel_id=1, source_target_pairs={{0,2},{1,3},{2,0},{3,1},{4,6},{5,7},{6,4},{7,5},{8,10},{9,11},{10,... | collective-permute-start | bytes 1277960 | tf_op jit(solution)/shard_map/ppermute | solution.py:401
  173.8 20.4 %collective-permute-start.21 = (bf16[416,512]{1,0:T(8,128)(2,1)S(1)}, bf16[416,512]{1,0:T(8,128)(2,1)S(1)}, u32[]{:S(2)}, u32[]{:S(2)}) collective-permute-start(bf16[416,512]{1,0:T(8,128)(2,1)S(1)} %get-tuple-element.79), channel_id=1, source_target_pairs={{0,3},{1,2},{2,1},{3,0},{4,7},{5,6},{6,5},{7,4},{8,11},{9,10},{10,... | collective-permute-start | bytes 1277960 | tf_op jit(solution)/shard_map/ppermute | solution.py:401
  175.2 28.2 %collective-permute-start.27 = (bf16[400,512]{1,0:T(8,128)(2,1)}, bf16[400,512]{1,0:T(8,128)(2,1)S(1)}, u32[]{:S(2)}, u32[]{:S(2)}) collective-permute-start(bf16[400,512]{1,0:T(8,128)(2,1)} %get-tuple-element.89), channel_id=1, source_target_pairs={{0,16},{4,20},{8,24},{12,28},{16,0},{20,4},{24,8},{28,12},{1,17},{... | collective-permute-start | bytes 1228808 | tf_op jit(solution)/shard_map/ppermute | solution.py:401
  178.7 33.5 %collective-permute-start.31 = (bf16[400,512]{1,0:T(8,128)(2,1)}, bf16[400,512]{1,0:T(8,128)(2,1)S(1)}, u32[]{:S(2)}, u32[]{:S(2)}) collective-permute-start(bf16[400,512]{1,0:T(8,128)(2,1)} %get-tuple-element.96), channel_id=1, source_target_pairs={{0,24},{4,28},{8,16},{12,20},{16,8},{20,12},{24,0},{28,4},{1,25},{... | collective-permute-start | bytes 1228808 | tf_op jit(solution)/shard_map/ppermute | solution.py:401
  185.9 17.5 %collective-permute-start.24 = (s16[416,256]{1,0:T(8,128)(2,1)S(1)}, s16[416,256]{1,0:T(8,128)(2,1)S(1)}, u32[]{:S(2)}, u32[]{:S(2)}) collective-permute-start(s16[416,256]{1,0:T(8,128)(2,1)S(1)} %get-tuple-element.86), channel_id=1, source_target_pairs={{0,1},{1,0},{2,3},{3,2},{4,5},{5,4},{6,7},{7,6},{8,9},{9,8},{10,11... | collective-permute-start | bytes 638984 | tf_op jit(solution)/shard_map/ppermute | solution.py:401
  187.8 15.6 %collective-permute-start.25 = (s16[416,256]{1,0:T(8,128)(2,1)S(1)}, s16[416,256]{1,0:T(8,128)(2,1)S(1)}, u32[]{:S(2)}, u32[]{:S(2)}) collective-permute-start(s16[416,256]{1,0:T(8,128)(2,1)S(1)} %get-tuple-element.87), channel_id=1, source_target_pairs={{0,2},{1,3},{2,0},{3,1},{4,6},{5,7},{6,4},{7,5},{8,10},{9,11},{10,... | collective-permute-start | bytes 638984 | tf_op jit(solution)/shard_map/ppermute | solution.py:401
  194.2 9.3 %collective-permute-start.26 = (s16[416,256]{1,0:T(8,128)(2,1)S(1)}, s16[416,256]{1,0:T(8,128)(2,1)S(1)}, u32[]{:S(2)}, u32[]{:S(2)}) collective-permute-start(s16[416,256]{1,0:T(8,128)(2,1)S(1)} %get-tuple-element.88), channel_id=1, source_target_pairs={{0,3},{1,2},{2,1},{3,0},{4,7},{5,6},{6,5},{7,4},{8,11},{9,10},{10,... | collective-permute-start | bytes 638984 | tf_op jit(solution)/shard_map/ppermute | solution.py:401
  205.0 7.2 %collective-permute-start.28 = (s16[416,128]{1,0:T(8,128)(2,1)S(1)}, s16[416,128]{1,0:T(8,128)(2,1)S(1)}, u32[]{:S(2)}, u32[]{:S(2)}) collective-permute-start(s16[416,128]{1,0:T(8,128)(2,1)S(1)} %get-tuple-element.92), channel_id=1, source_target_pairs={{0,1},{1,0},{2,3},{3,2},{4,5},{5,4},{6,7},{7,6},{8,9},{9,8},{10,11... | collective-permute-start | bytes 319496 | tf_op jit(solution)/shard_map/ppermute | solution.py:401
  205.5 6.7 %collective-permute-start.29 = (s16[416,128]{1,0:T(8,128)(2,1)S(1)}, s16[416,128]{1,0:T(8,128)(2,1)S(1)}, u32[]{:S(2)}, u32[]{:S(2)}) collective-permute-start(s16[416,128]{1,0:T(8,128)(2,1)S(1)} %get-tuple-element.93), channel_id=1, source_target_pairs={{0,2},{1,3},{2,0},{3,1},{4,6},{5,7},{6,4},{7,5},{8,10},{9,11},{10,... | collective-permute-start | bytes 319496 | tf_op jit(solution)/shard_map/ppermute | solution.py:401
  207.1 5.6 %collective-permute-start.30 = (s16[416,128]{1,0:T(8,128)(2,1)S(1)}, s16[416,128]{1,0:T(8,128)(2,1)S(1)}, u32[]{:S(2)}, u32[]{:S(2)}) collective-permute-start(s16[416,128]{1,0:T(8,128)(2,1)S(1)} %get-tuple-element.94), channel_id=1, source_target_pairs={{0,3},{1,2},{2,1},{3,0},{4,7},{5,6},{6,5},{7,4},{8,11},{9,10},{10,... | collective-permute-start | bytes 319496 | tf_op jit(solution)/shard_map/ppermute | solution.py:401
  214.2 5.8 %collective-permute-start.32 = (s16[416,128]{1,0:T(8,128)(2,1)S(1)}, s16[416,128]{1,0:T(8,128)(2,1)S(1)}, u32[]{:S(2)}, u32[]{:S(2)}) collective-permute-start(s16[416,128]{1,0:T(8,128)(2,1)S(1)} %get-tuple-element.99), channel_id=1, source_target_pairs={{0,1},{1,0},{2,3},{3,2},{4,5},{5,4},{6,7},{7,6},{8,9},{9,8},{10,11... | collective-permute-start | bytes 319496 | tf_op jit(solution)/shard_map/ppermute | solution.py:401
  215.3 7.0 %collective-permute-start.33 = (s16[416,128]{1,0:T(8,128)(2,1)S(1)}, s16[416,128]{1,0:T(8,128)(2,1)S(1)}, u32[]{:S(2)}, u32[]{:S(2)}) collective-permute-start(s16[416,128]{1,0:T(8,128)(2,1)S(1)} %get-tuple-element.100), channel_id=1, source_target_pairs={{0,2},{1,3},{2,0},{3,1},{4,6},{5,7},{6,4},{7,5},{8,10},{9,11},{10,... | collective-permute-start | bytes 319496 | tf_op jit(solution)/shard_map/ppermute | solution.py:401
  216.3 6.0 %collective-permute-start.34 = (s16[416,128]{1,0:T(8,128)(2,1)S(1)}, s16[416,128]{1,0:T(8,128)(2,1)S(1)}, u32[]{:S(2)}, u32[]{:S(2)}) collective-permute-start(s16[416,128]{1,0:T(8,128)(2,1)S(1)} %get-tuple-element.101), channel_id=1, source_target_pairs={{0,3},{1,2},{2,1},{3,0},{4,7},{5,6},{6,5},{7,4},{8,11},{9,10},{10,... | collective-permute-start | bytes 319496 | tf_op jit(solution)/shard_map/ppermute | solution.py:401
  222.3 5.9 %copy-start.1 = (s32[128,64]{0,1:T(8,128)S(1)}, s32[128,64]{0,1:T(8,128)}, u32[]{:S(2)}) copy-start(s32[128,64]{0,1:T(8,128)} %param.12) | copy-start | bytes 98308
  (7 other events, 6.8 us)
